TPU v7x, 256 devices: a whole 4x4x8 slice. The times are simulated.
256 devices in a mesh: cond: 4 (over z_hi), px: 64 (over z_lo, x, y, core).
Axes of the slice: x: 4, y: 4, z: 8 (z_hi: 4, z_lo: 2; z = z_hi * 2 + z_lo), core: 2. Of those that a mesh axis runs over, the one named last changes fastest.
Arguments:
- mask_level: float32 [8192, 8192], P('px'), may hold values from -6 to 6
- socs_kernels: float32 [4, 12, 2, 256, 256], P('cond'), may hold values from -3 to 3
- band_cutoff: int32 [4, 12], P('cond'), may hold values from 64 to 128
- kernel_weight: float32 [4, 12], P('cond'), may hold values from 0.05 to 1
- dose_scale: float32 [4], P('cond'), may hold values from 0.7 to 1.4
- shape_corner: int32 [256, 2], replicated, may hold values from 0 to 2047
- shape_extent: int32 [256, 2], replicated, may hold values from 32 to 160
Outputs:
- mask_gradient: float32 [8192, 8192], P('px', 'cond')
All inputs are finite; a program needn't handle non-finite values.
Results may differ from a plain program's by a relative error of at most 0.00011.
Values sent between devices are 32-bit elements; how exact they have to be, the bound alone decides.
No kernel may reach another device: no remote copies, remote signals or barrier semaphores. Data moves between devices by JAX's collectives and lax.ppermute only.
A program may use at most 192 MiB of HBM per device.

v0:
```python
import functools
import math

import jax
import jax.numpy as jnp
import numpy as np
from jax import lax
from jax.experimental import pallas as pl
from jax.experimental.pallas import tpu as pltpu
from jax.sharding import PartitionSpec as P

IMAGE = 2048
LANES = 128
steepness = 6.0
threshold = 0.3
f32 = jnp.float32
bf16 = jnp.bfloat16


def basis_slots(band):
    half = band // 2
    slots = np.arange(band)
    is_sin = (slots >= half) & (slots < band - 1)
    freq = np.where(slots < half, slots, np.where(is_sin, slots - (half - 1), half))
    return freq, is_sin


def basis_tables(band, width):
    freq, is_sin = basis_slots(band)
    fine = 2.0 * np.pi * ((np.arange(LANES)[:, None] * freq[None]) % width) / width
    big = 2.0 * np.pi * ((LANES * np.arange(width // LANES)[:, None] * freq[None]) % width) / width
    first = np.where(is_sin, np.sin(big), np.cos(big))
    second = np.where(is_sin, np.cos(big), -np.sin(big))
    edge = np.sin(2.0 * np.pi * ((np.arange(LANES) * (band // 2)) % width) / width)
    tables = (first, second, np.cos(fine), np.sin(fine))
    return tuple(table.astype(np.float32) for table in tables), edge.astype(np.float32)


def fold_table(band):
    half = band // 2
    both = np.zeros((2 * band, band), np.float32)
    for place in range(band):
        freq = place - half
        size = abs(freq)
        both[place, size if size < half else band - 1] = 1.0
        if 0 < size < half:
            both[band + place, half - 1 + size] = -1.0 if freq > 0 else 1.0
    return both


def wave(places, band, period):
    offsets = np.arange(band) - band // 2
    angle = 2.0 * np.pi * ((places[:, None] * offsets[None, :]) % period) / period
    return np.cos(angle), np.sin(angle)


def resample_table(band, image):
    coarse = 2 * band
    period = 2 * image
    base = np.arange(period)
    row = np.ones(period)
    for freq in range(1, band):
        row += 2.0 * np.cos(2.0 * np.pi * ((base * freq) % period) / period)
    row /= coarse
    place = (2 * np.arange(band) + 1) * (image // coarse)
    columns = 2 * np.arange(image)
    plus = row[(columns[None, :] - place[:, None]) % period]
    minus = row[(columns[None, :] + place[:, None]) % period]
    return np.concatenate([plus, minus], axis=0)


def halves(table):
    table = np.asarray(table, np.float32)
    top = table.astype(bf16)
    rest = (table - top.astype(np.float32)).astype(bf16)
    return top, rest


def split(value):
    top = value.astype(bf16)
    return top, (value - top.astype(f32)).astype(bf16)


def dot(left, right, left_dim=1, right_dim=0):
    return lax.dot_general(
        left, right, (((left_dim,), (right_dim,)), ((), ())), preferred_element_type=f32
    )


def dot_split(left, right, left_dim=1, right_dim=0):
    go = functools.partial(dot, left_dim=left_dim, right_dim=right_dim)
    return go(left[0], right[0]) + (go(left[1], right[0]) + go(left[0], right[1]))


def basis_rows(tables, start, blocks):
    first, second, fine_cos, fine_sin = tables
    parts = []
    for block in range(blocks):
        a = first[pl.ds(start + block, 1), :]
        b = second[pl.ds(start + block, 1), :]
        parts.append(a * fine_cos[...] + b * fine_sin[...])
    return parts[0] if blocks == 1 else jnp.concatenate(parts, axis=0)


def put(array, row, column, value):
    rows = lax.broadcasted_iota(jnp.int32, array.shape, 0)
    columns = lax.broadcasted_iota(jnp.int32, array.shape, 1)
    return jnp.where((rows == row) & (columns == column), value, array)


def store_pieces(out, array):
    band = array.shape[1]
    pieces = [array[:, place : place + LANES] for place in range(0, band, LANES)]
    flat = pieces[0] if len(pieces) == 1 else jnp.concatenate(pieces, axis=0)
    out[...] = flat.reshape(out.shape)


def load_pieces(ref, band):
    flat = ref[...].reshape(band * band // LANES, LANES)
    pieces = [flat[place : place + band] for place in range(0, flat.shape[0], band)]
    return pieces[0] if len(pieces) == 1 else jnp.concatenate(pieces, axis=1)


def mask_kernel(where, mask, first, second, fine_cos, fine_sin, edge_row, edge_col, out, total, side):
    step = pl.program_id(0)
    band = total.shape[1]
    blocks = mask.shape[1] // LANES
    tables = (first, second, fine_cos, fine_sin)

    @pl.when(step == 0)
    def _():
        total[...] = jnp.zeros_like(total)
        side[...] = jnp.zeros_like(side)

    transmit = jnp.tanh(mask[...])
    start = where[0] * (blocks * pl.num_programs(0)) + step * blocks
    columns = split(basis_rows(tables, start, blocks))
    total[...] += dot_split(split(transmit), columns)
    side[...] += jnp.sum(transmit, axis=0, keepdims=True)

    @pl.when(step == pl.num_programs(0) - 1)
    def _():
        row_part = total[...]
        rows = split(basis_rows(tables, where[1], 1))
        packed = dot_split(rows, split(row_part), 0, 0)
        edge_u = jnp.sum(edge_col[...] * row_part[:, 0:1])
        edge_v = jnp.sum(edge_row[...] * side[...])
        packed = put(put(packed, band - 1, 1, edge_u), 1, band - 1, edge_v)
        store_pieces(out, packed)


def target_kernel(where, corner, extent, corner_row, extent_row, out):
    rows_here, image = out.shape
    count = corner.shape[0]
    top = corner_row[0:1, :]
    rows = where[1] * rows_here + lax.broadcasted_iota(jnp.int32, (rows_here, count), 0)
    rows_in = (rows >= top) & (rows < top + extent_row[0:1, :])
    rows_in = jnp.where(rows_in, 1.0, 0.0).astype(bf16)
    left = corner[:, 1:2]
    right = left + extent[:, 1:2]
    step = min(512, image)
    for place in range(0, image, step):
        columns = place + lax.broadcasted_iota(jnp.int32, (count, step), 1)
        cols_in = jnp.where((columns >= left) & (columns < right), 1.0, 0.0).astype(bf16)
        out[:, place : place + step] = jnp.minimum(dot(rows_in, cols_in), 1.0)


def field_kernel(
    where,
    cutoff,
    weight,
    dose,
    packed,
    kernels,
    both,
    both_t,
    y_big,
    y_fine,
    x_hi,
    x_lo,
    up_hi,
    up_lo,
    target,
    out,
    kern,
    radius,
    spec,
    y_rows,
    y_cols,
    prod_hi,
    prod_lo,
    wide_hi,
    wide_lo,
    deep_hi,
    deep_lo,
    cs,
    gain,
    back,
    gs,
    sems,
    *,
    width,
):
    count, _, band, _ = kern.shape
    rows_here, image = target.shape
    half = band // 2
    total_rows = count * rows_here
    part = 64

    def copy(place):
        return pltpu.make_async_copy(kernels.at[0, place], kern.at[place], sems.at[place])

    for place in range(count):
        copy(place).start()

    big_cos = y_big[0, pl.ds(where[1], 1), :]
    big_sin = y_big[1, pl.ds(where[1], 1), :]
    cos_y = (big_cos * y_fine[0] - big_sin * y_fine[1]) * (1.0 / band)
    sin_y = (big_sin * y_fine[0] + big_cos * y_fine[1]) * (1.0 / band)
    table = jnp.concatenate(
        [
            jnp.concatenate([cos_y, 0.0 - sin_y], axis=1),
            jnp.concatenate([sin_y, cos_y], axis=1),
        ],
        axis=0,
    )
    table_hi, table_lo = split(table)
    y_rows[...] = jnp.concatenate([table_hi, table_lo], axis=0)
    table_hi, table_lo = table_hi.astype(f32), table_lo.astype(f32)
    stacked = jnp.concatenate([table_hi, table_hi, table_lo], axis=0)
    y_cols[...] = jnp.transpose(stacked).astype(bf16)
    fu = lax.broadcasted_iota(jnp.int32, (band, band), 0) - half
    fv = lax.broadcasted_iota(jnp.int32, (band, band), 1) - half
    radius[...] = fu * fu + fv * fv
    gs[...] = jnp.zeros_like(gs)

    box = load_pieces(packed, band)
    edge_u = box[band - 1 : band, 1:2] * (1.0 / width)
    edge_v = box[1:2, band - 1 : band] * (1.0 / width)
    box_hi, box_lo = split(box * (1.0 / width))
    opened = dot(both[...], box_hi) + dot(both[...], box_lo)
    box_hi, box_lo = split(opened)
    opened = dot(box_hi, both[...], 1, 1) + dot(box_lo, both[...], 1, 1)
    spec_im = opened[band:, :band] + opened[:band, band:]
    spec[0] = opened[:band, :band] - opened[band:, band:]
    at_u = (fu == -half) & (fv == 0)
    at_v = (fu == 0) & (fv == -half)
    spec[1] = spec_im + jnp.where(at_u, edge_u, 0.0) + jnp.where(at_v, edge_v, 0.0)

    def forward(place, carry):
        copy(place).wait()
        limit = cutoff[0, place]
        limit = limit * limit
        for start in range(0, band, part):
            here = pl.ds(start, part)
            inside = radius[here, :] <= limit
            k_re = jnp.where(inside, kern[place, 0, here, :], 0.0)
            k_im = jnp.where(inside, kern[place, 1, here, :], 0.0)
            kern[place, 0, here, :] = k_re
            kern[place, 1, here, :] = k_im
            s_re = spec[0, here, :]
            s_im = spec[1, here, :]
            re_hi, re_lo = split(k_re * s_re - k_im * s_im)
            im_hi, im_lo = split(k_re * s_im + k_im * s_re)
            prod_hi[here, :] = re_hi
            prod_lo[here, :] = re_lo
            there = pl.ds(band + start, part)
            prod_hi[there, :] = im_hi
            prod_lo[there, :] = im_lo
        main = dot(y_rows[...], prod_hi[...])
        rest = dot(y_rows[: 2 * rows_here, :], prod_lo[...])
        value = main[: 2 * rows_here] + (main[2 * rows_here :] + rest)
        hi, lo = split(value)
        here = pl.ds(pl.multiple_of(place * rows_here, rows_here), rows_here)
        there = pl.ds(pl.multiple_of(total_rows + place * rows_here, rows_here), rows_here)
        wide_hi[here, :] = hi[:rows_here]
        wide_lo[here, :] = lo[:rows_here]
        wide_hi[there, :] = hi[rows_here:]
        wide_lo[there, :] = lo[rows_here:]
        return carry

    lax.fori_loop(0, count, forward, 0)

    cs[...] = dot_split((wide_hi[...], wide_lo[...]), (x_hi[...], x_lo[...]))

    def fields(place):
        here = pl.ds(pl.multiple_of(place * rows_here, rows_here), rows_here)
        there = pl.ds(pl.multiple_of(total_rows + place * rows_here, rows_here), rows_here)
        c_re = cs[here, :band]
        s_re = cs[here, band:]
        c_im = cs[there, :band]
        s_im = cs[there, band:]
        return (c_re - s_im, c_im + s_re, c_re + s_im, c_im - s_re), here, there

    def add_power(place, carry):
        plus, minus = carry
        (p_re, p_im, m_re, m_im), _, _ = fields(place)
        scale = weight[0, place]
        return (
            plus + scale * (p_re * p_re + p_im * p_im),
            minus + scale * (m_re * m_re + m_im * m_im),
        )

    zero = jnp.zeros((rows_here, band), f32)
    plus, minus = lax.fori_loop(0, count, add_power, (zero, zero))
    power_hi, power_lo = split(jnp.concatenate([plus, minus], axis=1))
    power = jnp.concatenate([power_hi, power_lo], axis=0)
    dose_here = dose[0]
    scale = 2.0 * (width / band) * steepness * dose_here
    step = min(512, image)
    for place in range(0, image, step):
        here = pl.ds(place, step)
        main = dot(power, up_hi[:, here])
        rest = dot(power_hi, up_lo[:, here])
        intensity = main[:rows_here] + (main[rows_here:] + rest)
        level = steepness * (dose_here * intensity - threshold)
        resist = 1.0 / (1.0 + jnp.exp(0.0 - level))
        slope = scale * (resist - target[:, here]) * resist * (1.0 - resist)
        hi, lo = split(slope)
        gain[:rows_here, here] = hi
        gain[rows_here:, here] = lo
    main = dot(gain[...], up_hi[...], 1, 1)
    rest = dot(gain[:rows_here, :], up_lo[...], 1, 1)
    slope = 2.0 * (main[:rows_here] + (main[rows_here:] + rest))
    slope_plus = slope[:, :band]
    slope_minus = slope[:, band:]

    def pull(place, carry):
        (p_re, p_im, m_re, m_im), here, there = fields(place)
        scale = weight[0, place]
        plus = scale * slope_plus
        minus = scale * slope_minus
        p_re, p_im, m_re, m_im = plus * p_re, plus * p_im, minus * m_re, minus * m_im
        for rows, columns, value in (
            (here, slice(0, band), p_re + m_re),
            (here, slice(band, 2 * band), p_im - m_im),
            (there, slice(0, band), p_im + m_im),
            (there, slice(band, 2 * band), m_re - p_re),
        ):
            hi, lo = split(value)
            deep_hi[rows, columns] = hi
            deep_lo[rows, columns] = lo
        return carry

    lax.fori_loop(0, count, pull, 0)
    back[...] = dot_split((deep_hi[...], deep_lo[...]), (x_hi[...], x_lo[...]), 1, 1)

    def gather(place, carry):
        here = pl.ds(pl.multiple_of(place * rows_here, rows_here), rows_here)
        there = pl.ds(pl.multiple_of(total_rows + place * rows_here, rows_here), rows_here)
        hi, lo = split(jnp.concatenate([back[here, :], back[there, :]], axis=0))
        grad = dot(y_cols[...], jnp.concatenate([hi, lo, hi], axis=0))
        for start in range(0, band, part):
            here = pl.ds(start, part)
            k_re = kern[place, 0, here, :]
            k_im = kern[place, 1, here, :]
            g_re = grad[start : start + part]
            g_im = grad[band + start : band + start + part]
            gs[0, here, :] += k_re * g_re + k_im * g_im
            gs[1, here, :] += k_re * g_im - k_im * g_re
        return carry

    lax.fori_loop(0, count, gather, 0)
    g_re = gs[0]
    g_im = gs[1]
    edge_u = g_im[0:1, half : half + 1]
    edge_v = g_im[half : half + 1, 0:1]
    re_hi, re_lo = split(g_re)
    im_hi, im_lo = split(g_im)
    even, odd = both_t[:, :band], both_t[:, band:]
    left = dot(even, re_hi) + dot(even, re_lo) + dot(odd, im_hi) + dot(odd, im_lo)
    right = dot(even, im_hi) + dot(even, im_lo) - dot(odd, re_hi) - dot(odd, re_lo)
    l_hi, l_lo = split(left)
    r_hi, r_lo = split(right)
    even, odd = both[:band, :], both[band:, :]
    folded = dot(l_hi, even) + dot(l_lo, even) + dot(r_hi, odd) + dot(r_lo, odd)
    store_pieces(out, put(put(folded, band - 1, 1, edge_u), 1, band - 1, edge_v))


def spread_kernel(
    where, mask, packed, first, second, fine_cos, fine_sin, edge_row, edge_col, out, rows_hi, rows_lo, side
):
    step = pl.program_id(0)
    band = rows_hi.shape[1]
    blocks = mask.shape[1] // LANES
    tables = (first, second, fine_cos, fine_sin)
    width = first.shape[0] * LANES

    @pl.when(step == 0)
    def _():
        box = load_pieces(packed, band) * (1.0 / width)
        edge_u = box[band - 1 : band, 1:2]
        edge_v = box[1:2, band - 1 : band]
        box = put(put(box, band - 1, 1, 0.0), 1, band - 1, 0.0)
        mixed = dot_split(split(basis_rows(tables, where[1], 1)), split(box))
        hi, lo = split(mixed)
        rows_hi[: mixed.shape[0], :] = hi
        rows_hi[mixed.shape[0] :, :] = lo
        rows_lo[...] = edge_u * edge_col[...]
        side[...] = edge_v * edge_row[...]

    transmit = jnp.tanh(mask[...])
    start = where[0] * (blocks * pl.num_programs(0)) + step * blocks
    columns_hi, columns_lo = split(basis_rows(tables, start, blocks))
    count = mask.shape[0]
    main = dot(rows_hi[...], columns_hi, 1, 1)
    rest = dot(rows_hi[:count, :], columns_lo, 1, 1)
    grad = main[:count] + (main[count:] + rest) + rows_lo[...] + side[...]
    out[...] = grad * (1.0 - transmit * transmit)


def params():
    return pltpu.CompilerParams(vmem_limit_bytes=48 * 1024 * 1024)


def whole(array):
    rank = len(array.shape)
    return pl.BlockSpec(array.shape, lambda *_: (0,) * rank)


def local(
    mask_level, socs_kernels, band_cutoff, kernel_weight, dose_scale, shape_corner, shape_extent
):
    rows_here, width = mask_level.shape
    count = socs_kernels.shape[1]
    band = socs_kernels.shape[3]
    pencils = lax.axis_size("px")
    conds = lax.axis_size("cond")
    image_rows = IMAGE // pencils
    cols_here = width // conds
    where = jnp.stack([lax.axis_index("cond"), lax.axis_index("px")]).astype(jnp.int32)
    pieces = (pencils, band * band // LANES // pencils, LANES)

    tables, edge = basis_tables(band, width)
    chunk = min(512, cols_here)
    steps = cols_here // chunk
    edge_row = np.tile(edge, chunk // LANES)[None, :]
    edge_col = edge[:, None]
    consts = (*tables, edge_row, edge_col)

    mask_spec = pl.BlockSpec((rows_here, chunk), lambda i, w: (0, w[0] * steps + i))
    packed = pl.pallas_call(
        mask_kernel,
        out_shape=jax.ShapeDtypeStruct(pieces, f32),
        grid_spec=pltpu.PrefetchScalarGridSpec(
            num_scalar_prefetch=1,
            grid=(steps,),
            in_specs=[mask_spec, *(whole(table) for table in consts)],
            out_specs=pl.BlockSpec(pieces, lambda *_: (0, 0, 0)),
            scratch_shapes=[pltpu.VMEM((rows_here, band), f32), pltpu.VMEM((1, chunk), f32)],
        ),
        compiler_params=params(),
        name="mask_rows",
    )(where, mask_level, *consts)

    smem = pl.BlockSpec(memory_space=pltpu.SMEM)
    vmem = pl.BlockSpec(memory_space=pltpu.VMEM)
    target = pl.pallas_call(
        target_kernel,
        out_shape=jax.ShapeDtypeStruct((image_rows, IMAGE), f32),
        in_specs=[smem, vmem, vmem, vmem, vmem],
        out_specs=vmem,
        compiler_params=params(),
        name="target_rows",
    )(where, shape_corner, shape_extent, shape_corner.T, shape_extent.T)

    packed = exchange(packed)

    both = fold_table(band)
    y_big = np.stack(wave(image_rows * np.arange(pencils), band, IMAGE)).astype(np.float32)
    y_fine = np.stack(wave(np.arange(image_rows), band, IMAGE)).astype(np.float32)
    x_cos, x_sin = wave(2 * np.arange(band) + 1, band, 4 * band)
    x_hi, x_lo = halves(np.concatenate([x_cos.T, x_sin.T], axis=1))
    up_hi, up_lo = halves(resample_table(band, IMAGE))
    deep = 2 * count * image_rows
    folded = pl.pallas_call(
        functools.partial(field_kernel, width=width),
        out_shape=jax.ShapeDtypeStruct(pieces, f32),
        in_specs=[smem] * 4 + [vmem, pl.BlockSpec(memory_space=pl.ANY)] + [vmem] * 9,
        out_specs=vmem,
        scratch_shapes=[
            pltpu.VMEM((count, 2, band, band), f32),
            pltpu.VMEM((band, band), jnp.int32),
            pltpu.VMEM((2, band, band), f32),
            pltpu.VMEM((4 * image_rows, 2 * band), bf16),
            pltpu.VMEM((2 * band, 6 * image_rows), bf16),
            pltpu.VMEM((2 * band, band), bf16),
            pltpu.VMEM((2 * band, band), bf16),
            pltpu.VMEM((deep, band), bf16),
            pltpu.VMEM((deep, band), bf16),
            pltpu.VMEM((deep, 2 * band), bf16),
            pltpu.VMEM((deep, 2 * band), bf16),
            pltpu.VMEM((deep, 2 * band), f32),
            pltpu.VMEM((2 * image_rows, IMAGE), bf16),
            pltpu.VMEM((deep, band), f32),
            pltpu.VMEM((2, band, band), f32),
            pltpu.SemaphoreType.DMA((count,)),
        ],
        compiler_params=params(),
        name="image_rows",
    )(
        where,
        band_cutoff,
        kernel_weight,
        dose_scale,
        packed,
        socs_kernels,
        both.astype(bf16),
        both.T.astype(bf16),
        y_big,
        y_fine,
        x_hi,
        x_lo,
        up_hi,
        up_lo,
        target,
    )

    folded = exchange(folded)

    return pl.pallas_call(
        spread_kernel,
        out_shape=jax.ShapeDtypeStruct((rows_here, cols_here), f32),
        grid_spec=pltpu.PrefetchScalarGridSpec(
            num_scalar_prefetch=1,
            grid=(steps,),
            in_specs=[
                mask_spec,
                pl.BlockSpec(pieces, lambda *_: (0, 0, 0)),
                *(whole(table) for table in consts),
            ],
            out_specs=pl.BlockSpec((rows_here, chunk), lambda i, w: (0, i)),
            scratch_shapes=[
                pltpu.VMEM((2 * rows_here, band), bf16),
                pltpu.VMEM((rows_here, 1), f32),
                pltpu.VMEM((1, chunk), f32),
            ],
        ),
        compiler_params=params(),
        name="mask_gradient",
    )(where, mask_level, folded, *consts)


def exchange(packed):
    conds = lax.axis_size("cond")
    arrived = lax.all_to_all(packed, "px", split_axis=0, concat_axis=0, tiled=True)
    piece = jnp.sum(arrived, axis=0)
    others = [
        lax.ppermute(piece, "cond", [(i, (i + d) % conds) for i in range(conds)])
        for d in range(1, conds)
    ]
    piece = functools.reduce(jnp.add, others, piece)
    outgoing = jnp.broadcast_to(piece[None], packed.shape)
    return lax.all_to_all(outgoing, "px", split_axis=0, concat_axis=0, tiled=True)


def solution(mesh):
    in_specs = (
        P("px", None),
        P("cond", None, None, None, None),
        P("cond", None),
        P("cond", None),
        P("cond"),
        P(),
        P(),
    )
    out_specs = P("px", "cond")
    return jax.shard_map(local, mesh=mesh, in_specs=in_specs, out_specs=out_specs, check_vma=False)
```

profile of v0, /device:TPU:1, one launch (start us, length us, event | category | flops | bytes accessed | tf_op | source)
XLA Modules:
  0.0 119.7 jit_solution(6476642771206189364)
XLA Ops:
  0.0 0.0 copy-start.19
  0.0 0.0 copy-start.20
  0.0 0.0 copy-start.24
  0.0 0.0 copy-start.23
  0.0 0.1 pad_add_fusion.where
  0.1 0.0 copy-start
  0.1 2.2 %copy-done = f32[128,8192]{1,0:T(8,128)S(1)} copy-done((f32[128,8192]{1,0:T(8,128)S(1)}, f32[128,8192]{1,0:T(8,128)}, u32[]{:S(2)}) %copy-start) | copy-done | bytes 4194328
  2.3 0.9 copy-done.3
  3.2 0.9 copy-done.5
  4.1 0.8 copy-done.7
  4.9 0.8 copy-done.9
  5.8 0.8 copy-done.11
  6.6 0.7 copy-done.21
  7.3 2.5 %mask_rows.1 = f32[64,8,128]{2,1,0:T(8,128)S(1)} custom-call(s32[2]{0:T(128)S(1)} %pad_add_fusion.where, f32[128,8192]{1,0:T(8,128)S(1)} %copy-done, f32[64,256]{1,0:T(8,128)S(1)} %copy-done.11, f32[64,256]{1,0:T(8,128)S(1)} %copy-done.9, f32[128,256]{1,0:T(8,128)S(1)} %copy-done.5, f32[128,256]{1,0:T(8,128)S(1)} %copy-done.3, f32[1,512]{1,0:T(1,128)S(1)} %copy-done.21, ...), custom_call_target="tpu_custom_call" | custom-call | tf_op jit(solution)/shard_map/mask_rows/pallas_call | solution.py:442
  9.8 19.9 %all_to_all.20 = f32[64,8,128]{2,1,0:T(8,128)S(1)} all-to-all(f32[64,8,128]{2,1,0:T(8,128)S(1)} %mask_rows.1), channel_id=1, replica_groups=mesh['cond'=4,'px'=64] {'px'}, dimensions={0} | all-to-all | bytes 524288 | tf_op jit(solution)/shard_map/all_to_all | solution.py:546
  29.6 0.1 reduce_sum.18
  29.7 5.2 %collective-permute-start.2 = (f32[8,128]{1,0:T(8,128)S(1)}, f32[8,128]{1,0:T(8,128)S(1)}, u32[]{:S(2)}, u32[]{:S(2)}) collective-permute-start(f32[8,128]{1,0:T(8,128)S(1)} %reduce_sum.18), channel_id=1, source_target_pairs={{0,192},{64,0},{128,64},{192,128},{1,193},{65,1},{129,65},{193,129... | collective-permute-start | bytes 12296 | tf_op jit(solution)/shard_map/ppermute | solution.py:549
  34.9 1.2 collective-permute-start.1
  36.1 2.1 %collective-permute-start = (f32[8,128]{1,0:T(8,128)S(1)}, f32[8,128]{1,0:T(8,128)S(1)}, u32[]{:S(2)}, u32[]{:S(2)}) collective-permute-start(f32[8,128]{1,0:T(8,128)S(1)} %reduce_sum.18), channel_id=1, source_target_pairs={{0,64},{64,128},{128,192},{192,0},{1,65},{65,129},{129,193},{193,1... | collective-permute-start | bytes 12296 | tf_op jit(solution)/shard_map/ppermute | solution.py:549
  38.2 0.0 collective-permute-done.2
  38.2 3.1 %collective-permute-done.1 = f32[8,128]{1,0:T(8,128)S(1)} collective-permute-done((f32[8,128]{1,0:T(8,128)S(1)}, f32[8,128]{1,0:T(8,128)S(1)}, u32[]{:S(2)}, u32[]{:S(2)}) %collective-permute-start.1) | collective-permute-done | bytes 4128 | tf_op jit(solution)/shard_map/ppermute | solution.py:549
  41.3 0.0 collective-permute-done
  41.3 0.7 broadcast_in_dim.4
  42.0 5.9 %all-to-all-start.1 = ((f32[64,8,128]{2,1,0:T(8,128)}), f32[64,8,128]{2,1,0:T(8,128)S(1)}, u32[]{:S(2)}, u32[]{:S(2)}) async-start(f32[64,8,128]{2,1,0:T(8,128)} %broadcast_in_dim.4), calls=%async_computation.1 | async-start | bytes 524288 | tf_op jit(solution)/shard_map/all_to_all | solution.py:554
  48.6 0.0 copy-done.19
  48.6 0.1 copy.22.corner
  48.7 0.0 copy-done.20
  48.7 0.1 copy.23.extent
  48.9 1.0 target_rows.1.target
  49.9 0.0 copy-start.4
  49.9 0.0 copy-start.6
  49.9 0.0 copy-start.8
  49.9 0.0 copy-start.10
  50.0 0.0 copy-start.12
  50.0 7.8 %all-to-all-done.1.packed = f32[64,8,128]{2,1,0:T(8,128)S(1)} async-done(((f32[64,8,128]{2,1,0:T(8,128)}), f32[64,8,128]{2,1,0:T(8,128)S(1)}, u32[]{:S(2)}, u32[]{:S(2)}) %all-to-all-start.1) | async-done | bytes 262176 | tf_op jit(solution)/shard_map/all_to_all | solution.py:554
  57.8 0.0 copy-done.24
  57.8 0.0 copy-done.23
  57.8 0.0 copy-done.2
  57.8 0.0 copy-done.13
  57.8 0.0 copy-done.17
  57.8 0.0 copy-done.18
  57.8 0.0 copy-start.14
  57.8 0.9 copy-done.14
  58.8 0.9 copy-done.15
  59.7 0.9 copy-done.16
  60.7 15.6 %image_rows.1 = f32[64,8,128]{2,1,0:T(8,128)S(1)} custom-call(s32[2]{0:T(128)S(1)} %pad_add_fusion.where, s32[1,12]{1,0:T(1,128)S(1)} %copy-done.23, f32[1,12]{1,0:T(1,128)S(1)} %copy-done.24, f32[1]{0:T(128)S(6)} %copy.24.dose, f32[64,8,128]{2,1,0:T(8,128)S(1)} %all-to-all-done.1.packed, f32[1,12,2,256,256]{4,3,2,1,0:T(8,128)} %kernels.1, ...), custom_call_target="tpu_custom_call" | custom-call | tf_op jit(solution)/shard_map/image_rows/pallas_call | solution.py:476
  76.3 13.8 %all_to_all.21 = f32[64,8,128]{2,1,0:T(8,128)S(1)} all-to-all(f32[64,8,128]{2,1,0:T(8,128)S(1)} %image_rows.1), channel_id=1, replica_groups=mesh['cond'=4,'px'=64] {'px'}, dimensions={0} | all-to-all | bytes 524288 | tf_op jit(solution)/shard_map/all_to_all | solution.py:546
  90.0 0.1 reduce_sum.19
  90.1 1.3 %collective-permute-start.5 = (f32[8,128]{1,0:T(8,128)S(1)}, f32[8,128]{1,0:T(8,128)S(1)}, u32[]{:S(2)}, u32[]{:S(2)}) collective-permute-start(f32[8,128]{1,0:T(8,128)S(1)} %reduce_sum.19), channel_id=1, source_target_pairs={{0,192},{64,0},{128,64},{192,128},{1,193},{65,1},{129,65},{193,129... | collective-permute-start | bytes 12296 | tf_op jit(solution)/shard_map/ppermute | solution.py:549
  91.4 2.7 %collective-permute-start.4 = (f32[8,128]{1,0:T(8,128)S(1)}, f32[8,128]{1,0:T(8,128)S(1)}, u32[]{:S(2)}, u32[]{:S(2)}) collective-permute-start(f32[8,128]{1,0:T(8,128)S(1)} %reduce_sum.19), channel_id=1, source_target_pairs={{0,128},{64,192},{128,0},{192,64},{1,129},{65,193},{129,1},{193,65... | collective-permute-start | bytes 12296 | tf_op jit(solution)/shard_map/ppermute | solution.py:549
  94.1 2.3 %collective-permute-start.3 = (f32[8,128]{1,0:T(8,128)S(1)}, f32[8,128]{1,0:T(8,128)S(1)}, u32[]{:S(2)}, u32[]{:S(2)}) collective-permute-start(f32[8,128]{1,0:T(8,128)S(1)} %reduce_sum.19), channel_id=1, source_target_pairs={{0,64},{64,128},{128,192},{192,0},{1,65},{65,129},{129,193},{193,1... | collective-permute-start | bytes 12296 | tf_op jit(solution)/shard_map/ppermute | solution.py:549
  96.4 0.0 collective-permute-done.5
  96.4 1.4 %collective-permute-done.4 = f32[8,128]{1,0:T(8,128)S(1)} collective-permute-done((f32[8,128]{1,0:T(8,128)S(1)}, f32[8,128]{1,0:T(8,128)S(1)}, u32[]{:S(2)}, u32[]{:S(2)}) %collective-permute-start.4) | collective-permute-done | bytes 4128 | tf_op jit(solution)/shard_map/ppermute | solution.py:549
  97.8 1.2 %collective-permute-done.3 = f32[8,128]{1,0:T(8,128)S(1)} collective-permute-done((f32[8,128]{1,0:T(8,128)S(1)}, f32[8,128]{1,0:T(8,128)S(1)}, u32[]{:S(2)}, u32[]{:S(2)}) %collective-permute-start.3) | collective-permute-done | bytes 4128 | tf_op jit(solution)/shard_map/ppermute | solution.py:549
  99.0 15.0 %all_to_all.22.packed = f32[64,8,128]{2,1,0:T(8,128)S(1)} all-to-all(f32[64,8,128]{2,1,0:T(8,128)S(1)} %broadcast_in_dim.5), channel_id=1, replica_groups=mesh['cond'=4,'px'=64] {'px'}, dimensions={0} | all-to-all | bytes 524288 | tf_op jit(solution)/shard_map/all_to_all | solution.py:554
  114.1 0.0 copy-done.4
  114.1 0.0 copy-done.6
  114.1 0.0 copy-done.8
  114.1 0.0 copy-done.10
  114.1 0.0 copy-done.12
  114.1 0.0 copy-done.22
  114.1 0.0 copy-start.1
  114.1 2.2 %copy-done.1 = f32[128,8192]{1,0:T(8,128)S(1)} copy-done((f32[128,8192]{1,0:T(8,128)S(1)}, f32[128,8192]{1,0:T(8,128)}, u32[]{:S(2)}) %copy-start.1) | copy-done | bytes 4194328
  116.3 3.3 %mask_gradient.1 = f32[128,2048]{1,0:T(8,128)} custom-call(s32[2]{0:T(128)S(1)} %pad_add_fusion.where, f32[128,8192]{1,0:T(8,128)S(1)} %copy-done.1, f32[64,8,128]{2,1,0:T(8,128)S(1)} %all_to_all.22.packed, f32[64,256]{1,0:T(8,128)S(1)} %copy-done.12, f32[64,256]{1,0:T(8,128)S(1)} %copy-done.10, f32[128,256]{1,0:T(8,128)S(1)} %copy-done.6, ...), custom_call_target="tpu_custom_call" | custom-call | tf_op jit(solution)/shard_map/mask_gradient/pallas_call | solution.py:521
  (16 shorter events, 0.1 us)
Async XLA Ops:
  0.0 48.6 %copy-start.19 = (s32[256,2]{0,1:T(2,128)S(1)}, s32[256,2]{0,1:T(2,128)}, u32[]{:S(2)}) copy-start(s32[256,2]{0,1:T(2,128)} %param.26) | copy-start | bytes 6148
  0.0 48.7 %copy-start.20 = (s32[256,2]{0,1:T(2,128)S(1)}, s32[256,2]{0,1:T(2,128)}, u32[]{:S(2)}) copy-start(s32[256,2]{0,1:T(2,128)} %param.27) | copy-start | bytes 6148
  0.0 57.8 %copy-start.24 = (f32[1,12]{1,0:T(1,128)S(1)}, f32[1,12]{1,0:T(1,128)}, u32[]{:S(2)}) copy-start(f32[1,12]{1,0:T(1,128)} %weight.1) | copy-start | bytes 148
  0.0 57.8 %copy-start.23 = (s32[1,12]{1,0:T(1,128)S(1)}, s32[1,12]{1,0:T(1,128)}, u32[]{:S(2)}) copy-start(s32[1,12]{1,0:T(1,128)} %cutoff.1) | copy-start | bytes 148
  0.1 2.2 %copy-start = (f32[128,8192]{1,0:T(8,128)S(1)}, f32[128,8192]{1,0:T(8,128)}, u32[]{:S(2)}) copy-start(f32[128,8192]{1,0:T(8,128)} %mask.3) | copy-start | bytes 12582916
  2.3 0.9 copy-start.3
  3.2 0.9 copy-start.5
  4.1 0.8 copy-start.7
  4.9 0.8 copy-start.9
  5.8 0.8 copy-start.11
  6.6 0.7 copy-start.21
  7.3 50.5 %copy-start.2 = (bf16[512,2048]{1,0:T(8,128)(2,1)S(1)}, bf16[512,2048]{1,0:T(8,128)(2,1)}, u32[]{:S(2)}) copy-start(bf16[512,2048]{1,0:T(8,128)(2,1)} %constant.51.clone.up_hi) | copy-start | bytes 6291460
  7.3 50.5 %copy-start.13 = (bf16[256,512]{1,0:T(8,128)(2,1)S(1)}, bf16[256,512]{1,0:T(8,128)(2,1)}, u32[]{:S(2)}) copy-start(bf16[256,512]{1,0:T(8,128)(2,1)} %constant.50.clone.x_lo) | copy-start | bytes 786436
  7.3 50.5 %copy-start.17 = (f32[2,64,256]{2,1,0:T(8,128)S(1)}, f32[2,64,256]{2,1,0:T(8,128)}, u32[]{:S(2)}) copy-start(f32[2,64,256]{2,1,0:T(8,128)} %constant.47.clone.y_big) | copy-start | bytes 393220
  7.3 50.5 %copy-start.18 = (f32[2,32,256]{2,1,0:T(8,128)S(1)}, f32[2,32,256]{2,1,0:T(8,128)}, u32[]{:S(2)}) copy-start(f32[2,32,256]{2,1,0:T(8,128)} %constant.48.clone.y_fine) | copy-start | bytes 196612
  29.7 8.5 %collective-permute-start.2 = (f32[8,128]{1,0:T(8,128)S(1)}, f32[8,128]{1,0:T(8,128)S(1)}, u32[]{:S(2)}, u32[]{:S(2)}) collective-permute-start(f32[8,128]{1,0:T(8,128)S(1)} %reduce_sum.18), channel_id=1, source_target_pairs={{0,192},{64,0},{128,64},{192,128},{1,193},{65,1},{129,65},{193,129... | collective-permute-start | bytes 12296 | tf_op jit(solution)/shard_map/ppermute | solution.py:549
  34.9 6.4 %collective-permute-start.1 = (f32[8,128]{1,0:T(8,128)S(1)}, f32[8,128]{1,0:T(8,128)S(1)}, u32[]{:S(2)}, u32[]{:S(2)}) collective-permute-start(f32[8,128]{1,0:T(8,128)S(1)} %reduce_sum.18), channel_id=1, source_target_pairs={{0,128},{64,192},{128,0},{192,64},{1,129},{65,193},{129,1},{193,65... | collective-permute-start | bytes 12296 | tf_op jit(solution)/shard_map/ppermute | solution.py:549
  36.1 5.2 %collective-permute-start = (f32[8,128]{1,0:T(8,128)S(1)}, f32[8,128]{1,0:T(8,128)S(1)}, u32[]{:S(2)}, u32[]{:S(2)}) collective-permute-start(f32[8,128]{1,0:T(8,128)S(1)} %reduce_sum.18), channel_id=1, source_target_pairs={{0,64},{64,128},{128,192},{192,0},{1,65},{65,129},{129,193},{193,1... | collective-permute-start | bytes 12296 | tf_op jit(solution)/shard_map/ppermute | solution.py:549
  42.0 15.8 %all-to-all-start.1 = ((f32[64,8,128]{2,1,0:T(8,128)}), f32[64,8,128]{2,1,0:T(8,128)S(1)}, u32[]{:S(2)}, u32[]{:S(2)}) async-start(f32[64,8,128]{2,1,0:T(8,128)} %broadcast_in_dim.4), calls=%async_computation.1 | async-start | bytes 524288 | tf_op jit(solution)/shard_map/all_to_all | solution.py:554
  49.9 64.2 %copy-start.4 = (f32[128,256]{1,0:T(8,128)S(1)}, f32[128,256]{1,0:T(8,128)}, u32[]{:S(2)}) copy-start(f32[128,256]{1,0:T(8,128)} %constant.42.clone.fine_sin) | copy-start | bytes 393220
  49.9 64.2 %copy-start.6 = (f32[128,256]{1,0:T(8,128)S(1)}, f32[128,256]{1,0:T(8,128)}, u32[]{:S(2)}) copy-start(f32[128,256]{1,0:T(8,128)} %constant.41.clone.fine_cos) | copy-start | bytes 393220
  49.9 64.2 %copy-start.8 = (f32[128,1]{1,0:T(8,128)S(1)}, f32[128,1]{1,0:T(8,128)}, u32[]{:S(2)}) copy-start(f32[128,1]{1,0:T(8,128)} %constant.44.clone.edge_col) | copy-start | bytes 1540
  49.9 64.1 %copy-start.10 = (f32[64,256]{1,0:T(8,128)S(1)}, f32[64,256]{1,0:T(8,128)}, u32[]{:S(2)}) copy-start(f32[64,256]{1,0:T(8,128)} %constant.40.clone.second) | copy-start | bytes 196612
  50.0 64.1 %copy-start.12 = (f32[64,256]{1,0:T(8,128)S(1)}, f32[64,256]{1,0:T(8,128)}, u32[]{:S(2)}) copy-start(f32[64,256]{1,0:T(8,128)} %constant.39.clone.first) | copy-start | bytes 196612
  57.8 1.0 copy-start.14
  58.8 0.9 copy-start.15
  59.7 0.9 copy-start.16
  60.7 53.4 %copy-start.22 = (f32[1,512]{1,0:T(1,128)S(1)}, f32[1,512]{1,0:T(1,128)}, u32[]{:S(2)}) copy-start(f32[1,512]{1,0:T(1,128)} %constant.43.clone.edge_row) | copy-start | bytes 6148
  90.1 6.3 %collective-permute-start.5 = (f32[8,128]{1,0:T(8,128)S(1)}, f32[8,128]{1,0:T(8,128)S(1)}, u32[]{:S(2)}, u32[]{:S(2)}) collective-permute-start(f32[8,128]{1,0:T(8,128)S(1)} %reduce_sum.19), channel_id=1, source_target_pairs={{0,192},{64,0},{128,64},{192,128},{1,193},{65,1},{129,65},{193,129... | collective-permute-start | bytes 12296 | tf_op jit(solution)/shard_map/ppermute | solution.py:549
  91.4 6.4 %collective-permute-start.4 = (f32[8,128]{1,0:T(8,128)S(1)}, f32[8,128]{1,0:T(8,128)S(1)}, u32[]{:S(2)}, u32[]{:S(2)}) collective-permute-start(f32[8,128]{1,0:T(8,128)S(1)} %reduce_sum.19), channel_id=1, source_target_pairs={{0,128},{64,192},{128,0},{192,64},{1,129},{65,193},{129,1},{193,65... | collective-permute-start | bytes 12296 | tf_op jit(solution)/shard_map/ppermute | solution.py:549
  94.1 4.9 %collective-permute-start.3 = (f32[8,128]{1,0:T(8,128)S(1)}, f32[8,128]{1,0:T(8,128)S(1)}, u32[]{:S(2)}, u32[]{:S(2)}) collective-permute-start(f32[8,128]{1,0:T(8,128)S(1)} %reduce_sum.19), channel_id=1, source_target_pairs={{0,64},{64,128},{128,192},{192,0},{1,65},{65,129},{129,193},{193,1... | collective-permute-start | bytes 12296 | tf_op jit(solution)/shard_map/ppermute | solution.py:549
  114.1 2.2 %copy-start.1 = (f32[128,8192]{1,0:T(8,128)S(1)}, f32[128,8192]{1,0:T(8,128)}, u32[]{:S(2)}) copy-start(f32[128,8192]{1,0:T(8,128)} %mask.3) | copy-start | bytes 12582916
where the time goes:
time: 120 us
  blocking collectives  48.7 us (41%)
  Pallas kernels  22.4 us (19%)
  starting transfers between devices  20.6 us (17%)
  waiting for transfers between devices  13.5 us (11%)
  local copies, waits for them, and re-layouts  13.3 us (11%)
    all_to_all x2, blocking collectives, exchange(): lax.all_to_all(packed, 'px', split_axis=0, concat_axis=0, tiled=True)  33.6 us
    pallas_call x1, Pallas kernels, local(): pl.pallas_call(functools.partial(field_kernel, width=width), out_shape=ja...  15.6 us
    all_to_all x1, blocking collectives, exchange(): lax.all_to_all(outgoing, 'px', split_axis=0, concat_axis=0, tiled=True)  15 us
    ppermute x6, starting transfers between devices, exchange(): lax.ppermute(piece, 'cond', [(i, (i + d) % conds) for i in range(conds)])  14.7 us
    unnamed x52, local copies, waits for them, and re-layouts  12.6 us
    all_to_all x1, waiting for transfers between devices, exchange(): lax.all_to_all(outgoing, 'px', split_axis=0, concat_axis=0, tiled=True)  7.8 us
    all_to_all x1, starting transfers between devices, exchange(): lax.all_to_all(outgoing, 'px', split_axis=0, concat_axis=0, tiled=True)  5.9 us
    ppermute x6, waiting for transfers between devices, exchange(): lax.ppermute(piece, 'cond', [(i, (i + d) % conds) for i in range(conds)])  5.71 us
  transfers between devices with their start and end apart: 7, of which 4 were waited for; matrix products, arithmetic and copies ran while one was open for 0% of the time, Pallas kernels for 1%

commit v1 on v0

v1 whole, which is shorter than its diff:
```python
import functools
import math

import jax
import jax.numpy as jnp
import numpy as np
from jax import lax
from jax.experimental import pallas as pl
from jax.experimental.pallas import tpu as pltpu
from jax.sharding import PartitionSpec as P

IMAGE = 2048
LANES = 128
SLOTS = 2
steepness = 6.0
threshold = 0.3
f32 = jnp.float32
bf16 = jnp.bfloat16


def basis_slots(band):
    half = band // 2
    slots = np.arange(band)
    is_sin = (slots >= half) & (slots < band - 1)
    freq = np.where(slots < half, slots, np.where(is_sin, slots - (half - 1), half))
    return freq, is_sin


def basis_tables(band, width):
    freq, is_sin = basis_slots(band)
    fine = 2.0 * np.pi * ((np.arange(LANES)[:, None] * freq[None]) % width) / width
    big = 2.0 * np.pi * ((LANES * np.arange(width // LANES)[:, None] * freq[None]) % width) / width
    first = np.where(is_sin, np.sin(big), np.cos(big))
    second = np.where(is_sin, np.cos(big), -np.sin(big))
    edge = np.sin(2.0 * np.pi * ((np.arange(LANES) * (band // 2)) % width) / width)
    table = np.concatenate([np.cos(fine), np.sin(fine), first, second], axis=0)
    return table.astype(np.float32), edge.astype(np.float32)


def fold_table(band):
    half = band // 2
    both = np.zeros((2 * band, band), np.float32)
    for place in range(band):
        freq = place - half
        size = abs(freq)
        both[place, size if size < half else band - 1] = 1.0
        if 0 < size < half:
            both[band + place, half - 1 + size] = -1.0 if freq > 0 else 1.0
    return both


def wave(places, band, period):
    offsets = np.arange(band) - band // 2
    angle = 2.0 * np.pi * ((places[:, None] * offsets[None, :]) % period) / period
    return np.cos(angle), np.sin(angle)


def resample_table(band, image):
    coarse = 2 * band
    period = 2 * image
    base = np.arange(period)
    row = np.ones(period)
    for freq in range(1, band):
        row += 2.0 * np.cos(2.0 * np.pi * ((base * freq) % period) / period)
    row /= coarse
    place = (2 * np.arange(band) + 1) * (image // coarse)
    columns = 2 * np.arange(image)
    plus = row[(columns[None, :] - place[:, None]) % period]
    minus = row[(columns[None, :] + place[:, None]) % period]
    return np.concatenate([plus, minus], axis=0)


def halves(table):
    table = np.asarray(table, np.float32)
    top = table.astype(bf16)
    rest = (table - top.astype(np.float32)).astype(bf16)
    return top, rest


def split(value):
    top = value.astype(bf16)
    return top, (value - top.astype(f32)).astype(bf16)


def dot(left, right, left_dim=1, right_dim=0):
    return lax.dot_general(
        left, right, (((left_dim,), (right_dim,)), ((), ())), preferred_element_type=f32
    )


def dot_split(left, right, left_dim=1, right_dim=0):
    go = functools.partial(dot, left_dim=left_dim, right_dim=right_dim)
    return go(left[0], right[0]) + (go(left[1], right[0]) + go(left[0], right[1]))


def basis_rows(table, start, blocks):
    places = (table.shape[0] - 2 * LANES) // 2
    parts = []
    for block in range(blocks):
        a = table[pl.ds(2 * LANES + start + block, 1), :]
        b = table[pl.ds(2 * LANES + places + start + block, 1), :]
        parts.append(a * table[:LANES, :] + b * table[LANES : 2 * LANES, :])
    return parts[0] if blocks == 1 else jnp.concatenate(parts, axis=0)


def put(array, row, column, value):
    rows = lax.broadcasted_iota(jnp.int32, array.shape, 0)
    columns = lax.broadcasted_iota(jnp.int32, array.shape, 1)
    return jnp.where((rows == row) & (columns == column), value, array)


def store_pieces(out, array):
    band = array.shape[1]
    pieces = [array[:, place : place + LANES] for place in range(0, band, LANES)]
    flat = pieces[0] if len(pieces) == 1 else jnp.concatenate(pieces, axis=0)
    out[...] = flat.reshape(out.shape)


def load_pieces(ref, band):
    flat = ref[...].reshape(band * band // LANES, LANES)
    pieces = [flat[place : place + band] for place in range(0, flat.shape[0], band)]
    return pieces[0] if len(pieces) == 1 else jnp.concatenate(pieces, axis=1)


def mask_kernel(where, mask_hbm, table_hbm, edge_row, edge_col, out, mask, table, total, sems):
    count, rows_here, chunk = mask.shape
    band = total.shape[1]
    blocks = chunk // LANES

    def copy(place):
        columns = pl.ds(place * chunk, chunk)
        return pltpu.make_async_copy(mask_hbm.at[:, columns], mask.at[place], sems.at[place])

    copy_table = pltpu.make_async_copy(table_hbm, table, sems.at[count])
    copy(0).start()
    copy_table.start()
    for place in range(1, count):
        copy(place).start()
    copy_table.wait()
    side = jnp.zeros((1, LANES), f32)
    for place in range(count):
        copy(place).wait()
        transmit = jnp.tanh(mask[place])
        columns = split(basis_rows(table, place * blocks, blocks))
        value = dot_split(split(transmit), columns)
        if place == 0:
            total[...] = value
        else:
            total[...] += value
        line = jnp.sum(transmit, axis=0, keepdims=True)
        for start in range(0, chunk, LANES):
            side += line[:, start : start + LANES]
    row_part = total[...]
    rows = split(basis_rows(table, where[1], 1))
    packed = dot_split(rows, split(row_part), 0, 0)
    edge_u = jnp.sum(edge_col[...] * row_part[:, 0:1])
    edge_v = jnp.sum(edge_row[...] * side)
    packed = put(put(packed, band - 1, 1, edge_u), 1, band - 1, edge_v)
    store_pieces(out, packed)


def prepare_kernel(
    where,
    cutoff,
    corner,
    extent,
    corner_row,
    extent_row,
    y_big,
    y_fine,
    after,
    kernels,
    mask_hbm,
    table_hbm,
    target,
    kern,
    y_rows,
    y_cols,
    rows_hi,
    rows_lo,
    cols_hi,
    cols_lo,
    slope,
    table,
    sems,
):
    count, _, band, _ = kern.shape
    rows_here, image = target.shape
    cols_here = slope.shape[1]
    blocks = cols_here // LANES
    half = band // 2
    mine = pl.ds(pl.multiple_of(where[0] * cols_here, cols_here), cols_here)
    copy_table = pltpu.make_async_copy(table_hbm, table, sems.at[count])
    copy_mask = pltpu.make_async_copy(mask_hbm.at[:, mine], slope, sems.at[count + 1])

    def copy(place):
        return pltpu.make_async_copy(kernels.at[0, place], kern.at[place], sems.at[place])

    copy_table.start()
    copy_mask.start()
    for place in range(count):
        copy(place).start()

    rects = corner.shape[0]
    top = corner_row[0:1, :]
    rows = where[1] * rows_here + lax.broadcasted_iota(jnp.int32, (rows_here, rects), 0)
    rows_in = (rows >= top) & (rows < top + extent_row[0:1, :])
    rows_in = jnp.where(rows_in, 1.0, 0.0).astype(bf16)
    left = corner[:, 1:2]
    right = left + extent[:, 1:2]
    step = min(512, image)
    for place in range(0, image, step):
        columns = place + lax.broadcasted_iota(jnp.int32, (rects, step), 1)
        cols_in = jnp.where((columns >= left) & (columns < right), 1.0, 0.0).astype(bf16)
        target[:, place : place + step] = jnp.minimum(dot(rows_in, cols_in), 1.0)

    big_cos = y_big[0, pl.ds(where[1], 1), :]
    big_sin = y_big[1, pl.ds(where[1], 1), :]
    cos_y = (big_cos * y_fine[0] - big_sin * y_fine[1]) * (1.0 / band)
    sin_y = (big_sin * y_fine[0] + big_cos * y_fine[1]) * (1.0 / band)
    waves = jnp.concatenate(
        [
            jnp.concatenate([cos_y, 0.0 - sin_y], axis=1),
            jnp.concatenate([sin_y, cos_y], axis=1),
        ],
        axis=0,
    )
    waves_hi, waves_lo = split(waves)
    y_rows[...] = jnp.concatenate([waves_hi, waves_lo], axis=0)
    waves_hi, waves_lo = waves_hi.astype(f32), waves_lo.astype(f32)
    stacked = jnp.concatenate([waves_hi, waves_hi, waves_lo], axis=0)
    y_cols[...] = jnp.transpose(stacked).astype(bf16)

    copy_table.wait()
    hi, lo = split(basis_rows(table, where[1], 1))
    rows_hi[...] = hi
    rows_lo[...] = lo
    for block in range(blocks):
        here = pl.ds(block * LANES, LANES)
        hi, lo = split(basis_rows(table, where[0] * blocks + block, 1))
        cols_hi[here, :] = hi
        cols_lo[here, :] = lo
    copy_mask.wait()
    for start in range(0, cols_here, LANES):
        here = pl.ds(start, LANES)
        transmit = jnp.tanh(slope[:, here])
        slope[:, here] = 1.0 - transmit * transmit

    part = 64
    for start in range(0, band, part):
        here = pl.ds(start, part)
        fu = start - half + lax.broadcasted_iota(jnp.int32, (part, band), 0)
        fv = lax.broadcasted_iota(jnp.int32, (part, band), 1) - half
        radius = fu * fu + fv * fv
        for place in range(count):
            if start == 0:
                copy(place).wait()
            inside = radius <= cutoff[0, place] * cutoff[0, place]
            kern[place, 0, here, :] = jnp.where(inside, kern[place, 0, here, :], 0.0)
            kern[place, 1, here, :] = jnp.where(inside, kern[place, 1, here, :], 0.0)


def field_kernel(
    weight,
    dose,
    packed,
    kern,
    both,
    both_t,
    x_hi,
    x_lo,
    up_hi,
    up_lo,
    target,
    y_rows,
    y_cols,
    out,
    spec,
    prod_hi,
    prod_lo,
    wide_hi,
    wide_lo,
    deep_hi,
    deep_lo,
    cs,
    gain,
    back,
    gs,
    *,
    width,
):
    count, _, band, _ = kern.shape
    rows_here, image = target.shape
    half = band // 2
    total_rows = count * rows_here
    part = 64
    fu = lax.broadcasted_iota(jnp.int32, (band, band), 0) - half
    fv = lax.broadcasted_iota(jnp.int32, (band, band), 1) - half

    box = load_pieces(packed, band)
    edge_u = box[band - 1 : band, 1:2] * (1.0 / width)
    edge_v = box[1:2, band - 1 : band] * (1.0 / width)
    box_hi, box_lo = split(box * (1.0 / width))
    opened = dot(both[...], box_hi) + dot(both[...], box_lo)
    box_hi, box_lo = split(opened)
    opened = dot(box_hi, both[...], 1, 1) + dot(box_lo, both[...], 1, 1)
    spec_im = opened[band:, :band] + opened[:band, band:]
    spec[0] = opened[:band, :band] - opened[band:, band:]
    at_u = (fu == -half) & (fv == 0)
    at_v = (fu == 0) & (fv == -half)
    spec[1] = spec_im + jnp.where(at_u, edge_u, 0.0) + jnp.where(at_v, edge_v, 0.0)

    for place in range(count):
        slot = place % prod_hi.shape[0]
        for start in range(0, band, part):
            here = pl.ds(start, part)
            there = pl.ds(band + start, part)
            k_re = kern[place, 0, here, :]
            k_im = kern[place, 1, here, :]
            s_re = spec[0, here, :]
            s_im = spec[1, here, :]
            re_hi, re_lo = split(k_re * s_re - k_im * s_im)
            im_hi, im_lo = split(k_re * s_im + k_im * s_re)
            prod_hi[slot, here, :] = re_hi
            prod_lo[slot, here, :] = re_lo
            prod_hi[slot, there, :] = im_hi
            prod_lo[slot, there, :] = im_lo
        main = dot(y_rows[...], prod_hi[slot])
        rest = dot(y_rows[: 2 * rows_here, :], prod_lo[slot])
        hi, lo = split(main[: 2 * rows_here] + (main[2 * rows_here :] + rest))
        here = pl.ds(place * rows_here, rows_here)
        there = pl.ds(total_rows + place * rows_here, rows_here)
        wide_hi[here, :] = hi[:rows_here]
        wide_lo[here, :] = lo[:rows_here]
        wide_hi[there, :] = hi[rows_here:]
        wide_lo[there, :] = lo[rows_here:]

    cs[...] = dot_split((wide_hi[...], wide_lo[...]), (x_hi[...], x_lo[...]))

    def fields(place):
        here = pl.ds(place * rows_here, rows_here)
        there = pl.ds(total_rows + place * rows_here, rows_here)
        c_re = cs[here, :band]
        s_re = cs[here, band:]
        c_im = cs[there, :band]
        s_im = cs[there, band:]
        return (c_re - s_im, c_im + s_re, c_re + s_im, c_im - s_re), here, there

    plus = jnp.zeros((rows_here, band), f32)
    minus = jnp.zeros((rows_here, band), f32)
    for place in range(count):
        (p_re, p_im, m_re, m_im), _, _ = fields(place)
        scale = weight[0, place]
        plus += scale * (p_re * p_re + p_im * p_im)
        minus += scale * (m_re * m_re + m_im * m_im)
    power_hi, power_lo = split(jnp.concatenate([plus, minus], axis=1))
    power = jnp.concatenate([power_hi, power_lo], axis=0)
    dose_here = dose[0]
    scale = 2.0 * (width / band) * steepness * dose_here
    step = min(512, image)
    for place in range(0, image, step):
        here = pl.ds(place, step)
        main = dot(power, up_hi[:, here])
        rest = dot(power_hi, up_lo[:, here])
        intensity = main[:rows_here] + (main[rows_here:] + rest)
        level = steepness * (dose_here * intensity - threshold)
        resist = 1.0 / (1.0 + jnp.exp(0.0 - level))
        slope = scale * (resist - target[:, here]) * resist * (1.0 - resist)
        hi, lo = split(slope)
        gain[:rows_here, here] = hi
        gain[rows_here:, here] = lo
    main = dot(gain[...], up_hi[...], 1, 1)
    rest = dot(gain[:rows_here, :], up_lo[...], 1, 1)
    slope = 2.0 * (main[:rows_here] + (main[rows_here:] + rest))
    slope_plus = slope[:, :band]
    slope_minus = slope[:, band:]

    for place in range(count):
        (p_re, p_im, m_re, m_im), here, there = fields(place)
        scale = weight[0, place]
        plus = scale * slope_plus
        minus = scale * slope_minus
        p_re, p_im, m_re, m_im = plus * p_re, plus * p_im, minus * m_re, minus * m_im
        for rows, columns, value in (
            (here, slice(0, band), p_re + m_re),
            (here, slice(band, 2 * band), p_im - m_im),
            (there, slice(0, band), p_im + m_im),
            (there, slice(band, 2 * band), m_re - p_re),
        ):
            hi, lo = split(value)
            deep_hi[rows, columns] = hi
            deep_lo[rows, columns] = lo
    back[...] = dot_split((deep_hi[...], deep_lo[...]), (x_hi[...], x_lo[...]), 1, 1)

    for place in range(count):
        here = pl.ds(place * rows_here, rows_here)
        there = pl.ds(total_rows + place * rows_here, rows_here)
        hi, lo = split(jnp.concatenate([back[here, :], back[there, :]], axis=0))
        grad = dot(y_cols[...], jnp.concatenate([hi, lo, hi], axis=0))
        for start in range(0, band, part):
            here = pl.ds(start, part)
            k_re = kern[place, 0, here, :]
            k_im = kern[place, 1, here, :]
            g_re = grad[start : start + part]
            g_im = grad[band + start : band + start + part]
            if place == 0:
                gs[0, here, :] = k_re * g_re + k_im * g_im
                gs[1, here, :] = k_re * g_im - k_im * g_re
            else:
                gs[0, here, :] += k_re * g_re + k_im * g_im
                gs[1, here, :] += k_re * g_im - k_im * g_re
    g_re = gs[0]
    g_im = gs[1]
    edge_u = g_im[0:1, half : half + 1]
    edge_v = g_im[half : half + 1, 0:1]
    re_hi, re_lo = split(g_re)
    im_hi, im_lo = split(g_im)
    even, odd = both_t[:, :band], both_t[:, band:]
    left = dot(even, re_hi) + dot(even, re_lo) + dot(odd, im_hi) + dot(odd, im_lo)
    right = dot(even, im_hi) + dot(even, im_lo) - dot(odd, re_hi) - dot(odd, re_lo)
    l_hi, l_lo = split(left)
    r_hi, r_lo = split(right)
    even, odd = both[:band, :], both[band:, :]
    folded = dot(l_hi, even) + dot(l_lo, even) + dot(r_hi, odd) + dot(r_lo, odd)
    store_pieces(out, put(put(folded, band - 1, 1, edge_u), 1, band - 1, edge_v))


def spread_kernel(packed, slope, rows_hi, rows_lo, cols_hi, cols_lo, edge_row, edge_col, out, *, width):
    band = rows_hi.shape[1]
    count, cols_here = out.shape
    box = load_pieces(packed, band) * (1.0 / width)
    edge_u = box[band - 1 : band, 1:2]
    edge_v = box[1:2, band - 1 : band]
    box = put(put(box, band - 1, 1, 0.0), 1, band - 1, 0.0)
    mixed_hi, mixed_lo = split(dot_split((rows_hi[...], rows_lo[...]), split(box)))
    mixed = jnp.concatenate([mixed_hi, mixed_lo], axis=0)
    side = edge_u * edge_col[...] + edge_v * edge_row[...]
    step = min(512, cols_here)
    for start in range(0, cols_here, step):
        here = pl.ds(start, step)
        main = dot(mixed, cols_hi[here, :], 1, 1)
        rest = dot(mixed_hi, cols_lo[here, :], 1, 1)
        grad = main[:count] + (main[count:] + rest)
        for inner in range(0, step, LANES):
            there = pl.ds(start + inner, LANES)
            out[:, there] = (grad[:, inner : inner + LANES] + side) * slope[:, there]


def params(mebibytes):
    return pltpu.CompilerParams(vmem_limit_bytes=mebibytes * 1024 * 1024)


smem = pl.BlockSpec(memory_space=pltpu.SMEM)
vmem = pl.BlockSpec(memory_space=pltpu.VMEM)
anywhere = pl.BlockSpec(memory_space=pl.ANY)


def call_mask(where, mask_level, table, edge, pieces):
    rows_here, width = mask_level.shape
    band = table.shape[1]
    chunk = min(1024, width)
    steps = width // chunk
    return pl.pallas_call(
        mask_kernel,
        out_shape=jax.ShapeDtypeStruct(pieces, f32),
        in_specs=[smem, anywhere, anywhere, vmem, vmem],
        out_specs=vmem,
        scratch_shapes=[
            pltpu.VMEM((steps, rows_here, chunk), f32),
            pltpu.VMEM(table.shape, f32),
            pltpu.VMEM((rows_here, band), f32),
            pltpu.SemaphoreType.DMA((steps + 1,)),
        ],
        compiler_params=params(60),
        name="mask_rows",
    )(where, mask_level, table, edge[None, :], edge[:, None])


def call_prepare(where, band_cutoff, shape_corner, shape_extent, after, socs_kernels, mask_level, table, pencils, conds):
    rows_here, width = mask_level.shape
    _, count, _, band, _ = socs_kernels.shape
    image_rows = IMAGE // pencils
    cols_here = width // conds
    y_big = np.stack(wave(image_rows * np.arange(pencils), band, IMAGE)).astype(np.float32)
    y_fine = np.stack(wave(np.arange(image_rows), band, IMAGE)).astype(np.float32)
    shapes = [
        ((image_rows, IMAGE), f32),
        ((count, 2, band, band), f32),
        ((4 * image_rows, 2 * band), bf16),
        ((2 * band, 6 * image_rows), bf16),
        ((rows_here, band), bf16),
        ((rows_here, band), bf16),
        ((cols_here, band), bf16),
        ((cols_here, band), bf16),
        ((rows_here, cols_here), f32),
    ]
    return pl.pallas_call(
        prepare_kernel,
        out_shape=[jax.ShapeDtypeStruct(*shape) for shape in shapes],
        in_specs=[smem] * 2 + [vmem] * 6 + [anywhere] * 4,
        out_specs=[vmem] * len(shapes),
        scratch_shapes=[pltpu.VMEM(table.shape, f32), pltpu.SemaphoreType.DMA((count + 2,))],
        compiler_params=params(24),
        cost_estimate=pl.CostEstimate(flops=10**9, bytes_accessed=2 * 10**7, transcendentals=10**6),
        name="prepare",
    )(
        where,
        band_cutoff,
        shape_corner,
        shape_extent,
        shape_corner.T,
        shape_extent.T,
        y_big,
        y_fine,
        after,
        socs_kernels,
        mask_level,
        table,
    )


def call_field(kernel_weight, dose_scale, packed, kern, target, y_rows, y_cols, width):
    count, _, band, _ = kern.shape
    image_rows = target.shape[0]
    both = fold_table(band)
    x_cos, x_sin = wave(2 * np.arange(band) + 1, band, 4 * band)
    x_hi, x_lo = halves(np.concatenate([x_cos.T, x_sin.T], axis=1))
    up_hi, up_lo = halves(resample_table(band, IMAGE))
    deep = 2 * count * image_rows
    return pl.pallas_call(
        functools.partial(field_kernel, width=width),
        out_shape=jax.ShapeDtypeStruct(packed.shape, f32),
        in_specs=[smem] * 2 + [vmem] * 11,
        out_specs=vmem,
        scratch_shapes=[
            pltpu.VMEM((2, band, band), f32),
            pltpu.VMEM((SLOTS, 2 * band, band), bf16),
            pltpu.VMEM((SLOTS, 2 * band, band), bf16),
            pltpu.VMEM((deep, band), bf16),
            pltpu.VMEM((deep, band), bf16),
            pltpu.VMEM((deep, 2 * band), bf16),
            pltpu.VMEM((deep, 2 * band), bf16),
            pltpu.VMEM((deep, 2 * band), f32),
            pltpu.VMEM((2 * image_rows, IMAGE), bf16),
            pltpu.VMEM((deep, band), f32),
            pltpu.VMEM((2, band, band), f32),
        ],
        compiler_params=params(28),
        name="image_rows",
    )(
        kernel_weight,
        dose_scale,
        packed,
        kern,
        both.astype(bf16),
        both.T.astype(bf16),
        x_hi,
        x_lo,
        up_hi,
        up_lo,
        target,
        y_rows,
        y_cols,
    )


def call_spread(folded, slope, rows_hi, rows_lo, cols_hi, cols_lo, edge, width):
    return pl.pallas_call(
        functools.partial(spread_kernel, width=width),
        out_shape=jax.ShapeDtypeStruct(slope.shape, f32),
        in_specs=[vmem] * 8,
        out_specs=vmem,
        compiler_params=params(24),
        name="mask_gradient",
    )(folded, slope, rows_hi, rows_lo, cols_hi, cols_lo, edge[None, :], edge[:, None])


def local(
    mask_level, socs_kernels, band_cutoff, kernel_weight, dose_scale, shape_corner, shape_extent
):
    width = mask_level.shape[1]
    band = socs_kernels.shape[3]
    pencils = lax.axis_size("px")
    conds = lax.axis_size("cond")
    where = jnp.stack([lax.axis_index("cond"), lax.axis_index("px")]).astype(jnp.int32)
    pieces = (pencils, band * band // LANES // pencils, LANES)
    table, edge = basis_tables(band, width)

    packed = call_mask(where, mask_level, table, edge, pieces)
    piece = collect(packed)
    prepared = call_prepare(
        where, band_cutoff, shape_corner, shape_extent, piece, socs_kernels, mask_level, table, pencils, conds
    )
    target, kern, y_rows, y_cols, rows_hi, rows_lo, cols_hi, cols_lo, slope = prepared
    packed = hand_out(piece, pieces)
    folded = call_field(kernel_weight, dose_scale, packed, kern, target, y_rows, y_cols, width)
    piece = collect(folded)
    others = [
        lax.ppermute(piece, "cond", [(i, (i + d) % conds) for i in range(conds)])
        for d in range(1, conds)
    ]
    piece = functools.reduce(jnp.add, others, piece)
    folded = hand_out(piece, pieces)
    return call_spread(folded, slope, rows_hi, rows_lo, cols_hi, cols_lo, edge, width)


def collect(packed):
    arrived = lax.all_to_all(packed, "px", split_axis=0, concat_axis=0, tiled=True)
    return jnp.sum(arrived, axis=0)


def hand_out(piece, pieces):
    outgoing = jnp.broadcast_to(piece[None], pieces)
    return lax.all_to_all(outgoing, "px", split_axis=0, concat_axis=0, tiled=True)


def solution(mesh):
    in_specs = (
        P("px", None),
        P("cond", None, None, None, None),
        P("cond", None),
        P("cond", None),
        P("cond"),
        P(),
        P(),
    )
    out_specs = P("px", "cond")
    return jax.shard_map(local, mesh=mesh, in_specs=in_specs, out_specs=out_specs, check_vma=False)
```

time: 120 us -> 131 us (1.092)
  local copies, waits for them, and re-layouts: 13.3 us -> 34.4 us
  waiting for transfers between devices: 13.5 us -> 3.11 us
  starting transfers between devices: 20.6 us -> 13.7 us
  blocking collectives: 48.7 us -> 53.8 us
    unnamed x52 -> x74, local copies, waits for them, and re-layouts: 12.6 us -> 33.6 us
    all_to_all x1, waiting for transfers between devices: 7.8 us -> 0.01 us  [hand_out(): lax.all_to_all(outgoing, 'px', split_axis=0, concat_axis=0, tiled=True)]
    ppermute x6 -> x3, starting transfers between devices: 14.7 us -> 8.44 us  [local(): lax.ppermute(piece, 'cond', [(i, (i + d) % conds) for i in range(conds)])]
    all_to_all x3, blocking collectives: 48.7 us -> 53.8 us  [the longest x2 38.6 us: collect(): lax.all_to_all(packed, 'px', split_axis=0, concat_axis=0, tiled=True)]
    ppermute x6 -> x3, waiting for transfers between devices: 5.71 us -> 3.11 us  [local(): lax.ppermute(piece, 'cond', [(i, (i + d) % conds) for i in range(conds)])]
  transfers between devices with their start and end apart: 7 -> 4, of which waited for: 4 -> 1; matrix products, arithmetic and copies ran while one was open for 0% -> 1% of each run, Pallas kernels for 1% -> 2%
where the time goes in v1:
time: 131 us; the launch traced here: 130 us
  blocking collectives  53.8 us (41%)
  local copies, waits for them, and re-layouts  34.4 us (26%)
  Pallas kernels  23.4 us (18%)
  starting transfers between devices  13.7 us (10%)
  waiting for transfers between devices  3.11 us (2%)
    all_to_all x2, blocking collectives, collect(): lax.all_to_all(packed, 'px', split_axis=0, concat_axis=0, tiled=True)  38.6 us
    unnamed x74, local copies, waits for them, and re-layouts  33.6 us
    all_to_all x1, blocking collectives, hand_out(): lax.all_to_all(outgoing, 'px', split_axis=0, concat_axis=0, tiled=True)  15.2 us
    pallas_call x1, Pallas kernels, call_field(): pl.pallas_call(functools.partial(field_kernel, width=width), out_shape=ja...  10.7 us
    ppermute x3, starting transfers between devices, local(): lax.ppermute(piece, 'cond', [(i, (i + d) % conds) for i in range(conds)])  8.44 us
    pallas_call x1, Pallas kernels, call_mask(): pl.pallas_call(mask_kernel, out_shape=jax.ShapeDtypeStruct(pieces, f32),...  7.77 us
    all_to_all x1, starting transfers between devices, hand_out(): lax.all_to_all(outgoing, 'px', split_axis=0, concat_axis=0, tiled=True)  5.25 us
    ppermute x3, waiting for transfers between devices, local(): lax.ppermute(piece, 'cond', [(i, (i + d) % conds) for i in range(conds)])  3.11 us
  transfers between devices with their start and end apart: 4, of which 1 were waited for; matrix products, arithmetic and copies ran while one was open for 1% of the time, Pallas kernels for 2%

profile of v1, /device:TPU:1, one launch (start us, length us, event | category | flops | bytes accessed | tf_op | source)
XLA Modules:
  0.0 130.0 jit_solution(13512447302884124422)
XLA Ops:
  0.0 0.0 copy-start.6
  0.0 0.0 copy-start.30
  0.0 0.0 copy-start.31
  0.0 0.6 pad_add_fusion.where
  0.6 0.0 copy-start.33
  0.6 7.8 %mask_rows.1 = f32[64,8,128]{2,1,0:T(8,128)} custom-call(s32[2]{0:T(128)} %pad_add_fusion.where, f32[128,8192]{1,0:T(8,128)} %mask_hbm.3, f32[384,256]{1,0:T(8,128)} %constant.33.clone.table_hbm, f32[1,128]{1,0:T(1,128)} %constant.34.clone.edge_row, f32[128,1]{1,0:T(8,128)} %constant.35.clone.edge_col), custom_call_target="tpu_custom_call" | custom-call | tf_op jit(solution)/shard_map/mask_rows/pallas_call | solution.py:463
  8.4 20.1 %all_to_all.20 = f32[64,8,128]{2,1,0:T(8,128)S(1)} all-to-all(f32[64,8,128]{2,1,0:T(8,128)} %mask_rows.1), channel_id=1, replica_groups=mesh['cond'=4,'px'=64] {'px'}, dimensions={0} | all-to-all | bytes 524288 | tf_op jit(solution)/shard_map/all_to_all | solution.py:608
  28.5 0.1 reduce_sum.18.after
  28.6 0.8 broadcast_in_dim.4
  29.3 5.3 %all-to-all-start.1 = ((f32[64,8,128]{2,1,0:T(8,128)}), f32[64,8,128]{2,1,0:T(8,128)}, u32[]{:S(2)}, u32[]{:S(2)}) async-start(f32[64,8,128]{2,1,0:T(8,128)} %broadcast_in_dim.4), calls=%async_computation.1 | async-start | bytes 524288 | tf_op jit(solution)/shard_map/all_to_all | solution.py:614
  35.2 0.0 copy-done.30
  35.2 0.8 copy.21.corner
  36.0 0.0 copy-done.31
  36.0 0.8 copy.22.extent
  36.8 0.0 copy-done.6
  36.8 0.0 copy-done.33
  36.8 2.2 %copy-done = f32[128,8192]{1,0:T(8,128)S(1)} copy-done((f32[128,8192]{1,0:T(8,128)S(1)}, f32[128,8192]{1,0:T(8,128)}, u32[]{:S(2)}) %copy-start) | copy-done | bytes 4194328
  39.0 0.0 copy-start.1
  39.0 2.8 %copy-done.1 = f32[1,12,2,256,256]{4,3,2,1,0:T(8,128)S(1)} copy-done((f32[1,12,2,256,256]{4,3,2,1,0:T(8,128)S(1)}, f32[1,12,2,256,256]{4,3,2,1,0:T(8,128)}, u32[]{:S(2)}) %copy-start.1) | copy-done | bytes 6291480
  41.8 0.9 copy-done.11
  42.7 0.9 copy-done.12
  43.6 0.9 copy-done.22
  44.5 0.8 copy-done.29
  45.4 0.7 copy-done.34
  46.0 3.0 %prepare.1 = (f32[32,2048]{1,0:T(8,128)S(1)}, f32[12,2,256,256]{3,2,1,0:T(8,128)S(1)}, bf16[128,512]{1,0:T(8,128)(2,1)S(1)}, bf16[512,192]{1,0:T(8,128)(2,1)S(1)...) custom-call(s32[2]{0:T(128)S(1)} %copy-done.33, ...), custom_call_target="tpu_custom_call" | custom-call | flops 1000000000 | bytes 20000000 | tf_op jit(solution)/shard_map/prepare/pallas_call | solution.py:497
  49.1 0.0 copy-start.2
  49.1 2.6 %copy-done.2 = f32[12,2,256,256]{3,2,1,0:T(8,128)} copy-done((f32[12,2,256,256]{3,2,1,0:T(8,128)}, f32[12,2,256,256]{3,2,1,0:T(8,128)S(1)}, u32[]{:S(2)}) %copy-start.2) | copy-done | bytes 6291480
  51.7 1.0 copy-done.7
  52.7 1.0 copy-done.9
  53.6 0.7 copy-done.18
  54.4 0.7 copy-done.20
  55.1 0.7 copy-done.23
  55.7 0.6 copy-done.25
  56.4 0.6 copy-done.27
  57.0 0.0 all-to-all-done.1.packed
  57.0 0.0 copy-done.4
  57.0 2.8 %copy-done.3 = f32[12,2,256,256]{3,2,1,0:T(8,128)S(1)} copy-done((f32[12,2,256,256]{3,2,1,0:T(8,128)S(1)}, f32[12,2,256,256]{3,2,1,0:T(8,128)}, u32[]{:S(2)}) %copy-start.3) | copy-done | bytes 6291480
  59.8 1.6 %copy-done.5 = bf16[512,2048]{1,0:T(8,128)(2,1)S(1)} copy-done((bf16[512,2048]{1,0:T(8,128)(2,1)S(1)}, bf16[512,2048]{1,0:T(8,128)(2,1)}, u32[]{:S(2)}) %copy-start.5) | copy-done | bytes 2097176
  61.4 0.9 copy-done.14
  62.3 0.9 copy-done.15
  63.3 0.9 copy-done.16
  64.2 0.9 copy-done.17
  65.2 0.9 copy-done.19
  66.1 0.9 copy-done.21
  67.1 0.9 copy-done.24
  68.0 0.7 copy-done.35
  68.6 10.7 %image_rows.1 = f32[64,8,128]{2,1,0:T(8,128)S(1)} custom-call(f32[1,12]{1,0:T(1,128)S(1)} %copy-done.35, f32[1]{0:T(128)S(6)} %copy.23.dose, f32[64,8,128]{2,1,0:T(8,128)} %all-to-all-done.1.packed, f32[12,2,256,256]{3,2,1,0:T(8,128)S(1)} %copy-done.3, bf16[512,256]{1,0:T(8,128)(2,1)S(1)} %copy-done.17, bf16[256,512]{1,0:T(8,128)(2,1)S(1)} %copy-done.16, ...), custom_call_target="tpu_custom_call" | custom-call | tf_op jit(solution)/shard_map/image_rows/pallas_call | solution.py:530
  79.4 18.5 %all_to_all.21 = f32[64,8,128]{2,1,0:T(8,128)S(1)} all-to-all(f32[64,8,128]{2,1,0:T(8,128)S(1)} %image_rows.1), channel_id=1, replica_groups=mesh['cond'=4,'px'=64] {'px'}, dimensions={0} | all-to-all | bytes 524288 | tf_op jit(solution)/shard_map/all_to_all | solution.py:608
  97.9 0.1 reduce_sum.19
  98.0 5.2 %collective-permute-start.2 = (f32[8,128]{1,0:T(8,128)S(1)}, f32[8,128]{1,0:T(8,128)S(1)}, u32[]{:S(2)}, u32[]{:S(2)}) collective-permute-start(f32[8,128]{1,0:T(8,128)S(1)} %reduce_sum.19), channel_id=1, source_target_pairs={{0,192},{64,0},{128,64},{192,128},{1,193},{65,1},{129,65},{193,129... | collective-permute-start | bytes 12296 | tf_op jit(solution)/shard_map/ppermute | solution.py:599
  103.2 1.2 collective-permute-start.1
  104.4 2.0 %collective-permute-start = (f32[8,128]{1,0:T(8,128)S(1)}, f32[8,128]{1,0:T(8,128)S(1)}, u32[]{:S(2)}, u32[]{:S(2)}) collective-permute-start(f32[8,128]{1,0:T(8,128)S(1)} %reduce_sum.19), channel_id=1, source_target_pairs={{0,64},{64,128},{128,192},{192,0},{1,65},{65,129},{129,193},{193,1... | collective-permute-start | bytes 12296 | tf_op jit(solution)/shard_map/ppermute | solution.py:599
  106.4 0.0 collective-permute-done.2
  106.4 3.1 %collective-permute-done.1 = f32[8,128]{1,0:T(8,128)S(1)} collective-permute-done((f32[8,128]{1,0:T(8,128)S(1)}, f32[8,128]{1,0:T(8,128)S(1)}, u32[]{:S(2)}, u32[]{:S(2)}) %collective-permute-start.1) | collective-permute-done | bytes 4128 | tf_op jit(solution)/shard_map/ppermute | solution.py:599
  109.5 0.0 collective-permute-done
  109.6 15.2 %all_to_all.22.packed = f32[64,8,128]{2,1,0:T(8,128)S(1)} all-to-all(f32[64,8,128]{2,1,0:T(8,128)S(1)} %broadcast_in_dim.5), channel_id=1, replica_groups=mesh['cond'=4,'px'=64] {'px'}, dimensions={0} | all-to-all | bytes 524288 | tf_op jit(solution)/shard_map/all_to_all | solution.py:614
  124.8 0.0 copy-done.13
  124.8 0.0 copy-done.26
  124.8 0.0 copy-done.32
  124.8 0.0 copy-start.8
  124.8 1.2 copy-done.8
  126.0 1.2 copy-done.10
  127.2 0.8 copy-done.28
  128.1 1.9 %mask_gradient.1 = f32[128,2048]{1,0:T(8,128)} custom-call(f32[64,8,128]{2,1,0:T(8,128)S(1)} %all_to_all.22.packed, f32[128,2048]{1,0:T(8,128)S(1)} %copy-done.10, bf16[128,256]{1,0:T(8,128)(2,1)S(1)} %copy-done.26, bf16[128,256]{1,0:T(8,128)(2,1)S(1)} %copy-done.28, bf16[2048,256]{1,0:T(8,128)(2,1)S(1)} %get-tuple-element.21.cols_hi, ...), custom_call_target="tpu_custom_call" | custom-call | tf_op jit(solution)/shard_map/mask_gradient/pallas_call | solution.py:568
  (31 shorter events, 0.1 us)
Async XLA Ops:
  0.0 36.8 %copy-start.6 = (f32[384,256]{1,0:T(8,128)S(1)}, f32[384,256]{1,0:T(8,128)}, u32[]{:S(2)}) copy-start(f32[384,256]{1,0:T(8,128)} %constant.33.clone.table_hbm) | copy-start | bytes 1179652
  0.0 35.2 %copy-start.30 = (s32[256,2]{0,1:T(2,128)S(1)}, s32[256,2]{0,1:T(2,128)}, u32[]{:S(2)}) copy-start(s32[256,2]{0,1:T(2,128)} %param.25) | copy-start | bytes 6148
  0.0 36.0 %copy-start.31 = (s32[256,2]{0,1:T(2,128)S(1)}, s32[256,2]{0,1:T(2,128)}, u32[]{:S(2)}) copy-start(s32[256,2]{0,1:T(2,128)} %param.26) | copy-start | bytes 6148
  0.6 36.2 %copy-start.33 = (s32[2]{0:T(128)S(1)}, s32[2]{0:T(128)}, u32[]{:S(2)}) copy-start(s32[2]{0:T(128)} %pad_add_fusion.where) | copy-start | bytes 28
  29.3 27.7 %all-to-all-start.1 = ((f32[64,8,128]{2,1,0:T(8,128)}), f32[64,8,128]{2,1,0:T(8,128)}, u32[]{:S(2)}, u32[]{:S(2)}) async-start(f32[64,8,128]{2,1,0:T(8,128)} %broadcast_in_dim.4), calls=%async_computation.1 | async-start | bytes 524288 | tf_op jit(solution)/shard_map/all_to_all | solution.py:614
  36.8 2.2 %copy-start = (f32[128,8192]{1,0:T(8,128)S(1)}, f32[128,8192]{1,0:T(8,128)}, u32[]{:S(2)}) copy-start(f32[128,8192]{1,0:T(8,128)} %mask_hbm.3) | copy-start | bytes 12582916
  39.0 2.8 %copy-start.1 = (f32[1,12,2,256,256]{4,3,2,1,0:T(8,128)S(1)}, f32[1,12,2,256,256]{4,3,2,1,0:T(8,128)}, u32[]{:S(2)}) copy-start(f32[1,12,2,256,256]{4,3,2,1,0:T(8,128)} %kernels.1) | copy-start | bytes 18874372
  41.8 0.9 copy-start.11
  42.7 0.9 copy-start.12
  43.6 0.9 copy-start.22
  44.5 0.8 copy-start.29
  45.4 0.7 copy-start.34
  46.0 11.0 %copy-start.4 = (bf16[512,2048]{1,0:T(8,128)(2,1)S(1)}, bf16[512,2048]{1,0:T(8,128)(2,1)}, u32[]{:S(2)}) copy-start(bf16[512,2048]{1,0:T(8,128)(2,1)} %constant.43.clone.up_lo) | copy-start | bytes 6291460
  49.1 2.6 %copy-start.2 = (f32[12,2,256,256]{3,2,1,0:T(8,128)}, f32[12,2,256,256]{3,2,1,0:T(8,128)S(1)}, u32[]{:S(2)}) copy-start(f32[12,2,256,256]{3,2,1,0:T(8,128)S(1)} %get-tuple-element.14.kern) | copy-start | bytes 18874372
  51.7 1.0 copy-start.7
  52.7 1.0 copy-start.9
  53.6 0.7 copy-start.18
  54.3 0.7 copy-start.20
  55.1 0.7 copy-start.23
  55.7 0.6 copy-start.25
  56.4 0.6 copy-start.27
  57.0 2.8 %copy-start.3 = (f32[12,2,256,256]{3,2,1,0:T(8,128)S(1)}, f32[12,2,256,256]{3,2,1,0:T(8,128)}, u32[]{:S(2)}) copy-start(f32[12,2,256,256]{3,2,1,0:T(8,128)} %copy-done.2) | copy-start | bytes 18874372
  59.8 1.6 %copy-start.5 = (bf16[512,2048]{1,0:T(8,128)(2,1)S(1)}, bf16[512,2048]{1,0:T(8,128)(2,1)}, u32[]{:S(2)}) copy-start(bf16[512,2048]{1,0:T(8,128)(2,1)} %constant.42.clone.up_hi) | copy-start | bytes 6291460
  61.4 0.9 copy-start.14
  62.3 0.9 copy-start.15
  63.3 0.9 copy-start.16
  64.2 0.9 copy-start.17
  65.2 0.9 copy-start.19
  66.1 0.9 copy-start.21
  67.1 0.9 copy-start.24
  68.0 0.7 copy-start.35
  68.6 56.2 %copy-start.13 = (f32[128,1]{1,0:T(8,128)S(1)}, f32[128,1]{1,0:T(8,128)}, u32[]{:S(2)}) copy-start(f32[128,1]{1,0:T(8,128)} %constant.35.clone.edge_col) | copy-start | bytes 1540
  68.6 56.2 %copy-start.26 = (bf16[128,256]{1,0:T(8,128)(2,1)S(1)}, bf16[128,256]{1,0:T(8,128)(2,1)}, u32[]{:S(2)}) copy-start(bf16[128,256]{1,0:T(8,128)(2,1)} %copy-done.25) | copy-start | bytes 196612
  68.6 56.2 %copy-start.32 = (f32[1,128]{1,0:T(1,128)S(1)}, f32[1,128]{1,0:T(1,128)}, u32[]{:S(2)}) copy-start(f32[1,128]{1,0:T(1,128)} %constant.34.clone.edge_row) | copy-start | bytes 1540
  98.0 8.4 %collective-permute-start.2 = (f32[8,128]{1,0:T(8,128)S(1)}, f32[8,128]{1,0:T(8,128)S(1)}, u32[]{:S(2)}, u32[]{:S(2)}) collective-permute-start(f32[8,128]{1,0:T(8,128)S(1)} %reduce_sum.19), channel_id=1, source_target_pairs={{0,192},{64,0},{128,64},{192,128},{1,193},{65,1},{129,65},{193,129... | collective-permute-start | bytes 12296 | tf_op jit(solution)/shard_map/ppermute | solution.py:599
  103.2 6.4 %collective-permute-start.1 = (f32[8,128]{1,0:T(8,128)S(1)}, f32[8,128]{1,0:T(8,128)S(1)}, u32[]{:S(2)}, u32[]{:S(2)}) collective-permute-start(f32[8,128]{1,0:T(8,128)S(1)} %reduce_sum.19), channel_id=1, source_target_pairs={{0,128},{64,192},{128,0},{192,64},{1,129},{65,193},{129,1},{193,65... | collective-permute-start | bytes 12296 | tf_op jit(solution)/shard_map/ppermute | solution.py:599
  104.4 5.2 %collective-permute-start = (f32[8,128]{1,0:T(8,128)S(1)}, f32[8,128]{1,0:T(8,128)S(1)}, u32[]{:S(2)}, u32[]{:S(2)}) collective-permute-start(f32[8,128]{1,0:T(8,128)S(1)} %reduce_sum.19), channel_id=1, source_target_pairs={{0,64},{64,128},{128,192},{192,0},{1,65},{65,129},{129,193},{193,1... | collective-permute-start | bytes 12296 | tf_op jit(solution)/shard_map/ppermute | solution.py:599
  124.8 1.2 copy-start.8
  126.0 1.2 copy-start.10
  127.2 0.8 copy-start.28

commit v2 on v1

v2 whole, which is shorter than its diff:
```python
import functools
import math

import jax
import jax.numpy as jnp
import numpy as np
from jax import lax
from jax.experimental import pallas as pl
from jax.experimental.pallas import tpu as pltpu
from jax.sharding import PartitionSpec as P

IMAGE = 2048
LANES = 128
SLOTS = 2
ROOM = 60
AHEAD = 4
steepness = 6.0
threshold = 0.3
f32 = jnp.float32
bf16 = jnp.bfloat16


def basis_slots(band):
    half = band // 2
    even = np.arange(0, half, 2)
    odd = np.arange(1, half, 2)
    freq = np.concatenate([even, even[1:], [half], odd, odd])
    is_sin = np.concatenate([0 * even, 1 + 0 * even[1:], [0], 0 * odd, 1 + 0 * odd]) > 0
    return freq, is_sin


def basis_tables(band, width):
    freq, is_sin = basis_slots(band)
    fine = 2.0 * np.pi * ((np.arange(LANES)[:, None] * freq[None]) % width) / width
    big = 2.0 * np.pi * ((LANES * np.arange(width // LANES)[:, None] * freq[None]) % width) / width
    first = np.where(is_sin, np.sin(big), np.cos(big))
    second = np.where(is_sin, np.cos(big), -np.sin(big))
    edge = np.sin(2.0 * np.pi * ((np.arange(LANES) * (band // 2)) % width) / width)
    edge = np.tile(edge, (8, band // LANES))
    table = np.concatenate([np.cos(fine), np.sin(fine), first, second, edge], axis=0)
    return table.astype(np.float32)


def fold_table(band):
    half = band // 2
    freq, is_sin = basis_slots(band)
    both = np.zeros((2 * band, band), np.float32)
    for slot in range(band):
        places = [half - freq[slot]] if freq[slot] == half else [half - freq[slot], half + freq[slot]]
        for place in places:
            if is_sin[slot]:
                both[band + place, slot] = -1.0 if place > half else 1.0
            else:
                both[place, slot] = 1.0
    return both


def wave(places, band, period):
    offsets = np.arange(band) - band // 2
    angle = 2.0 * np.pi * ((places[:, None] * offsets[None, :]) % period) / period
    return np.cos(angle), np.sin(angle)


def resample_table(band, image):
    assert image == 8 * band
    base = np.arange(image)
    row = np.ones(image)
    for freq in range(1, band):
        row += 2.0 * np.cos(2.0 * np.pi * ((base * freq) % image) / image)
    row /= 2 * band
    place = 4 * np.arange(band)[:, None] + 2
    odd = 2 * np.arange(2 * band)[None, :] + 1
    near, far = row[(odd - place) % image], row[(odd + place) % image]
    fourth = 4 * np.arange(2 * band)[None, :]
    direct = [row[(fourth - place) % image], row[(fourth + place) % image]]
    return np.concatenate([(near + far) / 2, (near - far) / 2, *direct], axis=0)


def column_runs(band, image):
    return (
        (0, band, 2, 4),
        (band, band, image - 2, -4),
        (2 * band, 2 * band, 1, 2),
        (4 * band, 2 * band, image - 1, -2),
        (6 * band, 2 * band, 0, 4),
    )


def halves(table):
    table = np.asarray(table, np.float32)
    top = table.astype(bf16)
    rest = (table - top.astype(np.float32)).astype(bf16)
    return top, rest


def split(value):
    top = value.astype(bf16)
    return top, (value - top.astype(f32)).astype(bf16)


def dot(left, right, left_dim=1, right_dim=0):
    return lax.dot_general(
        left, right, (((left_dim,), (right_dim,)), ((), ())), preferred_element_type=f32
    )


def dot_split(left, right, left_dim=1, right_dim=0):
    go = functools.partial(dot, left_dim=left_dim, right_dim=right_dim)
    return go(left[0], right[0]) + (go(left[1], right[0]) + go(left[0], right[1]))


def basis_rows(table, start, blocks):
    places = (table.shape[0] - 2 * LANES - 8) // 2
    parts = []
    for block in range(blocks):
        a = table[pl.ds(2 * LANES + start + block, 1), :]
        b = table[pl.ds(2 * LANES + places + start + block, 1), :]
        parts.append(a * table[:LANES, :] + b * table[LANES : 2 * LANES, :])
    return parts[0] if blocks == 1 else jnp.concatenate(parts, axis=0)


def edges(table):
    last = table.shape[0] - 8
    half = table.shape[1] // 2
    return table[last : last + 1, :LANES], table[LANES : 2 * LANES, half - 1 : half]


def put(array, row, column, value):
    rows = lax.broadcasted_iota(jnp.int32, array.shape, 0)
    columns = lax.broadcasted_iota(jnp.int32, array.shape, 1)
    return jnp.where((rows == row) & (columns == column), value, array)


def store_pieces(out, array):
    band = array.shape[1]
    pieces = [array[:, place : place + LANES] for place in range(0, band, LANES)]
    flat = pieces[0] if len(pieces) == 1 else jnp.concatenate(pieces, axis=0)
    out[...] = flat.reshape(out.shape)


def load_pieces(ref, band):
    flat = ref[...].reshape(band * band // LANES, LANES)
    pieces = [flat[place : place + band] for place in range(0, flat.shape[0], band)]
    return pieces[0] if len(pieces) == 1 else jnp.concatenate(pieces, axis=1)


def mask_kernel(mask_hbm, table_hbm, out, mask, table, even, odd, sems):
    count, rows_here, chunk = mask.shape
    band = even.shape[1] // 2 * 2
    half = band // 2
    blocks = chunk // LANES
    pairs = count // 2
    order = [place + side * pairs for place in range(pairs) for side in range(2)]

    def copy(place):
        columns = pl.ds(place * chunk, chunk)
        return pltpu.make_async_copy(mask_hbm.at[:, columns], mask.at[place], sems.at[place])

    copy_table = pltpu.make_async_copy(table_hbm, table, sems.at[count])
    copy(order[0]).start()
    copy(order[1]).start()
    copy_table.start()
    for place in order[2:AHEAD]:
        copy(place).start()
    copy_table.wait()
    line = jnp.zeros((1, LANES), f32)
    for place in range(pairs):
        copy(place).wait()
        copy(place + pairs).wait()
        for ahead in order[2 * place + AHEAD : 2 * place + AHEAD + 2]:
            copy(ahead).start()
        near = jnp.tanh(mask[place])
        far = jnp.tanh(mask[place + pairs])
        hi, lo = split(basis_rows(table, place * blocks, blocks))
        for total, value, columns in (
            (even, near + far, slice(0, half)),
            (odd, near - far, slice(half, band)),
        ):
            weights = jnp.concatenate([hi[:, columns], lo[:, columns]], axis=1)
            product = dot(jnp.concatenate(split(value), axis=0), weights)
            if place == 0:
                total[...] = product
            else:
                total[...] += product
        both_sum = jnp.sum(near + far, axis=0, keepdims=True)
        for start in range(0, chunk, LANES):
            line += both_sum[:, start : start + LANES]
    parts = []
    for total in (even, odd):
        part = total[:rows_here, :] + total[rows_here:, :]
        parts.append(part[:, :half] + part[:, half:])
    row_part = jnp.concatenate(parts, axis=1)
    rows = split(basis_rows(table, lax.axis_index("px"), 1))
    packed = dot_split(rows, split(row_part), 0, 0)
    edge_row, edge_col = edges(table)
    edge_u = jnp.sum(edge_col * row_part[:, 0:1])
    edge_v = jnp.sum(edge_row * line)
    packed = put(put(packed, half - 1, 1, edge_u), 1, half - 1, edge_v)
    store_pieces(out, packed)


def prepare_kernel(
    corner,
    extent,
    y_big,
    y_fine,
    table,
    after,
    mask_hbm,
    target,
    y_rows,
    y_cols,
    rows,
    cols,
    slope,
    sem,
):
    band = table.shape[1]
    rows_here, image = target.shape
    cols_here = slope.shape[1]
    blocks = cols_here // LANES
    place_px = lax.axis_index("px")
    place_cond = lax.axis_index("cond")
    mine = pl.ds(pl.multiple_of(place_cond * cols_here, cols_here), cols_here)
    copy_mask = pltpu.make_async_copy(mask_hbm.at[:, mine], slope, sem)
    copy_mask.start()

    rects = corner.shape[1]
    top = corner[0:1, :]
    bottom = top + extent[0:1, :]
    left = corner[1:2, :]
    right = left + extent[1:2, :]
    places = place_px * rows_here + lax.broadcasted_iota(jnp.int32, (rows_here, rects), 0)
    rows_in = jnp.where((places >= top) & (places < bottom), 1.0, 0.0).astype(bf16)
    for start, count, first, stride in column_runs(band, image):
        places = first + stride * lax.broadcasted_iota(jnp.int32, (count, rects), 0)
        cols_in = jnp.where((places >= left) & (places < right), 1.0, 0.0).astype(bf16)
        target[:, start : start + count] = jnp.minimum(dot(rows_in, cols_in, 1, 1), 1.0)

    big_cos = y_big[0, pl.ds(place_px, 1), :]
    big_sin = y_big[1, pl.ds(place_px, 1), :]
    cos_y = (big_cos * y_fine[0] - big_sin * y_fine[1]) * (1.0 / band)
    sin_y = (big_sin * y_fine[0] + big_cos * y_fine[1]) * (1.0 / band)
    waves = jnp.concatenate(
        [
            jnp.concatenate([cos_y, 0.0 - sin_y], axis=1),
            jnp.concatenate([sin_y, cos_y], axis=1),
        ],
        axis=0,
    )
    waves_hi, waves_lo = split(waves)
    y_rows[...] = jnp.concatenate([waves_hi, waves_lo], axis=0)
    waves_hi, waves_lo = waves_hi.astype(f32), waves_lo.astype(f32)
    stacked = jnp.concatenate([waves_hi, waves_hi, waves_lo], axis=0)
    y_cols[...] = jnp.transpose(stacked).astype(bf16)

    hi, lo = split(basis_rows(table, place_px, 1))
    rows[0] = hi
    rows[1] = lo
    for block in range(blocks):
        here = pl.ds(block * LANES, LANES)
        hi, lo = split(basis_rows(table, place_cond * blocks + block, 1))
        cols[0, here, :] = hi
        cols[1, here, :] = lo
    copy_mask.wait()
    for start in range(0, cols_here, LANES):
        here = pl.ds(start, LANES)
        transmit = jnp.tanh(slope[:, here])
        slope[:, here] = 1.0 - transmit * transmit


def field_kernel(
    cutoff_hbm,
    weight_hbm,
    dose_hbm,
    packed_hbm,
    both_hbm,
    y_rows_hbm,
    kernels,
    x_hbm,
    up_hbm,
    target_hbm,
    y_cols_hbm,
    both_t_hbm,
    out,
    cutoff,
    weight,
    dose,
    packed,
    both,
    y_rows,
    kern,
    x_wave,
    up,
    target,
    y_cols,
    both_t,
    spec,
    radius,
    prod_hi,
    prod_lo,
    wide_hi,
    wide_lo,
    deep_hi,
    deep_lo,
    cs,
    back,
    gs,
    sems,
    kern_sems,
    *,
    width,
):
    count, _, band, _ = kern.shape
    rows_here, image = target.shape
    half = band // 2
    total_rows = count * rows_here
    part = 64
    pairs = (
        (packed_hbm, packed),
        (cutoff_hbm, cutoff),
        (weight_hbm, weight),
        (dose_hbm, dose),
        (both_hbm, both),
        (y_rows_hbm, y_rows),
        (x_hbm, x_wave),
        (up_hbm, up),
        (target_hbm, target),
        (y_cols_hbm, y_cols),
        (both_t_hbm, both_t),
    )
    copies = [pltpu.make_async_copy(*pair, sems.at[place]) for place, pair in enumerate(pairs)]
    copy_x, copy_up, copy_target, copy_y_cols, copy_both_t = copies[6:]

    def copy(place):
        return pltpu.make_async_copy(kernels.at[0, place], kern.at[place], kern_sems.at[place])

    for early in copies[:6]:
        early.start()
    later = [copy(place) for place in range(count)] + copies[6:]
    for item in later[:AHEAD]:
        item.start()
    fu = lax.broadcasted_iota(jnp.int32, (band, band), 0) - half
    fv = lax.broadcasted_iota(jnp.int32, (band, band), 1) - half
    radius[...] = fu * fu + fv * fv
    for early in copies[:6]:
        early.wait()

    box = load_pieces(packed, band)
    edge_u = box[half - 1 : half, 1:2] * (1.0 / width)
    edge_v = box[1:2, half - 1 : half] * (1.0 / width)
    box_hi, box_lo = split(box * (1.0 / width))
    opened = dot(both[...], box_hi) + dot(both[...], box_lo)
    box_hi, box_lo = split(opened)
    opened = dot(box_hi, both[...], 1, 1) + dot(box_lo, both[...], 1, 1)
    spec_im = opened[band:, :band] + opened[:band, band:]
    spec[0] = opened[:band, :band] - opened[band:, band:]
    at_u = (fu == -half) & (fv == 0)
    at_v = (fu == 0) & (fv == -half)
    spec[1] = spec_im + jnp.where(at_u, edge_u, 0.0) + jnp.where(at_v, edge_v, 0.0)

    for place in range(count):
        copy(place).wait()
        if place + AHEAD < len(later):
            later[place + AHEAD].start()
        limit = cutoff[0, place] * cutoff[0, place]
        slot = place % prod_hi.shape[0]
        for start in range(0, band, part):
            here = pl.ds(start, part)
            there = pl.ds(band + start, part)
            inside = radius[here, :] <= limit
            k_re = jnp.where(inside, kern[place, 0, here, :], 0.0)
            k_im = jnp.where(inside, kern[place, 1, here, :], 0.0)
            kern[place, 0, here, :] = k_re
            kern[place, 1, here, :] = k_im
            s_re = spec[0, here, :]
            s_im = spec[1, here, :]
            re_hi, re_lo = split(k_re * s_re - k_im * s_im)
            im_hi, im_lo = split(k_re * s_im + k_im * s_re)
            prod_hi[slot, here, :] = re_hi
            prod_lo[slot, here, :] = re_lo
            prod_hi[slot, there, :] = im_hi
            prod_lo[slot, there, :] = im_lo
        main = dot(y_rows[...], prod_hi[slot])
        rest = dot(y_rows[: 2 * rows_here, :], prod_lo[slot])
        hi, lo = split(main[: 2 * rows_here] + (main[2 * rows_here :] + rest))
        here = pl.ds(place * rows_here, rows_here)
        there = pl.ds(total_rows + place * rows_here, rows_here)
        wide_hi[here, :] = hi[:rows_here]
        wide_lo[here, :] = lo[:rows_here]
        wide_hi[there, :] = hi[rows_here:]
        wide_lo[there, :] = lo[rows_here:]

    for item in later[count + AHEAD :]:
        item.start()
    copy_x.wait()
    cs[...] = dot_split((wide_hi[...], wide_lo[...]), (x_wave[0], x_wave[1]))

    def fields(place):
        here = pl.ds(place * rows_here, rows_here)
        there = pl.ds(total_rows + place * rows_here, rows_here)
        c_re = cs[here, :band]
        s_re = cs[here, band:]
        c_im = cs[there, :band]
        s_im = cs[there, band:]
        return (c_re - s_im, c_im + s_re, c_re + s_im, c_im - s_re), here, there

    plus = jnp.zeros((rows_here, band), f32)
    minus = jnp.zeros((rows_here, band), f32)
    for place in range(count):
        (p_re, p_im, m_re, m_im), _, _ = fields(place)
        scale = weight[0, place]
        plus += scale * (p_re * p_re + p_im * p_im)
        minus += scale * (m_re * m_re + m_im * m_im)
    dose_here = dose[0]
    scale = 2.0 * (width / band) * steepness * dose_here

    def slope_of(intensity, start):
        level = steepness * (dose_here * intensity - threshold)
        resist = 1.0 / (1.0 + jnp.exp(0.0 - level))
        aim = target[:, start : start + intensity.shape[1]]
        return scale * (resist - aim) * resist * (1.0 - resist)

    def resample(value, rows, transposed):
        hi, lo = split(value)
        dim = 1 if transposed else 0
        main = dot(jnp.concatenate([hi, lo], axis=0), up[0, rows, :], 1, dim)
        rest = dot(hi, up[1, rows, :], 1, dim)
        return main[:rows_here] + (main[rows_here:] + rest)

    sums, gaps, whole_rows = slice(0, band), slice(band, 2 * band), slice(2 * band, 4 * band)
    copy_up.wait()
    copy_target.wait()
    sum_part = resample(plus + minus, sums, False)
    gap_part = resample(plus - minus, gaps, False)
    fourth = resample(jnp.concatenate([plus, minus], axis=1), whole_rows, False)
    slope_plus = slope_of(plus, 0)
    slope_minus = slope_of(minus, band)
    right = slope_of(sum_part + gap_part, 2 * band)
    left = slope_of(sum_part - gap_part, 4 * band)
    fourth = resample(slope_of(fourth, 6 * band), whole_rows, True)
    sum_part = resample(right + left, sums, True)
    gap_part = resample(right - left, gaps, True)
    slope_plus = 2.0 * (slope_plus + (sum_part + gap_part) + fourth[:, :band])
    slope_minus = 2.0 * (slope_minus + (sum_part - gap_part) + fourth[:, band:])

    for place in range(count):
        (p_re, p_im, m_re, m_im), here, there = fields(place)
        scale = weight[0, place]
        plus = scale * slope_plus
        minus = scale * slope_minus
        p_re, p_im, m_re, m_im = plus * p_re, plus * p_im, minus * m_re, minus * m_im
        for rows, columns, value in (
            (here, slice(0, band), p_re + m_re),
            (here, slice(band, 2 * band), p_im - m_im),
            (there, slice(0, band), p_im + m_im),
            (there, slice(band, 2 * band), m_re - p_re),
        ):
            hi, lo = split(value)
            deep_hi[rows, columns] = hi
            deep_lo[rows, columns] = lo
    back[...] = dot_split((deep_hi[...], deep_lo[...]), (x_wave[0], x_wave[1]), 1, 1)

    copy_y_cols.wait()
    copy_both_t.wait()
    for place in range(count):
        here = pl.ds(place * rows_here, rows_here)
        there = pl.ds(total_rows + place * rows_here, rows_here)
        hi, lo = split(jnp.concatenate([back[here, :], back[there, :]], axis=0))
        grad = dot(y_cols[...], jnp.concatenate([hi, lo, hi], axis=0))
        for start in range(0, band, part):
            here = pl.ds(start, part)
            k_re = kern[place, 0, here, :]
            k_im = kern[place, 1, here, :]
            g_re = grad[start : start + part]
            g_im = grad[band + start : band + start + part]
            if place == 0:
                gs[0, here, :] = k_re * g_re + k_im * g_im
                gs[1, here, :] = k_re * g_im - k_im * g_re
            else:
                gs[0, here, :] += k_re * g_re + k_im * g_im
                gs[1, here, :] += k_re * g_im - k_im * g_re
    g_re = gs[0]
    g_im = gs[1]
    edge_u = g_im[0:1, half : half + 1]
    edge_v = g_im[half : half + 1, 0:1]
    re_hi, re_lo = split(g_re)
    im_hi, im_lo = split(g_im)
    even, odd = both_t[:, :band], both_t[:, band:]
    left = dot(even, re_hi) + dot(even, re_lo) + dot(odd, im_hi) + dot(odd, im_lo)
    right = dot(even, im_hi) + dot(even, im_lo) - dot(odd, re_hi) - dot(odd, re_lo)
    l_hi, l_lo = split(left)
    r_hi, r_lo = split(right)
    even, odd = both[:band, :], both[band:, :]
    folded = dot(l_hi, even) + dot(l_lo, even) + dot(r_hi, odd) + dot(r_lo, odd)
    store_pieces(out, put(put(folded, half - 1, 1, edge_u), 1, half - 1, edge_v))


def spread_kernel(
    packed_hbm,
    rows_hbm,
    table_hbm,
    cols_hbm,
    slope_hbm,
    out_hbm,
    packed,
    rows,
    table,
    cols,
    slope,
    out,
    sems,
    in_sems,
    out_sems,
    *,
    width,
):
    band = rows.shape[2]
    half = band // 2
    steps, count, step = out.shape

    def copy_in(place):
        here = pl.ds(place * step, step)
        return (
            pltpu.make_async_copy(cols_hbm.at[:, here, :], cols.at[place], in_sems.at[2 * place]),
            pltpu.make_async_copy(slope_hbm.at[:, here], slope.at[place], in_sems.at[2 * place + 1]),
        )

    def copy_out(place):
        here = pl.ds(place * step, step)
        return pltpu.make_async_copy(out.at[place], out_hbm.at[:, here], out_sems.at[place])

    pairs = ((packed_hbm, packed), (rows_hbm, rows), (table_hbm, table))
    early = [pltpu.make_async_copy(*pair, sems.at[place]) for place, pair in enumerate(pairs)]
    for copy in early:
        copy.start()
    for copy in copy_in(0):
        copy.start()
    for copy in early:
        copy.wait()
    for place in range(1, steps):
        for copy in copy_in(place):
            copy.start()
    box = load_pieces(packed, band) * (1.0 / width)
    edge_u = box[half - 1 : half, 1:2]
    edge_v = box[1:2, half - 1 : half]
    box = put(put(box, half - 1, 1, 0.0), 1, half - 1, 0.0)
    mixed_hi, mixed_lo = split(dot_split((rows[0], rows[1]), split(box)))
    mixed = jnp.concatenate([mixed_hi, mixed_lo], axis=0)
    edge_row, edge_col = edges(table)
    side = edge_u * edge_col + edge_v * edge_row
    for place in range(steps):
        for copy in copy_in(place):
            copy.wait()
        main = dot(mixed, cols[place, 0], 1, 1)
        rest = dot(mixed_hi, cols[place, 1], 1, 1)
        grad = main[:count] + (main[count:] + rest)
        for inner in range(0, step, LANES):
            there = pl.ds(inner, LANES)
            out[place, :, there] = (grad[:, inner : inner + LANES] + side) * slope[place, :, there]
        copy_out(place).start()
    for place in range(steps):
        copy_out(place).wait()


def params(mebibytes):
    return pltpu.CompilerParams(vmem_limit_bytes=mebibytes * 1024 * 1024)


vmem = pl.BlockSpec(memory_space=pltpu.VMEM)
anywhere = pl.BlockSpec(memory_space=pl.ANY)


def call_mask(mask_level, table, pieces):
    rows_here, width = mask_level.shape
    band = table.shape[1]
    chunk = min(512, width // 4)
    steps = width // chunk
    return pl.pallas_call(
        mask_kernel,
        out_shape=jax.ShapeDtypeStruct(pieces, f32),
        in_specs=[anywhere, anywhere],
        out_specs=vmem,
        scratch_shapes=[
            pltpu.VMEM((steps, rows_here, chunk), f32),
            pltpu.VMEM(table.shape, f32),
            pltpu.VMEM((2 * rows_here, band), f32),
            pltpu.VMEM((2 * rows_here, band), f32),
            pltpu.SemaphoreType.DMA((steps + 1,)),
        ],
        compiler_params=params(ROOM),
        name="mask_rows",
    )(mask_level, table)


def call_prepare(shape_corner, shape_extent, after, mask_level, table, band, pencils, conds):
    rows_here, width = mask_level.shape
    image_rows = IMAGE // pencils
    cols_here = width // conds
    y_big = np.stack(wave(image_rows * np.arange(pencils), band, IMAGE)).astype(np.float32)
    y_fine = np.stack(wave(np.arange(image_rows), band, IMAGE)).astype(np.float32)
    shapes = [
        ((image_rows, IMAGE), f32),
        ((4 * image_rows, 2 * band), bf16),
        ((2 * band, 6 * image_rows), bf16),
        ((2, rows_here, band), bf16),
        ((2, cols_here, band), bf16),
        ((rows_here, cols_here), f32),
    ]
    return pl.pallas_call(
        prepare_kernel,
        out_shape=[jax.ShapeDtypeStruct(*shape) for shape in shapes],
        in_specs=[vmem] * 5 + [anywhere] * 2,
        out_specs=[vmem] * len(shapes),
        scratch_shapes=[pltpu.SemaphoreType.DMA],
        compiler_params=params(ROOM),
        cost_estimate=pl.CostEstimate(flops=10**9, bytes_accessed=2 * 10**7, transcendentals=10**6),
        name="prepare",
    )(shape_corner.T, shape_extent.T, y_big, y_fine, table, after, mask_level)


def call_field(
    band_cutoff, kernel_weight, dose_scale, packed, socs_kernels, target, y_rows, y_cols, width
):
    _, count, _, band, _ = socs_kernels.shape
    image_rows = target.shape[0]
    both = fold_table(band)
    x_cos, x_sin = wave(2 * np.arange(band) + 1, band, 4 * band)
    x_wave = np.stack(halves(np.concatenate([x_cos.T, x_sin.T], axis=1)))
    up = np.stack(halves(resample_table(band, IMAGE)))
    deep = 2 * count * image_rows
    return pl.pallas_call(
        functools.partial(field_kernel, width=width),
        out_shape=jax.ShapeDtypeStruct(packed.shape, f32),
        in_specs=[anywhere] * 12,
        out_specs=vmem,
        scratch_shapes=[
            pltpu.SMEM(band_cutoff.shape, jnp.int32),
            pltpu.SMEM(kernel_weight.shape, f32),
            pltpu.SMEM(dose_scale.shape, f32),
            pltpu.VMEM(packed.shape, f32),
            pltpu.VMEM(both.shape, bf16),
            pltpu.VMEM(y_rows.shape, bf16),
            pltpu.VMEM((count, 2, band, band), f32),
            pltpu.VMEM(x_wave.shape, bf16),
            pltpu.VMEM(up.shape, bf16),
            pltpu.VMEM(target.shape, f32),
            pltpu.VMEM(y_cols.shape, bf16),
            pltpu.VMEM(both.T.shape, bf16),
            pltpu.VMEM((2, band, band), f32),
            pltpu.VMEM((band, band), jnp.int32),
            pltpu.VMEM((SLOTS, 2 * band, band), bf16),
            pltpu.VMEM((SLOTS, 2 * band, band), bf16),
            pltpu.VMEM((deep, band), bf16),
            pltpu.VMEM((deep, band), bf16),
            pltpu.VMEM((deep, 2 * band), bf16),
            pltpu.VMEM((deep, 2 * band), bf16),
            pltpu.VMEM((deep, 2 * band), f32),
            pltpu.VMEM((deep, band), f32),
            pltpu.VMEM((2, band, band), f32),
            pltpu.SemaphoreType.DMA((11,)),
            pltpu.SemaphoreType.DMA((count,)),
        ],
        compiler_params=params(ROOM),
        name="image_rows",
    )(
        band_cutoff,
        kernel_weight,
        dose_scale,
        packed,
        both.astype(bf16),
        y_rows,
        socs_kernels,
        x_wave,
        up,
        target,
        y_cols,
        both.T.astype(bf16),
    )


def call_spread(folded, slope, rows, cols, table, width):
    count, cols_here = slope.shape
    band = rows.shape[2]
    step = min(512, cols_here)
    steps = cols_here // step
    return pl.pallas_call(
        functools.partial(spread_kernel, width=width),
        out_shape=jax.ShapeDtypeStruct(slope.shape, f32),
        in_specs=[anywhere] * 5,
        out_specs=anywhere,
        scratch_shapes=[
            pltpu.VMEM(folded.shape, f32),
            pltpu.VMEM(rows.shape, bf16),
            pltpu.VMEM(table.shape, f32),
            pltpu.VMEM((steps, 2, step, band), bf16),
            pltpu.VMEM((steps, count, step), f32),
            pltpu.VMEM((steps, count, step), f32),
            pltpu.SemaphoreType.DMA((3,)),
            pltpu.SemaphoreType.DMA((2 * steps,)),
            pltpu.SemaphoreType.DMA((steps,)),
        ],
        compiler_params=params(ROOM),
        name="mask_gradient",
    )(folded, rows, table, cols, slope)


def local(
    mask_level, socs_kernels, band_cutoff, kernel_weight, dose_scale, shape_corner, shape_extent
):
    width = mask_level.shape[1]
    band = socs_kernels.shape[3]
    pencils = lax.axis_size("px")
    conds = lax.axis_size("cond")
    pieces = (pencils, band * band // LANES // pencils, LANES)
    table = basis_tables(band, width)

    packed = call_mask(mask_level, table, pieces)
    piece = collect(packed)
    target, y_rows, y_cols, rows, cols, slope = call_prepare(
        shape_corner, shape_extent, piece, mask_level, table, band, pencils, conds
    )
    packed = hand_out(piece, pieces)
    folded = call_field(
        band_cutoff, kernel_weight, dose_scale, packed, socs_kernels, target, y_rows, y_cols, width
    )
    piece = collect(folded)
    others = [
        lax.ppermute(piece, "cond", [(i, (i + d) % conds) for i in range(conds)])
        for d in range(1, conds)
    ]
    piece = functools.reduce(jnp.add, others, piece)
    folded = hand_out(piece, pieces)
    return call_spread(folded, slope, rows, cols, table, width)


def collect(packed):
    arrived = lax.all_to_all(packed, "px", split_axis=0, concat_axis=0, tiled=True)
    return jnp.sum(arrived, axis=0)


def hand_out(piece, pieces):
    outgoing = jnp.broadcast_to(piece[None], pieces)
    return lax.all_to_all(outgoing, "px", split_axis=0, concat_axis=0, tiled=True)


def solution(mesh):
    in_specs = (
        P("px", None),
        P("cond", None, None, None, None),
        P("cond", None),
        P("cond", None),
        P("cond"),
        P(),
        P(),
    )
    out_specs = P("px", "cond")
    return jax.shard_map(local, mesh=mesh, in_specs=in_specs, out_specs=out_specs, check_vma=False)
```

time: 131 us -> 103 us (0.79)
  local copies, waits for them, and re-layouts: 34.4 us -> 1.45 us
  Pallas kernels: 23.4 us -> 28.9 us
  waiting for transfers between devices: 3.11 us -> 7.73 us
  blocking collectives: 53.8 us -> 50.1 us
    unnamed x74 -> x4, local copies, waits for them, and re-layouts: 33.6 us -> 0.71 us
    all_to_all x1, waiting for transfers between devices: 0.01 us -> 4.61 us  [hand_out(): lax.all_to_all(outgoing, 'px', split_axis=0, concat_axis=0, tiled=True)]
    all_to_all x2, blocking collectives: 38.6 us -> 34.5 us  [collect(): lax.all_to_all(packed, 'px', split_axis=0, concat_axis=0, tiled=True)]
    pallas_call x1, Pallas kernels: 10.7 us -> 13.6 us  [call_field(): pl.pallas_call(functools.partial(field_kernel, width=width), out_shape=ja...]
    pallas_call x1, Pallas kernels: 1.88 us -> 4.53 us  [call_spread(): pl.pallas_call(functools.partial(spread_kernel, width=width), out_shape=j...]
    pallas_call x1, Pallas kernels: 7.77 us -> 6.22 us  [call_mask(): pl.pallas_call(mask_kernel, out_shape=jax.ShapeDtypeStruct(pieces, f32),...]
    pallas_call x1, Pallas kernels: 3.03 us -> 4.57 us  [call_prepare(): pl.pallas_call(prepare_kernel, out_shape=[jax.ShapeDtypeStruct(*shape) fo...]
  transfers between devices with their start and end apart: 4 -> 4, of which waited for: 1 -> 2; matrix products, arithmetic and copies ran while one was open for 1% -> 0% of each run, Pallas kernels for 2% -> 4%
where the time goes in v2:
time: 103 us; the launch traced here: 102 us
  blocking collectives  50.1 us (49%)
  Pallas kernels  28.9 us (28%)
  starting transfers between devices  12.9 us (13%)
  waiting for transfers between devices  7.73 us (8%)
  local copies, waits for them, and re-layouts  1.45 us (1%)
    all_to_all x2, blocking collectives, collect(): lax.all_to_all(packed, 'px', split_axis=0, concat_axis=0, tiled=True)  34.5 us
    all_to_all x1, blocking collectives, hand_out(): lax.all_to_all(outgoing, 'px', split_axis=0, concat_axis=0, tiled=True)  15.6 us
    pallas_call x1, Pallas kernels, call_field(): pl.pallas_call(functools.partial(field_kernel, width=width), out_shape=ja...  13.6 us
    ppermute x3, starting transfers between devices, local(): lax.ppermute(piece, 'cond', [(i, (i + d) % conds) for i in range(conds)])  8.45 us
    pallas_call x1, Pallas kernels, call_mask(): pl.pallas_call(mask_kernel, out_shape=jax.ShapeDtypeStruct(pieces, f32),...  6.22 us
    all_to_all x1, waiting for transfers between devices, hand_out(): lax.all_to_all(outgoing, 'px', split_axis=0, concat_axis=0, tiled=True)  4.61 us
    pallas_call x1, Pallas kernels, call_prepare(): pl.pallas_call(prepare_kernel, out_shape=[jax.ShapeDtypeStruct(*shape) fo...  4.57 us
    pallas_call x1, Pallas kernels, call_spread(): pl.pallas_call(functools.partial(spread_kernel, width=width), out_shape=j...  4.53 us
  transfers between devices with their start and end apart: 4, of which 2 were waited for; matrix products, arithmetic and copies ran while one was open for 0% of the time, Pallas kernels for 4%

profile of v2, /device:TPU:1, one launch (start us, length us, event | category | flops | bytes accessed | tf_op | source)
XLA Modules:
  0.0 102.1 jit_solution(14711395150586183810)
XLA Ops:
  0.0 6.2 %mask_rows.1 = f32[64,8,128]{2,1,0:T(8,128)} custom-call(f32[128,8192]{1,0:T(8,128)} %mask_hbm.3, f32[392,256]{1,0:T(8,128)} %constant.16.clone.table_hbm.table), custom_call_target="tpu_custom_call" | custom-call | tf_op jit(solution)/shard_map/mask_rows/pallas_call | solution.py:579
  6.2 20.1 %all_to_all.20 = f32[64,8,128]{2,1,0:T(8,128)S(1)} all-to-all(f32[64,8,128]{2,1,0:T(8,128)} %mask_rows.1), channel_id=1, replica_groups=mesh['cond'=4,'px'=64] {'px'}, dimensions={0} | all-to-all | bytes 524288 | tf_op jit(solution)/shard_map/all_to_all | solution.py:738
  26.3 0.1 reduce_sum.18.after
  26.4 0.0 copy-start.1
  26.4 0.7 broadcast_in_dim.4
  27.1 4.5 %all-to-all-start.1 = ((f32[64,8,128]{2,1,0:T(8,128)}), f32[64,8,128]{2,1,0:T(8,128)S(1)}, u32[]{:S(2)}, u32[]{:S(2)}) async-start(f32[64,8,128]{2,1,0:T(8,128)} %broadcast_in_dim.4), calls=%async_computation.1 | async-start | bytes 524288 | tf_op jit(solution)/shard_map/all_to_all | solution.py:744
  32.2 0.0 copy-done.1
  32.3 4.6 %prepare.1 = (f32[32,2048]{1,0:T(8,128)}, bf16[128,512]{1,0:T(8,128)(2,1)}, bf16[512,192]{1,0:T(8,128)(2,1)}, bf16[2,128,256]{2,1,0:T(8,128)(2,1)}, bf16[2,2048,256]{2,1,0:T(8,128)(2,1)}, /*index=5*/f32[128,2048]{1,0:T(8,128)}) custom-call(s32[2,256]{1,0:T(2,128)} %bitcast.2, s32[2,256]{1,0:T(2,128)} %bitcast.3, f32[2,64,256]{2,1,0:T(8,128)} %constant.17.clone.y_big, ...), custom_call_target="tpu_custom_call" | custom-call | flops 1000000000 | bytes 20000000 | tf_op jit(solution)/shard_map/prepare/pallas_call | solution.py:610
  36.8 4.6 %all-to-all-done.1.packed_hbm = f32[64,8,128]{2,1,0:T(8,128)S(1)} async-done(((f32[64,8,128]{2,1,0:T(8,128)}), f32[64,8,128]{2,1,0:T(8,128)S(1)}, u32[]{:S(2)}, u32[]{:S(2)}) %all-to-all-start.1) | async-done | bytes 262176 | tf_op jit(solution)/shard_map/all_to_all | solution.py:744
  41.4 0.0 copy-start
  41.4 0.7 copy-done
  42.1 13.6 %image_rows.1 = f32[64,8,128]{2,1,0:T(8,128)} custom-call(s32[1,12]{1,0:T(1,128)} %cutoff_hbm.1, f32[1,12]{1,0:T(1,128)} %weight_hbm.1, f32[1]{0:T(128)S(6)} %copy.15.dose_hbm, f32[64,8,128]{2,1,0:T(8,128)} %copy-done, bf16[512,256]{1,0:T(8,128)(2,1)} %constant.19.clone.both_hbm, bf16[128,512]{1,0:T(8,128)(2,1)} %get-tuple-element.11.y_rows_hbm, ...), custom_call_target="tpu_custom_call" | custom-call | tf_op jit(solution)/shard_map/image_rows/pallas_call | solution.py:632
  55.8 14.4 %all_to_all.21 = f32[64,8,128]{2,1,0:T(8,128)S(1)} all-to-all(f32[64,8,128]{2,1,0:T(8,128)} %image_rows.1), channel_id=1, replica_groups=mesh['cond'=4,'px'=64] {'px'}, dimensions={0} | all-to-all | bytes 524288 | tf_op jit(solution)/shard_map/all_to_all | solution.py:738
  70.2 0.1 reduce_sum.19
  70.2 5.2 %collective-permute-start.2 = (f32[8,128]{1,0:T(8,128)S(1)}, f32[8,128]{1,0:T(8,128)S(1)}, u32[]{:S(2)}, u32[]{:S(2)}) collective-permute-start(f32[8,128]{1,0:T(8,128)S(1)} %reduce_sum.19), channel_id=1, source_target_pairs={{0,192},{64,0},{128,64},{192,128},{1,193},{65,1},{129,65},{193,129... | collective-permute-start | bytes 12296 | tf_op jit(solution)/shard_map/ppermute | solution.py:729
  75.4 1.1 %collective-permute-start.1 = (f32[8,128]{1,0:T(8,128)S(1)}, f32[8,128]{1,0:T(8,128)S(1)}, u32[]{:S(2)}, u32[]{:S(2)}) collective-permute-start(f32[8,128]{1,0:T(8,128)S(1)} %reduce_sum.19), channel_id=1, source_target_pairs={{0,128},{64,192},{128,0},{192,64},{1,129},{65,193},{129,1},{193,65... | collective-permute-start | bytes 12296 | tf_op jit(solution)/shard_map/ppermute | solution.py:729
  76.6 2.1 %collective-permute-start = (f32[8,128]{1,0:T(8,128)S(1)}, f32[8,128]{1,0:T(8,128)S(1)}, u32[]{:S(2)}, u32[]{:S(2)}) collective-permute-start(f32[8,128]{1,0:T(8,128)S(1)} %reduce_sum.19), channel_id=1, source_target_pairs={{0,64},{64,128},{128,192},{192,0},{1,65},{65,129},{129,193},{193,1... | collective-permute-start | bytes 12296 | tf_op jit(solution)/shard_map/ppermute | solution.py:729
  78.7 0.0 collective-permute-done.2
  78.7 3.1 %collective-permute-done.1 = f32[8,128]{1,0:T(8,128)S(1)} collective-permute-done((f32[8,128]{1,0:T(8,128)S(1)}, f32[8,128]{1,0:T(8,128)S(1)}, u32[]{:S(2)}, u32[]{:S(2)}) %collective-permute-start.1) | collective-permute-done | bytes 4128 | tf_op jit(solution)/shard_map/ppermute | solution.py:729
  81.8 0.0 collective-permute-done
  81.8 15.6 %all_to_all.22.packed_hbm = f32[64,8,128]{2,1,0:T(8,128)} all-to-all(f32[64,8,128]{2,1,0:T(8,128)S(1)} %broadcast_in_dim.5), channel_id=1, replica_groups=mesh['cond'=4,'px'=64] {'px'}, dimensions={0} | all-to-all | bytes 524288 | tf_op jit(solution)/shard_map/all_to_all | solution.py:744
  97.4 4.5 %mask_gradient.1 = f32[128,2048]{1,0:T(8,128)} custom-call(f32[64,8,128]{2,1,0:T(8,128)} %all_to_all.22.packed_hbm, bf16[2,128,256]{2,1,0:T(8,128)(2,1)} %get-tuple-element.14.rows_hbm, f32[392,256]{1,0:T(8,128)} %constant.16.clone.table_hbm.table, bf16[2,2048,256]{2,1,0:T(8,128)(2,1)} %get-tuple-element.15.cols_hbm, f32[128,2048]{1,0:T(8,128)} %get-tuple-element.16.slope_hbm), custom_call_target="tpu_custom_call" | custom-call | tf_op jit(solution)/shard_map/mask_gradient/pallas_call | solution.py:687
  (2 shorter events, 0.0 us)
Async XLA Ops:
  26.4 5.9 %copy-start.1 = (f32[8,128]{1,0:T(8,128)}, f32[8,128]{1,0:T(8,128)S(1)}, u32[]{:S(2)}) copy-start(f32[8,128]{1,0:T(8,128)S(1)} %reduce_sum.18.after) | copy-start | bytes 12292
  27.1 14.3 %all-to-all-start.1 = ((f32[64,8,128]{2,1,0:T(8,128)}), f32[64,8,128]{2,1,0:T(8,128)S(1)}, u32[]{:S(2)}, u32[]{:S(2)}) async-start(f32[64,8,128]{2,1,0:T(8,128)} %broadcast_in_dim.4), calls=%async_computation.1 | async-start | bytes 524288 | tf_op jit(solution)/shard_map/all_to_all | solution.py:744
  41.4 0.7 copy-start
  70.2 8.5 %collective-permute-start.2 = (f32[8,128]{1,0:T(8,128)S(1)}, f32[8,128]{1,0:T(8,128)S(1)}, u32[]{:S(2)}, u32[]{:S(2)}) collective-permute-start(f32[8,128]{1,0:T(8,128)S(1)} %reduce_sum.19), channel_id=1, source_target_pairs={{0,192},{64,0},{128,64},{192,128},{1,193},{65,1},{129,65},{193,129... | collective-permute-start | bytes 12296 | tf_op jit(solution)/shard_map/ppermute | solution.py:729
  75.4 6.4 %collective-permute-start.1 = (f32[8,128]{1,0:T(8,128)S(1)}, f32[8,128]{1,0:T(8,128)S(1)}, u32[]{:S(2)}, u32[]{:S(2)}) collective-permute-start(f32[8,128]{1,0:T(8,128)S(1)} %reduce_sum.19), channel_id=1, source_target_pairs={{0,128},{64,192},{128,0},{192,64},{1,129},{65,193},{129,1},{193,65... | collective-permute-start | bytes 12296 | tf_op jit(solution)/shard_map/ppermute | solution.py:729
  76.6 5.2 %collective-permute-start = (f32[8,128]{1,0:T(8,128)S(1)}, f32[8,128]{1,0:T(8,128)S(1)}, u32[]{:S(2)}, u32[]{:S(2)}) collective-permute-start(f32[8,128]{1,0:T(8,128)S(1)} %reduce_sum.19), channel_id=1, source_target_pairs={{0,64},{64,128},{128,192},{192,0},{1,65},{65,129},{129,193},{193,1... | collective-permute-start | bytes 12296 | tf_op jit(solution)/shard_map/ppermute | solution.py:729

commit v3 on v2

--- a/solution.py
+++ b/solution.py
@@ -160,15 +160,13 @@
     copy(order[0]).start()
     copy(order[1]).start()
     copy_table.start()
-    for place in order[2:AHEAD]:
+    for place in order[2:]:
         copy(place).start()
     copy_table.wait()
     line = jnp.zeros((1, LANES), f32)
     for place in range(pairs):
         copy(place).wait()
         copy(place + pairs).wait()
-        for ahead in order[2 * place + AHEAD : 2 * place + AHEAD + 2]:
-            copy(ahead).start()
         near = jnp.tanh(mask[place])
         far = jnp.tanh(mask[place + pairs])
         hi, lo = split(basis_rows(table, place * blocks, blocks))
@@ -204,21 +202,17 @@
     extent,
     y_big,
     y_fine,
-    table,
     after,
     mask_hbm,
     target,
     y_rows,
     y_cols,
-    rows,
-    cols,
     slope,
     sem,
 ):
-    band = table.shape[1]
+    band = y_fine.shape[2]
     rows_here, image = target.shape
     cols_here = slope.shape[1]
-    blocks = cols_here // LANES
     place_px = lax.axis_index("px")
     place_cond = lax.axis_index("cond")
     mine = pl.ds(pl.multiple_of(place_cond * cols_here, cols_here), cols_here)
@@ -254,14 +248,6 @@
     stacked = jnp.concatenate([waves_hi, waves_hi, waves_lo], axis=0)
     y_cols[...] = jnp.transpose(stacked).astype(bf16)
 
-    hi, lo = split(basis_rows(table, place_px, 1))
-    rows[0] = hi
-    rows[1] = lo
-    for block in range(blocks):
-        here = pl.ds(block * LANES, LANES)
-        hi, lo = split(basis_rows(table, place_cond * blocks + block, 1))
-        cols[0, here, :] = hi
-        cols[1, here, :] = lo
     copy_mask.wait()
     for start in range(0, cols_here, LANES):
         here = pl.ds(start, LANES)
@@ -496,62 +482,39 @@
     store_pieces(out, put(put(folded, half - 1, 1, edge_u), 1, half - 1, edge_v))
 
 
-def spread_kernel(
-    packed_hbm,
-    rows_hbm,
-    table_hbm,
-    cols_hbm,
-    slope_hbm,
-    out_hbm,
-    packed,
-    rows,
-    table,
-    cols,
-    slope,
-    out,
-    sems,
-    in_sems,
-    out_sems,
-    *,
-    width,
-):
-    band = rows.shape[2]
+def spread_kernel(packed, table, slope_hbm, out_hbm, slope, out, cols, in_sems, out_sems):
+    steps, count, step = out.shape
+    band = table.shape[1]
     half = band // 2
-    steps, count, step = out.shape
+    blocks = step // LANES
+    width = (table.shape[0] - 2 * LANES - 8) // 2 * LANES
+    first_block = lax.axis_index("cond") * (steps * blocks)
 
     def copy_in(place):
         here = pl.ds(place * step, step)
-        return (
-            pltpu.make_async_copy(cols_hbm.at[:, here, :], cols.at[place], in_sems.at[2 * place]),
-            pltpu.make_async_copy(slope_hbm.at[:, here], slope.at[place], in_sems.at[2 * place + 1]),
-        )
+        return pltpu.make_async_copy(slope_hbm.at[:, here], slope.at[place], in_sems.at[place])
 
     def copy_out(place):
         here = pl.ds(place * step, step)
         return pltpu.make_async_copy(out.at[place], out_hbm.at[:, here], out_sems.at[place])
 
-    pairs = ((packed_hbm, packed), (rows_hbm, rows), (table_hbm, table))
-    early = [pltpu.make_async_copy(*pair, sems.at[place]) for place, pair in enumerate(pairs)]
-    for copy in early:
-        copy.start()
-    for copy in copy_in(0):
-        copy.start()
-    for copy in early:
-        copy.wait()
-    for place in range(1, steps):
-        for copy in copy_in(place):
-            copy.start()
+    for place in range(steps):
+        copy_in(place).start()
+    row_hi, row_lo = split(basis_rows(table, lax.axis_index("px"), 1))
+    for place in range(steps):
+        hi, lo = split(basis_rows(table, first_block + place * blocks, blocks))
+        cols[place, 0] = hi
+        cols[place, 1] = lo
     box = load_pieces(packed, band) * (1.0 / width)
     edge_u = box[half - 1 : half, 1:2]
     edge_v = box[1:2, half - 1 : half]
     box = put(put(box, half - 1, 1, 0.0), 1, half - 1, 0.0)
-    mixed_hi, mixed_lo = split(dot_split((rows[0], rows[1]), split(box)))
+    mixed_hi, mixed_lo = split(dot_split((row_hi, row_lo), split(box)))
     mixed = jnp.concatenate([mixed_hi, mixed_lo], axis=0)
     edge_row, edge_col = edges(table)
     side = edge_u * edge_col + edge_v * edge_row
     for place in range(steps):
-        for copy in copy_in(place):
-            copy.wait()
+        copy_in(place).wait()
         main = dot(mixed, cols[place, 0], 1, 1)
         rest = dot(mixed_hi, cols[place, 1], 1, 1)
         grad = main[:count] + (main[count:] + rest)
@@ -593,7 +556,7 @@
     )(mask_level, table)
 
 
-def call_prepare(shape_corner, shape_extent, after, mask_level, table, band, pencils, conds):
+def call_prepare(shape_corner, shape_extent, after, mask_level, band, pencils, conds):
     rows_here, width = mask_level.shape
     image_rows = IMAGE // pencils
     cols_here = width // conds
@@ -603,20 +566,18 @@
         ((image_rows, IMAGE), f32),
         ((4 * image_rows, 2 * band), bf16),
         ((2 * band, 6 * image_rows), bf16),
-        ((2, rows_here, band), bf16),
-        ((2, cols_here, band), bf16),
         ((rows_here, cols_here), f32),
     ]
     return pl.pallas_call(
         prepare_kernel,
         out_shape=[jax.ShapeDtypeStruct(*shape) for shape in shapes],
-        in_specs=[vmem] * 5 + [anywhere] * 2,
+        in_specs=[vmem] * 4 + [anywhere] * 2,
         out_specs=[vmem] * len(shapes),
         scratch_shapes=[pltpu.SemaphoreType.DMA],
         compiler_params=params(ROOM),
         cost_estimate=pl.CostEstimate(flops=10**9, bytes_accessed=2 * 10**7, transcendentals=10**6),
         name="prepare",
-    )(shape_corner.T, shape_extent.T, y_big, y_fine, table, after, mask_level)
+    )(shape_corner.T, shape_extent.T, y_big, y_fine, after, mask_level)
 
 
 def call_field(
@@ -679,30 +640,26 @@
     )
 
 
-def call_spread(folded, slope, rows, cols, table, width):
+def call_spread(folded, slope, table):
     count, cols_here = slope.shape
-    band = rows.shape[2]
+    band = table.shape[1]
     step = min(512, cols_here)
     steps = cols_here // step
     return pl.pallas_call(
-        functools.partial(spread_kernel, width=width),
+        spread_kernel,
         out_shape=jax.ShapeDtypeStruct(slope.shape, f32),
-        in_specs=[anywhere] * 5,
+        in_specs=[vmem, vmem, anywhere],
         out_specs=anywhere,
         scratch_shapes=[
-            pltpu.VMEM(folded.shape, f32),
-            pltpu.VMEM(rows.shape, bf16),
-            pltpu.VMEM(table.shape, f32),
-            pltpu.VMEM((steps, 2, step, band), bf16),
             pltpu.VMEM((steps, count, step), f32),
             pltpu.VMEM((steps, count, step), f32),
-            pltpu.SemaphoreType.DMA((3,)),
-            pltpu.SemaphoreType.DMA((2 * steps,)),
+            pltpu.VMEM((steps, 2, step, band), bf16),
+            pltpu.SemaphoreType.DMA((steps,)),
             pltpu.SemaphoreType.DMA((steps,)),
         ],
-        compiler_params=params(ROOM),
+        compiler_params=params(40),
         name="mask_gradient",
-    )(folded, rows, table, cols, slope)
+    )(folded, table, slope)
 
 
 def local(
@@ -717,21 +674,19 @@
 
     packed = call_mask(mask_level, table, pieces)
     piece = collect(packed)
-    target, y_rows, y_cols, rows, cols, slope = call_prepare(
-        shape_corner, shape_extent, piece, mask_level, table, band, pencils, conds
+    target, y_rows, y_cols, slope = call_prepare(
+        shape_corner, shape_extent, piece, mask_level, band, pencils, conds
     )
     packed = hand_out(piece, pieces)
     folded = call_field(
         band_cutoff, kernel_weight, dose_scale, packed, socs_kernels, target, y_rows, y_cols, width
     )
     piece = collect(folded)
-    others = [
-        lax.ppermute(piece, "cond", [(i, (i + d) % conds) for i in range(conds)])
-        for d in range(1, conds)
-    ]
-    piece = functools.reduce(jnp.add, others, piece)
+    copies = jnp.broadcast_to(piece[None], (conds, *piece.shape))
+    copies = lax.all_to_all(copies, "cond", split_axis=0, concat_axis=0, tiled=True)
+    piece = jnp.sum(copies, axis=0)
     folded = hand_out(piece, pieces)
-    return call_spread(folded, slope, rows, cols, table, width)
+    return call_spread(folded, slope, table)
 
 
 def collect(packed):

time: 103 us -> 102 us (level)
  blocking collectives: 50.1 us -> 63.4 us
  starting transfers between devices: 12.9 us -> 4.47 us
  Pallas kernels: 28.9 us -> 25 us
  waiting for transfers between devices: 7.73 us -> 5.8 us
    all_to_all x0 -> x1, blocking collectives: none -> 13.7 us  [local(): lax.all_to_all(copies, 'cond', split_axis=0, concat_axis=0, tiled=True)]
    ppermute x3 -> x0, starting transfers between devices: 8.45 us -> none  [local(): lax.ppermute(piece, 'cond', [(i, (i + d) % conds) for i in range(conds)])]
    ppermute x3 -> x0, waiting for transfers between devices: 3.12 us -> none  [local(): lax.ppermute(piece, 'cond', [(i, (i + d) % conds) for i in range(conds)])]
    pallas_call x1, Pallas kernels: 6.22 us -> 4.6 us  [call_mask(): pl.pallas_call(mask_kernel, out_shape=jax.ShapeDtypeStruct(pieces, f32),...]
    pallas_call x1, Pallas kernels: 4.53 us -> 3.32 us  [call_spread(): pl.pallas_call(spread_kernel, out_shape=jax.ShapeDtypeStruct(slope.shape,...]
    all_to_all x1, waiting for transfers between devices: 4.61 us -> 5.8 us  [hand_out(): lax.all_to_all(outgoing, 'px', split_axis=0, concat_axis=0, tiled=True)]
    pallas_call x1, Pallas kernels: 4.57 us -> 3.37 us  [call_prepare(): pl.pallas_call(prepare_kernel, out_shape=[jax.ShapeDtypeStruct(*shape) fo...]
  transfers between devices with their start and end apart: 4 -> 1, of which waited for: 2 -> 1; matrix products, arithmetic and copies ran while one was open for 0% -> 0% of each run, Pallas kernels for 4% -> 3%
where the time goes in v3:
time: 102 us; the launch traced here: 101 us
  blocking collectives  63.4 us (62%)
  Pallas kernels  25 us (25%)
  waiting for transfers between devices  5.8 us (6%)
  starting transfers between devices  4.47 us (4%)
  local copies, waits for them, and re-layouts  1.46 us (1%)
    all_to_all x2, blocking collectives, collect(): lax.all_to_all(packed, 'px', split_axis=0, concat_axis=0, tiled=True)  34.5 us
    all_to_all x1, blocking collectives, hand_out(): lax.all_to_all(outgoing, 'px', split_axis=0, concat_axis=0, tiled=True)  15.2 us
    pallas_call x1, Pallas kernels, call_field(): pl.pallas_call(functools.partial(field_kernel, width=width), out_shape=ja...  13.7 us
    all_to_all x1, blocking collectives, local(): lax.all_to_all(copies, 'cond', split_axis=0, concat_axis=0, tiled=True)  13.7 us
    all_to_all x1, waiting for transfers between devices, hand_out(): lax.all_to_all(outgoing, 'px', split_axis=0, concat_axis=0, tiled=True)  5.8 us
    pallas_call x1, Pallas kernels, call_mask(): pl.pallas_call(mask_kernel, out_shape=jax.ShapeDtypeStruct(pieces, f32),...  4.6 us
    all_to_all x1, starting transfers between devices, hand_out(): lax.all_to_all(outgoing, 'px', split_axis=0, concat_axis=0, tiled=True)  4.47 us
    pallas_call x1, Pallas kernels, call_prepare(): pl.pallas_call(prepare_kernel, out_shape=[jax.ShapeDtypeStruct(*shape) fo...  3.37 us
  transfers between devices with their start and end apart: 1, of which 1 were waited for; matrix products, arithmetic and copies ran while one was open for 0% of the time, Pallas kernels for 3%

profile of v3, /device:TPU:1, one launch (start us, length us, event | category | flops | bytes accessed | tf_op | source)
XLA Modules:
  0.0 101.1 jit_solution(4975009732299138057)
XLA Ops:
  0.0 4.6 %mask_rows.1 = f32[64,8,128]{2,1,0:T(8,128)} custom-call(f32[128,8192]{1,0:T(8,128)} %mask_hbm.3, f32[392,256]{1,0:T(8,128)} %constant.16.clone.table_hbm.table), custom_call_target="tpu_custom_call" | custom-call | tf_op jit(solution)/shard_map/mask_rows/pallas_call | solution.py:542
  4.6 20.1 %all_to_all.25 = f32[64,8,128]{2,1,0:T(8,128)S(1)} all-to-all(f32[64,8,128]{2,1,0:T(8,128)} %mask_rows.1), channel_id=1, replica_groups=mesh['cond'=4,'px'=64] {'px'}, dimensions={0} | all-to-all | bytes 524288 | tf_op jit(solution)/shard_map/all_to_all | solution.py:693
  24.7 0.1 reduce_sum.27.after
  24.8 0.0 copy-start.3
  24.8 0.7 broadcast_in_dim.6
  25.5 4.5 %all-to-all-start.1 = ((f32[64,8,128]{2,1,0:T(8,128)}), f32[64,8,128]{2,1,0:T(8,128)S(1)}, u32[]{:S(2)}, u32[]{:S(2)}) async-start(f32[64,8,128]{2,1,0:T(8,128)} %broadcast_in_dim.6), calls=%async_computation.1 | async-start | bytes 524288 | tf_op jit(solution)/shard_map/all_to_all | solution.py:699
  30.6 0.0 copy-done.3
  30.6 3.4 %prepare.1 = (f32[32,2048]{1,0:T(8,128)}, bf16[128,512]{1,0:T(8,128)(2,1)}, bf16[512,192]{1,0:T(8,128)(2,1)}, f32[128,2048]{1,0:T(8,128)}) custom-call(s32[2,256]{1,0:T(2,128)} %bitcast.2, s32[2,256]{1,0:T(2,128)} %bitcast.3, f32[2,64,256]{2,1,0:T(8,128)} %constant.17.clone.y_big, f32[2,32,256]{2,1,0:T(8,128)} %constant.18.clone.y_fine, f32[8,128]{1,0:T(8,128)} %copy-done.3, ...), custom_call_target="tpu_custom_call" | custom-call | flops 1000000000 | bytes 20000000 | tf_op jit(solution)/shard_map/prepare/pallas_call | solution.py:571
  34.0 5.8 %all-to-all-done.1.packed_hbm = f32[64,8,128]{2,1,0:T(8,128)S(1)} async-done(((f32[64,8,128]{2,1,0:T(8,128)}), f32[64,8,128]{2,1,0:T(8,128)S(1)}, u32[]{:S(2)}, u32[]{:S(2)}) %all-to-all-start.1) | async-done | bytes 262176 | tf_op jit(solution)/shard_map/all_to_all | solution.py:699
  39.8 0.0 copy-start.2
  39.8 0.7 copy-done.2
  40.5 0.0 copy-start
  40.5 0.0 copy-start.1
  40.5 13.7 %image_rows.1 = f32[64,8,128]{2,1,0:T(8,128)} custom-call(s32[1,12]{1,0:T(1,128)} %cutoff_hbm.1, f32[1,12]{1,0:T(1,128)} %weight_hbm.1, f32[1]{0:T(128)S(6)} %copy.15.dose_hbm, f32[64,8,128]{2,1,0:T(8,128)} %copy-done.2, bf16[512,256]{1,0:T(8,128)(2,1)} %constant.19.clone.both_hbm, bf16[128,512]{1,0:T(8,128)(2,1)} %get-tuple-element.9.y_rows_hbm, ...), custom_call_target="tpu_custom_call" | custom-call | tf_op jit(solution)/shard_map/image_rows/pallas_call | solution.py:593
  54.3 14.4 %all_to_all.26 = f32[64,8,128]{2,1,0:T(8,128)S(1)} all-to-all(f32[64,8,128]{2,1,0:T(8,128)} %image_rows.1), channel_id=1, replica_groups=mesh['cond'=4,'px'=64] {'px'}, dimensions={0} | all-to-all | bytes 524288 | tf_op jit(solution)/shard_map/all_to_all | solution.py:693
  68.6 0.1 reduce_sum.28
  68.7 13.7 %all_to_all.27 = f32[4,8,128]{2,1,0:T(8,128)S(1)} all-to-all(f32[4,8,128]{2,1,0:T(8,128)S(1)} %broadcast_in_dim.7), channel_id=1, replica_groups=mesh['cond'=4,'px'=64] {'cond'}, dimensions={0} | all-to-all | bytes 32768 | tf_op jit(solution)/shard_map/all_to_all | solution.py:686
  82.5 15.2 %all_to_all.28.packed = f32[64,8,128]{2,1,0:T(8,128)S(1)} all-to-all(f32[64,8,128]{2,1,0:T(8,128)S(1)} %broadcast_in_dim.8), channel_id=1, replica_groups=mesh['cond'=4,'px'=64] {'px'}, dimensions={0} | all-to-all | bytes 524288 | tf_op jit(solution)/shard_map/all_to_all | solution.py:699
  97.7 0.0 copy-done
  97.7 0.0 copy-done.1
  97.7 3.3 %mask_gradient.1 = f32[128,2048]{1,0:T(8,128)} custom-call(f32[64,8,128]{2,1,0:T(8,128)S(1)} %all_to_all.28.packed, f32[392,256]{1,0:T(8,128)S(1)} %copy-done, f32[128,2048]{1,0:T(8,128)S(1)} %copy-done.1), custom_call_target="tpu_custom_call" | custom-call | tf_op jit(solution)/shard_map/mask_gradient/pallas_call | solution.py:648
  (3 shorter events, 0.0 us)
Async XLA Ops:
  24.8 5.9 %copy-start.3 = (f32[8,128]{1,0:T(8,128)}, f32[8,128]{1,0:T(8,128)S(1)}, u32[]{:S(2)}) copy-start(f32[8,128]{1,0:T(8,128)S(1)} %reduce_sum.27.after) | copy-start | bytes 12292
  25.5 14.3 %all-to-all-start.1 = ((f32[64,8,128]{2,1,0:T(8,128)}), f32[64,8,128]{2,1,0:T(8,128)S(1)}, u32[]{:S(2)}, u32[]{:S(2)}) async-start(f32[64,8,128]{2,1,0:T(8,128)} %broadcast_in_dim.6), calls=%async_computation.1 | async-start | bytes 524288 | tf_op jit(solution)/shard_map/all_to_all | solution.py:699
  39.8 0.7 copy-start.2
  40.5 57.2 %copy-start = (f32[392,256]{1,0:T(8,128)S(1)}, f32[392,256]{1,0:T(8,128)}, u32[]{:S(2)}) copy-start(f32[392,256]{1,0:T(8,128)} %constant.16.clone.table_hbm.table) | copy-start | bytes 1204228
  40.5 57.2 %copy-start.1 = (f32[128,2048]{1,0:T(8,128)S(1)}, f32[128,2048]{1,0:T(8,128)}, u32[]{:S(2)}) copy-start(f32[128,2048]{1,0:T(8,128)} %get-tuple-element.12.slope_hbm) | copy-start | bytes 3145732

commit v4 on v3

--- a/solution.py
+++ b/solution.py
@@ -682,9 +682,11 @@
         band_cutoff, kernel_weight, dose_scale, packed, socs_kernels, target, y_rows, y_cols, width
     )
     piece = collect(folded)
-    copies = jnp.broadcast_to(piece[None], (conds, *piece.shape))
-    copies = lax.all_to_all(copies, "cond", split_axis=0, concat_axis=0, tiled=True)
-    piece = jnp.sum(copies, axis=0)
+    others = [
+        lax.ppermute(piece, "cond", [(i, (i + d) % conds) for i in range(conds)])
+        for d in range(1, conds)
+    ]
+    piece = functools.reduce(jnp.add, others, piece)
     folded = hand_out(piece, pieces)
     return call_spread(folded, slope, table)
 

time: 102 us -> 99.6 us (0.976)
  blocking collectives: 63.4 us -> 49.9 us
  starting transfers between devices: 4.47 us -> 12.9 us
  waiting for transfers between devices: 5.8 us -> 8.9 us
    all_to_all x1 -> x0, blocking collectives: 13.7 us -> none  [local(): lax.all_to_all(copies, 'cond', split_axis=0, concat_axis=0, tiled=True)]
    ppermute x0 -> x3, starting transfers between devices: none -> 8.45 us  [local(): lax.ppermute(piece, 'cond', [(i, (i + d) % conds) for i in range(conds)])]
    ppermute x0 -> x3, waiting for transfers between devices: none -> 3.1 us  [local(): lax.ppermute(piece, 'cond', [(i, (i + d) % conds) for i in range(conds)])]
  transfers between devices with their start and end apart: 1 -> 4, of which waited for: 1 -> 2; matrix products, arithmetic and copies ran while one was open for 0% -> 0% of each run, Pallas kernels for 3% -> 3%
where the time goes in v4:
time: 99.6 us; the launch traced here: 99.2 us
  blocking collectives  49.9 us (50%)
  Pallas kernels  25 us (25%)
  starting transfers between devices  12.9 us (13%)
  waiting for transfers between devices  8.9 us (9%)
  local copies, waits for them, and re-layouts  1.43 us (1%)
    all_to_all x2, blocking collectives, collect(): lax.all_to_all(packed, 'px', split_axis=0, concat_axis=0, tiled=True)  34.5 us
    all_to_all x1, blocking collectives, hand_out(): lax.all_to_all(outgoing, 'px', split_axis=0, concat_axis=0, tiled=True)  15.4 us
    pallas_call x1, Pallas kernels, call_field(): pl.pallas_call(functools.partial(field_kernel, width=width), out_shape=ja...  13.8 us
    ppermute x3, starting transfers between devices, local(): lax.ppermute(piece, 'cond', [(i, (i + d) % conds) for i in range(conds)])  8.45 us
    all_to_all x1, waiting for transfers between devices, hand_out(): lax.all_to_all(outgoing, 'px', split_axis=0, concat_axis=0, tiled=True)  5.8 us
    pallas_call x1, Pallas kernels, call_mask(): pl.pallas_call(mask_kernel, out_shape=jax.ShapeDtypeStruct(pieces, f32),...  4.6 us
    all_to_all x1, starting transfers between devices, hand_out(): lax.all_to_all(outgoing, 'px', split_axis=0, concat_axis=0, tiled=True)  4.46 us
    pallas_call x1, Pallas kernels, call_prepare(): pl.pallas_call(prepare_kernel, out_shape=[jax.ShapeDtypeStruct(*shape) fo...  3.37 us
  transfers between devices with their start and end apart: 4, of which 2 were waited for; matrix products, arithmetic and copies ran while one was open for 0% of the time, Pallas kernels for 3%

profile of v4, /device:TPU:1, one launch (start us, length us, event | category | flops | bytes accessed | tf_op | source)
XLA Modules:
  0.0 99.2 jit_solution(10906257091187537326)
XLA Ops:
  0.0 4.6 %mask_rows.1 = f32[64,8,128]{2,1,0:T(8,128)} custom-call(f32[128,8192]{1,0:T(8,128)} %mask_hbm.3, f32[392,256]{1,0:T(8,128)} %constant.16.clone.table_hbm.table), custom_call_target="tpu_custom_call" | custom-call | tf_op jit(solution)/shard_map/mask_rows/pallas_call | solution.py:542
  4.6 20.1 %all_to_all.20 = f32[64,8,128]{2,1,0:T(8,128)S(1)} all-to-all(f32[64,8,128]{2,1,0:T(8,128)} %mask_rows.1), channel_id=1, replica_groups=mesh['cond'=4,'px'=64] {'px'}, dimensions={0} | all-to-all | bytes 524288 | tf_op jit(solution)/shard_map/all_to_all | solution.py:695
  24.7 0.1 reduce_sum.18.after
  24.8 0.0 copy-start.3
  24.8 0.7 broadcast_in_dim.4
  25.5 4.5 %all-to-all-start.1 = ((f32[64,8,128]{2,1,0:T(8,128)}), f32[64,8,128]{2,1,0:T(8,128)S(1)}, u32[]{:S(2)}, u32[]{:S(2)}) async-start(f32[64,8,128]{2,1,0:T(8,128)} %broadcast_in_dim.4), calls=%async_computation.1 | async-start | bytes 524288 | tf_op jit(solution)/shard_map/all_to_all | solution.py:701
  30.6 0.0 copy-done.3
  30.6 3.4 %prepare.1 = (f32[32,2048]{1,0:T(8,128)}, bf16[128,512]{1,0:T(8,128)(2,1)}, bf16[512,192]{1,0:T(8,128)(2,1)}, f32[128,2048]{1,0:T(8,128)}) custom-call(s32[2,256]{1,0:T(2,128)} %bitcast.2, s32[2,256]{1,0:T(2,128)} %bitcast.3, f32[2,64,256]{2,1,0:T(8,128)} %constant.17.clone.y_big, f32[2,32,256]{2,1,0:T(8,128)} %constant.18.clone.y_fine, f32[8,128]{1,0:T(8,128)} %copy-done.3, ...), custom_call_target="tpu_custom_call" | custom-call | flops 1000000000 | bytes 20000000 | tf_op jit(solution)/shard_map/prepare/pallas_call | solution.py:571
  34.0 5.8 %all-to-all-done.1.packed_hbm = f32[64,8,128]{2,1,0:T(8,128)S(1)} async-done(((f32[64,8,128]{2,1,0:T(8,128)}), f32[64,8,128]{2,1,0:T(8,128)S(1)}, u32[]{:S(2)}, u32[]{:S(2)}) %all-to-all-start.1) | async-done | bytes 262176 | tf_op jit(solution)/shard_map/all_to_all | solution.py:701
  39.8 0.0 copy-start.2
  39.8 0.7 copy-done.2
  40.5 0.0 copy-start
  40.5 0.0 copy-start.1
  40.5 13.8 %image_rows.1 = f32[64,8,128]{2,1,0:T(8,128)} custom-call(s32[1,12]{1,0:T(1,128)} %cutoff_hbm.1, f32[1,12]{1,0:T(1,128)} %weight_hbm.1, f32[1]{0:T(128)S(6)} %copy.15.dose_hbm, f32[64,8,128]{2,1,0:T(8,128)} %copy-done.2, bf16[512,256]{1,0:T(8,128)(2,1)} %constant.19.clone.both_hbm, bf16[128,512]{1,0:T(8,128)(2,1)} %get-tuple-element.9.y_rows_hbm, ...), custom_call_target="tpu_custom_call" | custom-call | tf_op jit(solution)/shard_map/image_rows/pallas_call | solution.py:593
  54.3 14.4 %all_to_all.21 = f32[64,8,128]{2,1,0:T(8,128)S(1)} all-to-all(f32[64,8,128]{2,1,0:T(8,128)} %image_rows.1), channel_id=1, replica_groups=mesh['cond'=4,'px'=64] {'px'}, dimensions={0} | all-to-all | bytes 524288 | tf_op jit(solution)/shard_map/all_to_all | solution.py:695
  68.6 0.1 reduce_sum.19
  68.7 5.2 %collective-permute-start.2 = (f32[8,128]{1,0:T(8,128)S(1)}, f32[8,128]{1,0:T(8,128)S(1)}, u32[]{:S(2)}, u32[]{:S(2)}) collective-permute-start(f32[8,128]{1,0:T(8,128)S(1)} %reduce_sum.19), channel_id=1, source_target_pairs={{0,192},{64,0},{128,64},{192,128},{1,193},{65,1},{129,65},{193,129... | collective-permute-start | bytes 12296 | tf_op jit(solution)/shard_map/ppermute | solution.py:686
  73.9 1.2 %collective-permute-start.1 = (f32[8,128]{1,0:T(8,128)S(1)}, f32[8,128]{1,0:T(8,128)S(1)}, u32[]{:S(2)}, u32[]{:S(2)}) collective-permute-start(f32[8,128]{1,0:T(8,128)S(1)} %reduce_sum.19), channel_id=1, source_target_pairs={{0,128},{64,192},{128,0},{192,64},{1,129},{65,193},{129,1},{193,65... | collective-permute-start | bytes 12296 | tf_op jit(solution)/shard_map/ppermute | solution.py:686
  75.0 2.1 %collective-permute-start = (f32[8,128]{1,0:T(8,128)S(1)}, f32[8,128]{1,0:T(8,128)S(1)}, u32[]{:S(2)}, u32[]{:S(2)}) collective-permute-start(f32[8,128]{1,0:T(8,128)S(1)} %reduce_sum.19), channel_id=1, source_target_pairs={{0,64},{64,128},{128,192},{192,0},{1,65},{65,129},{129,193},{193,1... | collective-permute-start | bytes 12296 | tf_op jit(solution)/shard_map/ppermute | solution.py:686
  77.1 0.0 collective-permute-done.2
  77.1 3.1 %collective-permute-done.1 = f32[8,128]{1,0:T(8,128)S(1)} collective-permute-done((f32[8,128]{1,0:T(8,128)S(1)}, f32[8,128]{1,0:T(8,128)S(1)}, u32[]{:S(2)}, u32[]{:S(2)}) %collective-permute-start.1) | collective-permute-done | bytes 4128 | tf_op jit(solution)/shard_map/ppermute | solution.py:686
  80.2 0.0 collective-permute-done
  80.3 15.4 %all_to_all.22.packed = f32[64,8,128]{2,1,0:T(8,128)S(1)} all-to-all(f32[64,8,128]{2,1,0:T(8,128)S(1)} %broadcast_in_dim.5), channel_id=1, replica_groups=mesh['cond'=4,'px'=64] {'px'}, dimensions={0} | all-to-all | bytes 524288 | tf_op jit(solution)/shard_map/all_to_all | solution.py:701
  95.7 0.0 copy-done
  95.7 0.0 copy-done.1
  95.7 3.3 %mask_gradient.1 = f32[128,2048]{1,0:T(8,128)} custom-call(f32[64,8,128]{2,1,0:T(8,128)S(1)} %all_to_all.22.packed, f32[392,256]{1,0:T(8,128)S(1)} %copy-done, f32[128,2048]{1,0:T(8,128)S(1)} %copy-done.1), custom_call_target="tpu_custom_call" | custom-call | tf_op jit(solution)/shard_map/mask_gradient/pallas_call | solution.py:648
  (2 shorter events, 0.0 us)
Async XLA Ops:
  24.8 5.8 %copy-start.3 = (f32[8,128]{1,0:T(8,128)}, f32[8,128]{1,0:T(8,128)S(1)}, u32[]{:S(2)}) copy-start(f32[8,128]{1,0:T(8,128)S(1)} %reduce_sum.18.after) | copy-start | bytes 12292
  25.5 14.3 %all-to-all-start.1 = ((f32[64,8,128]{2,1,0:T(8,128)}), f32[64,8,128]{2,1,0:T(8,128)S(1)}, u32[]{:S(2)}, u32[]{:S(2)}) async-start(f32[64,8,128]{2,1,0:T(8,128)} %broadcast_in_dim.4), calls=%async_computation.1 | async-start | bytes 524288 | tf_op jit(solution)/shard_map/all_to_all | solution.py:701
  39.8 0.7 copy-start.2
  40.5 55.2 %copy-start = (f32[392,256]{1,0:T(8,128)S(1)}, f32[392,256]{1,0:T(8,128)}, u32[]{:S(2)}) copy-start(f32[392,256]{1,0:T(8,128)} %constant.16.clone.table_hbm.table) | copy-start | bytes 1204228
  40.5 55.2 %copy-start.1 = (f32[128,2048]{1,0:T(8,128)S(1)}, f32[128,2048]{1,0:T(8,128)}, u32[]{:S(2)}) copy-start(f32[128,2048]{1,0:T(8,128)} %get-tuple-element.12.slope_hbm) | copy-start | bytes 3145732
  68.7 8.5 %collective-permute-start.2 = (f32[8,128]{1,0:T(8,128)S(1)}, f32[8,128]{1,0:T(8,128)S(1)}, u32[]{:S(2)}, u32[]{:S(2)}) collective-permute-start(f32[8,128]{1,0:T(8,128)S(1)} %reduce_sum.19), channel_id=1, source_target_pairs={{0,192},{64,0},{128,64},{192,128},{1,193},{65,1},{129,65},{193,129... | collective-permute-start | bytes 12296 | tf_op jit(solution)/shard_map/ppermute | solution.py:686
  73.9 6.4 %collective-permute-start.1 = (f32[8,128]{1,0:T(8,128)S(1)}, f32[8,128]{1,0:T(8,128)S(1)}, u32[]{:S(2)}, u32[]{:S(2)}) collective-permute-start(f32[8,128]{1,0:T(8,128)S(1)} %reduce_sum.19), channel_id=1, source_target_pairs={{0,128},{64,192},{128,0},{192,64},{1,129},{65,193},{129,1},{193,65... | collective-permute-start | bytes 12296 | tf_op jit(solution)/shard_map/ppermute | solution.py:686
  75.0 5.2 %collective-permute-start = (f32[8,128]{1,0:T(8,128)S(1)}, f32[8,128]{1,0:T(8,128)S(1)}, u32[]{:S(2)}, u32[]{:S(2)}) collective-permute-start(f32[8,128]{1,0:T(8,128)S(1)} %reduce_sum.19), channel_id=1, source_target_pairs={{0,64},{64,128},{128,192},{192,0},{1,65},{65,129},{129,193},{193,1... | collective-permute-start | bytes 12296 | tf_op jit(solution)/shard_map/ppermute | solution.py:686

commit v5 on v4

--- a/solution.py
+++ b/solution.py
@@ -202,21 +202,26 @@
     extent,
     y_big,
     y_fine,
+    table,
     after,
     mask_hbm,
     target,
     y_rows,
     y_cols,
+    tables,
     slope,
     sem,
 ):
     band = y_fine.shape[2]
     rows_here, image = target.shape
-    cols_here = slope.shape[1]
+    count, cols_here = slope.shape
+    count -= 8
+    blocks = cols_here // LANES
+    width = (table.shape[0] - 2 * LANES - 8) // 2 * LANES
     place_px = lax.axis_index("px")
     place_cond = lax.axis_index("cond")
     mine = pl.ds(pl.multiple_of(place_cond * cols_here, cols_here), cols_here)
-    copy_mask = pltpu.make_async_copy(mask_hbm.at[:, mine], slope, sem)
+    copy_mask = pltpu.make_async_copy(mask_hbm.at[:, mine], slope.at[:count, :], sem)
     copy_mask.start()
 
     rects = corner.shape[1]
@@ -226,10 +231,10 @@
     right = left + extent[1:2, :]
     places = place_px * rows_here + lax.broadcasted_iota(jnp.int32, (rows_here, rects), 0)
     rows_in = jnp.where((places >= top) & (places < bottom), 1.0, 0.0).astype(bf16)
-    for start, count, first, stride in column_runs(band, image):
-        places = first + stride * lax.broadcasted_iota(jnp.int32, (count, rects), 0)
+    for start, run, first, stride in column_runs(band, image):
+        places = first + stride * lax.broadcasted_iota(jnp.int32, (run, rects), 0)
         cols_in = jnp.where((places >= left) & (places < right), 1.0, 0.0).astype(bf16)
-        target[:, start : start + count] = jnp.minimum(dot(rows_in, cols_in, 1, 1), 1.0)
+        target[:, start : start + run] = jnp.minimum(dot(rows_in, cols_in, 1, 1), 1.0)
 
     big_cos = y_big[0, pl.ds(place_px, 1), :]
     big_sin = y_big[1, pl.ds(place_px, 1), :]
@@ -248,11 +253,19 @@
     stacked = jnp.concatenate([waves_hi, waves_hi, waves_lo], axis=0)
     y_cols[...] = jnp.transpose(stacked).astype(bf16)
 
+    for block in range(blocks + 1):
+        here = pl.ds(block * LANES, LANES)
+        place = place_cond * blocks + block if block < blocks else place_px
+        hi, lo = split(basis_rows(table, place, 1))
+        tables[0, here, :] = hi
+        tables[1, here, :] = lo
     copy_mask.wait()
+    edge_row, _ = edges(table)
     for start in range(0, cols_here, LANES):
         here = pl.ds(start, LANES)
-        transmit = jnp.tanh(slope[:, here])
-        slope[:, here] = 1.0 - transmit * transmit
+        transmit = jnp.tanh(slope[:count, here])
+        slope[:count, here] = (1.0 - transmit * transmit) * (1.0 / width)
+        slope[count:, here] = jnp.broadcast_to(edge_row, (8, LANES))
 
 
 def field_kernel(
@@ -472,58 +485,40 @@
     edge_v = g_im[half : half + 1, 0:1]
     re_hi, re_lo = split(g_re)
     im_hi, im_lo = split(g_im)
-    even, odd = both_t[:, :band], both_t[:, band:]
-    left = dot(even, re_hi) + dot(even, re_lo) + dot(odd, im_hi) + dot(odd, im_lo)
-    right = dot(even, im_hi) + dot(even, im_lo) - dot(odd, re_hi) - dot(odd, re_lo)
-    l_hi, l_lo = split(left)
-    r_hi, r_lo = split(right)
-    even, odd = both[:band, :], both[band:, :]
-    folded = dot(l_hi, even) + dot(l_lo, even) + dot(r_hi, odd) + dot(r_lo, odd)
+    stacked = jnp.concatenate([re_hi, re_lo, im_hi, im_lo], axis=0)
+    with_even = dot(stacked, both[:band, :])
+    with_odd = dot(stacked, both[band:, :])
+    re_even = with_even[:band] + with_even[band : 2 * band]
+    im_even = with_even[2 * band : 3 * band] + with_even[3 * band :]
+    re_odd = with_odd[:band] + with_odd[band : 2 * band]
+    im_odd = with_odd[2 * band : 3 * band] + with_odd[3 * band :]
+    hi, lo = split(jnp.concatenate([re_even + im_odd, im_even - re_odd], axis=0))
+    folded = dot(both_t[...], hi) + dot(both_t[...], lo)
     store_pieces(out, put(put(folded, half - 1, 1, edge_u), 1, half - 1, edge_v))
 
 
-def spread_kernel(packed, table, slope_hbm, out_hbm, slope, out, cols, in_sems, out_sems):
-    steps, count, step = out.shape
-    band = table.shape[1]
+def spread_kernel(packed, tables, slope, out):
+    count, cols_here = out.shape
+    band = tables.shape[2]
     half = band // 2
-    blocks = step // LANES
-    width = (table.shape[0] - 2 * LANES - 8) // 2 * LANES
-    first_block = lax.axis_index("cond") * (steps * blocks)
-
-    def copy_in(place):
-        here = pl.ds(place * step, step)
-        return pltpu.make_async_copy(slope_hbm.at[:, here], slope.at[place], in_sems.at[place])
-
-    def copy_out(place):
-        here = pl.ds(place * step, step)
-        return pltpu.make_async_copy(out.at[place], out_hbm.at[:, here], out_sems.at[place])
-
-    for place in range(steps):
-        copy_in(place).start()
-    row_hi, row_lo = split(basis_rows(table, lax.axis_index("px"), 1))
-    for place in range(steps):
-        hi, lo = split(basis_rows(table, first_block + place * blocks, blocks))
-        cols[place, 0] = hi
-        cols[place, 1] = lo
-    box = load_pieces(packed, band) * (1.0 / width)
+    rows = pl.ds(cols_here, count)
+    box = load_pieces(packed, band)
     edge_u = box[half - 1 : half, 1:2]
     edge_v = box[1:2, half - 1 : half]
     box = put(put(box, half - 1, 1, 0.0), 1, half - 1, 0.0)
-    mixed_hi, mixed_lo = split(dot_split((row_hi, row_lo), split(box)))
+    mixed_hi, mixed_lo = split(dot_split((tables[0, rows, :], tables[1, rows, :]), split(box)))
     mixed = jnp.concatenate([mixed_hi, mixed_lo], axis=0)
-    edge_row, edge_col = edges(table)
-    side = edge_u * edge_col + edge_v * edge_row
-    for place in range(steps):
-        copy_in(place).wait()
-        main = dot(mixed, cols[place, 0], 1, 1)
-        rest = dot(mixed_hi, cols[place, 1], 1, 1)
+    edge = jnp.broadcast_to(slope[count : count + 1, :LANES], (LANES, LANES))
+    side = edge_u * jnp.transpose(edge) + edge_v * edge
+    step = min(512, cols_here)
+    for start in range(0, cols_here, step):
+        here = pl.ds(start, step)
+        main = dot(mixed, tables[0, here, :], 1, 1)
+        rest = dot(mixed_hi, tables[1, here, :], 1, 1)
         grad = main[:count] + (main[count:] + rest)
         for inner in range(0, step, LANES):
-            there = pl.ds(inner, LANES)
-            out[place, :, there] = (grad[:, inner : inner + LANES] + side) * slope[place, :, there]
-        copy_out(place).start()
-    for place in range(steps):
-        copy_out(place).wait()
+            there = pl.ds(start + inner, LANES)
+            out[:, there] = (grad[:, inner : inner + LANES] + side) * slope[:count, there]
 
 
 def params(mebibytes):
@@ -556,8 +551,9 @@
     )(mask_level, table)
 
 
-def call_prepare(shape_corner, shape_extent, after, mask_level, band, pencils, conds):
+def call_prepare(shape_corner, shape_extent, after, mask_level, table, pencils, conds):
     rows_here, width = mask_level.shape
+    band = table.shape[1]
     image_rows = IMAGE // pencils
     cols_here = width // conds
     y_big = np.stack(wave(image_rows * np.arange(pencils), band, IMAGE)).astype(np.float32)
@@ -566,18 +562,19 @@
         ((image_rows, IMAGE), f32),
         ((4 * image_rows, 2 * band), bf16),
         ((2 * band, 6 * image_rows), bf16),
-        ((rows_here, cols_here), f32),
+        ((2, cols_here + rows_here, band), bf16),
+        ((rows_here + 8, cols_here), f32),
     ]
     return pl.pallas_call(
         prepare_kernel,
         out_shape=[jax.ShapeDtypeStruct(*shape) for shape in shapes],
-        in_specs=[vmem] * 4 + [anywhere] * 2,
+        in_specs=[vmem] * 5 + [anywhere] * 2,
         out_specs=[vmem] * len(shapes),
         scratch_shapes=[pltpu.SemaphoreType.DMA],
         compiler_params=params(ROOM),
         cost_estimate=pl.CostEstimate(flops=10**9, bytes_accessed=2 * 10**7, transcendentals=10**6),
         name="prepare",
-    )(shape_corner.T, shape_extent.T, y_big, y_fine, after, mask_level)
+    )(shape_corner.T, shape_extent.T, y_big, y_fine, table, after, mask_level)
 
 
 def call_field(
@@ -640,26 +637,16 @@
     )
 
 
-def call_spread(folded, slope, table):
+def call_spread(folded, tables, slope):
     count, cols_here = slope.shape
-    band = table.shape[1]
-    step = min(512, cols_here)
-    steps = cols_here // step
     return pl.pallas_call(
         spread_kernel,
-        out_shape=jax.ShapeDtypeStruct(slope.shape, f32),
-        in_specs=[vmem, vmem, anywhere],
-        out_specs=anywhere,
-        scratch_shapes=[
-            pltpu.VMEM((steps, count, step), f32),
-            pltpu.VMEM((steps, count, step), f32),
-            pltpu.VMEM((steps, 2, step, band), bf16),
-            pltpu.SemaphoreType.DMA((steps,)),
-            pltpu.SemaphoreType.DMA((steps,)),
-        ],
+        out_shape=jax.ShapeDtypeStruct((count - 8, cols_here), f32),
+        in_specs=[vmem] * 3,
+        out_specs=vmem,
         compiler_params=params(40),
         name="mask_gradient",
-    )(folded, table, slope)
+    )(folded, tables, slope)
 
 
 def local(
@@ -674,8 +661,8 @@
 
     packed = call_mask(mask_level, table, pieces)
     piece = collect(packed)
-    target, y_rows, y_cols, slope = call_prepare(
-        shape_corner, shape_extent, piece, mask_level, band, pencils, conds
+    target, y_rows, y_cols, tables, slope = call_prepare(
+        shape_corner, shape_extent, piece, mask_level, table, pencils, conds
     )
     packed = hand_out(piece, pieces)
     folded = call_field(
@@ -688,7 +675,7 @@
     ]
     piece = functools.reduce(jnp.add, others, piece)
     folded = hand_out(piece, pieces)
-    return call_spread(folded, slope, table)
+    return call_spread(folded, tables, slope)
 
 
 def collect(packed):

time: 99.6 us -> 99.7 us (level)
  waiting for transfers between devices: 8.9 us -> 7.72 us
    pallas_call x1, Pallas kernels: 3.31 us -> 1.89 us  [call_spread(): pl.pallas_call(spread_kernel, out_shape=jax.ShapeDtypeStruct((count - 8,...]
    pallas_call x1, Pallas kernels: 3.37 us -> 4.55 us  [call_prepare(): pl.pallas_call(prepare_kernel, out_shape=[jax.ShapeDtypeStruct(*shape) fo...]
    all_to_all x1, waiting for transfers between devices: 5.8 us -> 4.62 us  [hand_out(): lax.all_to_all(outgoing, 'px', split_axis=0, concat_axis=0, tiled=True)]
  transfers between devices with their start and end apart: 4 -> 4, of which waited for: 2 -> 2; matrix products, arithmetic and copies ran while one was open for 0% -> 0% of each run, Pallas kernels for 3% -> 5%
where the time goes in v5:
time: 99.7 us; the launch traced here: 99.3 us
  blocking collectives  50.5 us (51%)
  Pallas kernels  24.9 us (25%)
  starting transfers between devices  12.9 us (13%)
  waiting for transfers between devices  7.72 us (8%)
  local copies, waits for them, and re-layouts  1.45 us (1%)
  other arithmetic  1.09 us (1%)
    all_to_all x2, blocking collectives, collect(): lax.all_to_all(packed, 'px', split_axis=0, concat_axis=0, tiled=True)  35.3 us
    all_to_all x1, blocking collectives, hand_out(): lax.all_to_all(outgoing, 'px', split_axis=0, concat_axis=0, tiled=True)  15.2 us
    pallas_call x1, Pallas kernels, call_field(): pl.pallas_call(functools.partial(field_kernel, width=width), out_shape=ja...  13.8 us
    ppermute x3, starting transfers between devices, local(): lax.ppermute(piece, 'cond', [(i, (i + d) % conds) for i in range(conds)])  8.45 us
    all_to_all x1, waiting for transfers between devices, hand_out(): lax.all_to_all(outgoing, 'px', split_axis=0, concat_axis=0, tiled=True)  4.62 us
    pallas_call x1, Pallas kernels, call_mask(): pl.pallas_call(mask_kernel, out_shape=jax.ShapeDtypeStruct(pieces, f32),...  4.6 us
    pallas_call x1, Pallas kernels, call_prepare(): pl.pallas_call(prepare_kernel, out_shape=[jax.ShapeDtypeStruct(*shape) fo...  4.55 us
    all_to_all x1, starting transfers between devices, hand_out(): lax.all_to_all(outgoing, 'px', split_axis=0, concat_axis=0, tiled=True)  4.48 us
  transfers between devices with their start and end apart: 4, of which 2 were waited for; matrix products, arithmetic and copies ran while one was open for 0% of the time, Pallas kernels for 5%

profile of v5, /device:TPU:1, one launch (start us, length us, event | category | flops | bytes accessed | tf_op | source)
XLA Modules:
  0.0 99.3 jit_solution(14224222767845026224)
XLA Ops:
  0.0 4.6 %mask_rows.1 = f32[64,8,128]{2,1,0:T(8,128)} custom-call(f32[128,8192]{1,0:T(8,128)} %mask_hbm.3, f32[392,256]{1,0:T(8,128)} %constant.16.clone.table_hbm.table), custom_call_target="tpu_custom_call" | custom-call | tf_op jit(solution)/shard_map/mask_rows/pallas_call | solution.py:537
  4.6 20.1 %all_to_all.20 = f32[64,8,128]{2,1,0:T(8,128)S(1)} all-to-all(f32[64,8,128]{2,1,0:T(8,128)} %mask_rows.1), channel_id=1, replica_groups=mesh['cond'=4,'px'=64] {'px'}, dimensions={0} | all-to-all | bytes 524288 | tf_op jit(solution)/shard_map/all_to_all | solution.py:682
  24.7 0.1 reduce_sum.18.after
  24.8 0.0 copy-start.3
  24.8 0.7 broadcast_in_dim.4
  25.5 4.5 %all-to-all-start.1 = ((f32[64,8,128]{2,1,0:T(8,128)}), f32[64,8,128]{2,1,0:T(8,128)S(1)}, u32[]{:S(2)}, u32[]{:S(2)}) async-start(f32[64,8,128]{2,1,0:T(8,128)} %broadcast_in_dim.4), calls=%async_computation.1 | async-start | bytes 524288 | tf_op jit(solution)/shard_map/all_to_all | solution.py:688
  30.6 0.0 copy-done.3
  30.6 4.6 %prepare.1 = (f32[32,2048]{1,0:T(8,128)}, bf16[128,512]{1,0:T(8,128)(2,1)}, bf16[512,192]{1,0:T(8,128)(2,1)}, bf16[2,2176,256]{2,1,0:T(8,128)(2,1)}, f32[136,2048]{1,0:T(8,128)}) custom-call(s32[2,256]{1,0:T(2,128)} %bitcast.2, s32[2,256]{1,0:T(2,128)} %bitcast.3, f32[2,64,256]{2,1,0:T(8,128)} %constant.17.clone.y_big, f32[2,32,256]{2,1,0:T(8,128)} %constant.18.clone.y_fine, ...), custom_call_target="tpu_custom_call" | custom-call | flops 1000000000 | bytes 20000000 | tf_op jit(solution)/shard_map/prepare/pallas_call | solution.py:568
  35.2 4.6 %all-to-all-done.1.packed_hbm = f32[64,8,128]{2,1,0:T(8,128)S(1)} async-done(((f32[64,8,128]{2,1,0:T(8,128)}), f32[64,8,128]{2,1,0:T(8,128)S(1)}, u32[]{:S(2)}, u32[]{:S(2)}) %all-to-all-start.1) | async-done | bytes 262176 | tf_op jit(solution)/shard_map/all_to_all | solution.py:688
  39.8 0.0 copy-start.2
  39.8 0.7 copy-done.2
  40.5 0.0 copy-start
  40.5 13.8 %image_rows.1 = f32[64,8,128]{2,1,0:T(8,128)} custom-call(s32[1,12]{1,0:T(1,128)} %cutoff_hbm.1, f32[1,12]{1,0:T(1,128)} %weight_hbm.1, f32[1]{0:T(128)S(6)} %copy.15.dose_hbm, f32[64,8,128]{2,1,0:T(8,128)} %copy-done.2, bf16[512,256]{1,0:T(8,128)(2,1)} %constant.19.clone.both_hbm, bf16[128,512]{1,0:T(8,128)(2,1)} %get-tuple-element.10.y_rows_hbm, ...), custom_call_target="tpu_custom_call" | custom-call | tf_op jit(solution)/shard_map/image_rows/pallas_call | solution.py:590
  54.3 0.0 copy-start.1
  54.4 15.2 %all_to_all.21 = f32[64,8,128]{2,1,0:T(8,128)} all-to-all(f32[64,8,128]{2,1,0:T(8,128)} %image_rows.1), channel_id=1, replica_groups=mesh['cond'=4,'px'=64] {'px'}, dimensions={0} | all-to-all | bytes 524288 | tf_op jit(solution)/shard_map/all_to_all | solution.py:682
  69.6 1.0 %reduce_sum.19 = f32[8,128]{1,0:T(8,128)S(1)} reduce(f32[64,8,128]{2,1,0:T(8,128)} %all_to_all.21, f32[]{:T(128)} %constant.7.clone.1), dimensions={0}, to_apply=%region_1.0 | reduce | flops 64512 | bytes 266244 | tf_op jit(solution)/shard_map/reduce_sum | solution.py:683
  70.6 5.2 %collective-permute-start.2 = (f32[8,128]{1,0:T(8,128)S(1)}, f32[8,128]{1,0:T(8,128)S(1)}, u32[]{:S(2)}, u32[]{:S(2)}) collective-permute-start(f32[8,128]{1,0:T(8,128)S(1)} %reduce_sum.19), channel_id=1, source_target_pairs={{0,192},{64,0},{128,64},{192,128},{1,193},{65,1},{129,65},{193,129... | collective-permute-start | bytes 12296 | tf_op jit(solution)/shard_map/ppermute | solution.py:673
  75.8 1.2 %collective-permute-start.1 = (f32[8,128]{1,0:T(8,128)S(1)}, f32[8,128]{1,0:T(8,128)S(1)}, u32[]{:S(2)}, u32[]{:S(2)}) collective-permute-start(f32[8,128]{1,0:T(8,128)S(1)} %reduce_sum.19), channel_id=1, source_target_pairs={{0,128},{64,192},{128,0},{192,64},{1,129},{65,193},{129,1},{193,65... | collective-permute-start | bytes 12296 | tf_op jit(solution)/shard_map/ppermute | solution.py:673
  76.9 2.1 %collective-permute-start = (f32[8,128]{1,0:T(8,128)S(1)}, f32[8,128]{1,0:T(8,128)S(1)}, u32[]{:S(2)}, u32[]{:S(2)}) collective-permute-start(f32[8,128]{1,0:T(8,128)S(1)} %reduce_sum.19), channel_id=1, source_target_pairs={{0,64},{64,128},{128,192},{192,0},{1,65},{65,129},{129,193},{193,1... | collective-permute-start | bytes 12296 | tf_op jit(solution)/shard_map/ppermute | solution.py:673
  79.0 0.0 collective-permute-done.2
  79.0 3.1 %collective-permute-done.1 = f32[8,128]{1,0:T(8,128)S(1)} collective-permute-done((f32[8,128]{1,0:T(8,128)S(1)}, f32[8,128]{1,0:T(8,128)S(1)}, u32[]{:S(2)}, u32[]{:S(2)}) %collective-permute-start.1) | collective-permute-done | bytes 4128 | tf_op jit(solution)/shard_map/ppermute | solution.py:673
  82.1 0.0 collective-permute-done
  82.2 15.2 %all_to_all.22.packed = f32[64,8,128]{2,1,0:T(8,128)S(1)} all-to-all(f32[64,8,128]{2,1,0:T(8,128)S(1)} %broadcast_in_dim.5), channel_id=1, replica_groups=mesh['cond'=4,'px'=64] {'px'}, dimensions={0} | all-to-all | bytes 524288 | tf_op jit(solution)/shard_map/all_to_all | solution.py:688
  97.4 0.0 copy-done
  97.4 0.0 copy-done.1
  97.4 1.9 %mask_gradient.1 = f32[128,2048]{1,0:T(8,128)} custom-call(f32[64,8,128]{2,1,0:T(8,128)S(1)} %all_to_all.22.packed, bf16[2,2176,256]{2,1,0:T(8,128)(2,1)S(1)} %copy-done, f32[136,2048]{1,0:T(8,128)S(1)} %copy-done.1), custom_call_target="tpu_custom_call" | custom-call | tf_op jit(solution)/shard_map/mask_gradient/pallas_call | solution.py:642
  (2 shorter events, 0.0 us)
Async XLA Ops:
  24.8 5.9 %copy-start.3 = (f32[8,128]{1,0:T(8,128)}, f32[8,128]{1,0:T(8,128)S(1)}, u32[]{:S(2)}) copy-start(f32[8,128]{1,0:T(8,128)S(1)} %reduce_sum.18.after) | copy-start | bytes 12292
  25.5 14.3 %all-to-all-start.1 = ((f32[64,8,128]{2,1,0:T(8,128)}), f32[64,8,128]{2,1,0:T(8,128)S(1)}, u32[]{:S(2)}, u32[]{:S(2)}) async-start(f32[64,8,128]{2,1,0:T(8,128)} %broadcast_in_dim.4), calls=%async_computation.1 | async-start | bytes 524288 | tf_op jit(solution)/shard_map/all_to_all | solution.py:688
  39.8 0.7 copy-start.2
  40.5 56.9 %copy-start = (bf16[2,2176,256]{2,1,0:T(8,128)(2,1)S(1)}, bf16[2,2176,256]{2,1,0:T(8,128)(2,1)}, u32[]{:S(2)}) copy-start(bf16[2,2176,256]{2,1,0:T(8,128)(2,1)} %get-tuple-element.13.tables) | copy-start | bytes 6684676
  54.3 43.0 %copy-start.1 = (f32[136,2048]{1,0:T(8,128)S(1)}, f32[136,2048]{1,0:T(8,128)}, u32[]{:S(2)}) copy-start(f32[136,2048]{1,0:T(8,128)} %get-tuple-element.14.slope) | copy-start | bytes 3342340
  70.6 8.5 %collective-permute-start.2 = (f32[8,128]{1,0:T(8,128)S(1)}, f32[8,128]{1,0:T(8,128)S(1)}, u32[]{:S(2)}, u32[]{:S(2)}) collective-permute-start(f32[8,128]{1,0:T(8,128)S(1)} %reduce_sum.19), channel_id=1, source_target_pairs={{0,192},{64,0},{128,64},{192,128},{1,193},{65,1},{129,65},{193,129... | collective-permute-start | bytes 12296 | tf_op jit(solution)/shard_map/ppermute | solution.py:673
  75.8 6.4 %collective-permute-start.1 = (f32[8,128]{1,0:T(8,128)S(1)}, f32[8,128]{1,0:T(8,128)S(1)}, u32[]{:S(2)}, u32[]{:S(2)}) collective-permute-start(f32[8,128]{1,0:T(8,128)S(1)} %reduce_sum.19), channel_id=1, source_target_pairs={{0,128},{64,192},{128,0},{192,64},{1,129},{65,193},{129,1},{193,65... | collective-permute-start | bytes 12296 | tf_op jit(solution)/shard_map/ppermute | solution.py:673
  76.9 5.2 %collective-permute-start = (f32[8,128]{1,0:T(8,128)S(1)}, f32[8,128]{1,0:T(8,128)S(1)}, u32[]{:S(2)}, u32[]{:S(2)}) collective-permute-start(f32[8,128]{1,0:T(8,128)S(1)} %reduce_sum.19), channel_id=1, source_target_pairs={{0,64},{64,128},{128,192},{192,0},{1,65},{65,129},{129,193},{193,1... | collective-permute-start | bytes 12296 | tf_op jit(solution)/shard_map/ppermute | solution.py:673

commit v6 on v4

--- a/solution.py
+++ b/solution.py
@@ -482,48 +482,32 @@
     store_pieces(out, put(put(folded, half - 1, 1, edge_u), 1, half - 1, edge_v))
 
 
-def spread_kernel(packed, table, slope_hbm, out_hbm, slope, out, cols, in_sems, out_sems):
-    steps, count, step = out.shape
+def spread_kernel(packed, table, slope, out):
+    count, cols_here = out.shape
     band = table.shape[1]
     half = band // 2
+    step = min(512, cols_here)
     blocks = step // LANES
     width = (table.shape[0] - 2 * LANES - 8) // 2 * LANES
-    first_block = lax.axis_index("cond") * (steps * blocks)
-
-    def copy_in(place):
-        here = pl.ds(place * step, step)
-        return pltpu.make_async_copy(slope_hbm.at[:, here], slope.at[place], in_sems.at[place])
-
-    def copy_out(place):
-        here = pl.ds(place * step, step)
-        return pltpu.make_async_copy(out.at[place], out_hbm.at[:, here], out_sems.at[place])
-
-    for place in range(steps):
-        copy_in(place).start()
-    row_hi, row_lo = split(basis_rows(table, lax.axis_index("px"), 1))
-    for place in range(steps):
-        hi, lo = split(basis_rows(table, first_block + place * blocks, blocks))
-        cols[place, 0] = hi
-        cols[place, 1] = lo
+    first_block = lax.axis_index("cond") * (cols_here // LANES)
     box = load_pieces(packed, band) * (1.0 / width)
     edge_u = box[half - 1 : half, 1:2]
     edge_v = box[1:2, half - 1 : half]
     box = put(put(box, half - 1, 1, 0.0), 1, half - 1, 0.0)
-    mixed_hi, mixed_lo = split(dot_split((row_hi, row_lo), split(box)))
+    mixed_hi, mixed_lo = split(
+        dot_split(split(basis_rows(table, lax.axis_index("px"), 1)), split(box))
+    )
     mixed = jnp.concatenate([mixed_hi, mixed_lo], axis=0)
     edge_row, edge_col = edges(table)
     side = edge_u * edge_col + edge_v * edge_row
-    for place in range(steps):
-        copy_in(place).wait()
-        main = dot(mixed, cols[place, 0], 1, 1)
-        rest = dot(mixed_hi, cols[place, 1], 1, 1)
+    for start in range(0, cols_here, step):
+        hi, lo = split(basis_rows(table, first_block + start // LANES, blocks))
+        main = dot(mixed, hi, 1, 1)
+        rest = dot(mixed_hi, lo, 1, 1)
         grad = main[:count] + (main[count:] + rest)
         for inner in range(0, step, LANES):
-            there = pl.ds(inner, LANES)
-            out[place, :, there] = (grad[:, inner : inner + LANES] + side) * slope[place, :, there]
-        copy_out(place).start()
-    for place in range(steps):
-        copy_out(place).wait()
+            there = pl.ds(start + inner, LANES)
+            out[:, there] = (grad[:, inner : inner + LANES] + side) * slope[:, there]
 
 
 def params(mebibytes):
@@ -641,22 +625,11 @@
 
 
 def call_spread(folded, slope, table):
-    count, cols_here = slope.shape
-    band = table.shape[1]
-    step = min(512, cols_here)
-    steps = cols_here // step
     return pl.pallas_call(
         spread_kernel,
         out_shape=jax.ShapeDtypeStruct(slope.shape, f32),
-        in_specs=[vmem, vmem, anywhere],
-        out_specs=anywhere,
-        scratch_shapes=[
-            pltpu.VMEM((steps, count, step), f32),
-            pltpu.VMEM((steps, count, step), f32),
-            pltpu.VMEM((steps, 2, step, band), bf16),
-            pltpu.SemaphoreType.DMA((steps,)),
-            pltpu.SemaphoreType.DMA((steps,)),
-        ],
+        in_specs=[vmem] * 3,
+        out_specs=vmem,
         compiler_params=params(40),
         name="mask_gradient",
     )(folded, table, slope)

time: 99.6 us -> 97.8 us (0.982)
  Pallas kernels: 25 us -> 23.7 us
    pallas_call x1, Pallas kernels: 3.31 us -> 1.97 us  [call_spread(): pl.pallas_call(spread_kernel, out_shape=jax.ShapeDtypeStruct(slope.shape,...]
where the time goes in v6:
time: 97.8 us; the launch traced here: 97.5 us
  blocking collectives  49.7 us (51%)
  Pallas kernels  23.7 us (24%)
  starting transfers between devices  12.9 us (13%)
  waiting for transfers between devices  8.9 us (9%)
  local copies, waits for them, and re-layouts  1.43 us (1%)
    all_to_all x2, blocking collectives, collect(): lax.all_to_all(packed, 'px', split_axis=0, concat_axis=0, tiled=True)  34.5 us
    all_to_all x1, blocking collectives, hand_out(): lax.all_to_all(outgoing, 'px', split_axis=0, concat_axis=0, tiled=True)  15.2 us
    pallas_call x1, Pallas kernels, call_field(): pl.pallas_call(functools.partial(field_kernel, width=width), out_shape=ja...  13.8 us
    ppermute x3, starting transfers between devices, local(): lax.ppermute(piece, 'cond', [(i, (i + d) % conds) for i in range(conds)])  8.45 us
    all_to_all x1, waiting for transfers between devices, hand_out(): lax.all_to_all(outgoing, 'px', split_axis=0, concat_axis=0, tiled=True)  5.8 us
    pallas_call x1, Pallas kernels, call_mask(): pl.pallas_call(mask_kernel, out_shape=jax.ShapeDtypeStruct(pieces, f32),...  4.6 us
    all_to_all x1, starting transfers between devices, hand_out(): lax.all_to_all(outgoing, 'px', split_axis=0, concat_axis=0, tiled=True)  4.46 us
    pallas_call x1, Pallas kernels, call_prepare(): pl.pallas_call(prepare_kernel, out_shape=[jax.ShapeDtypeStruct(*shape) fo...  3.37 us
  transfers between devices with their start and end apart: 4, of which 2 were waited for; matrix products, arithmetic and copies ran while one was open for 0% of the time, Pallas kernels for 3%

profile of v6, /device:TPU:1, one launch (start us, length us, event | category | flops | bytes accessed | tf_op | source)
XLA Modules:
  0.0 97.5 jit_solution(14468492589756761370)
XLA Ops:
  0.0 4.6 %mask_rows.1 = f32[64,8,128]{2,1,0:T(8,128)} custom-call(f32[128,8192]{1,0:T(8,128)} %mask_hbm.3, f32[392,256]{1,0:T(8,128)} %constant.16.clone.table_hbm.table), custom_call_target="tpu_custom_call" | custom-call | tf_op jit(solution)/shard_map/mask_rows/pallas_call | solution.py:526
  4.6 20.1 %all_to_all.20 = f32[64,8,128]{2,1,0:T(8,128)S(1)} all-to-all(f32[64,8,128]{2,1,0:T(8,128)} %mask_rows.1), channel_id=1, replica_groups=mesh['cond'=4,'px'=64] {'px'}, dimensions={0} | all-to-all | bytes 524288 | tf_op jit(solution)/shard_map/all_to_all | solution.py:668
  24.7 0.1 reduce_sum.18.after
  24.8 0.0 copy-start.3
  24.8 0.7 broadcast_in_dim.4
  25.5 4.5 %all-to-all-start.1 = ((f32[64,8,128]{2,1,0:T(8,128)}), f32[64,8,128]{2,1,0:T(8,128)S(1)}, u32[]{:S(2)}, u32[]{:S(2)}) async-start(f32[64,8,128]{2,1,0:T(8,128)} %broadcast_in_dim.4), calls=%async_computation.1 | async-start | bytes 524288 | tf_op jit(solution)/shard_map/all_to_all | solution.py:674
  30.6 0.0 copy-done.3
  30.6 3.4 %prepare.1 = (f32[32,2048]{1,0:T(8,128)}, bf16[128,512]{1,0:T(8,128)(2,1)}, bf16[512,192]{1,0:T(8,128)(2,1)}, f32[128,2048]{1,0:T(8,128)}) custom-call(s32[2,256]{1,0:T(2,128)} %bitcast.2, s32[2,256]{1,0:T(2,128)} %bitcast.3, f32[2,64,256]{2,1,0:T(8,128)} %constant.17.clone.y_big, f32[2,32,256]{2,1,0:T(8,128)} %constant.18.clone.y_fine, f32[8,128]{1,0:T(8,128)} %copy-done.3, ...), custom_call_target="tpu_custom_call" | custom-call | flops 1000000000 | bytes 20000000 | tf_op jit(solution)/shard_map/prepare/pallas_call | solution.py:555
  34.0 5.8 %all-to-all-done.1.packed_hbm = f32[64,8,128]{2,1,0:T(8,128)S(1)} async-done(((f32[64,8,128]{2,1,0:T(8,128)}), f32[64,8,128]{2,1,0:T(8,128)S(1)}, u32[]{:S(2)}, u32[]{:S(2)}) %all-to-all-start.1) | async-done | bytes 262176 | tf_op jit(solution)/shard_map/all_to_all | solution.py:674
  39.8 0.0 copy-start.2
  39.8 0.7 copy-done.2
  40.5 0.0 copy-start
  40.5 0.0 copy-start.1
  40.5 13.8 %image_rows.1 = f32[64,8,128]{2,1,0:T(8,128)} custom-call(s32[1,12]{1,0:T(1,128)} %cutoff_hbm.1, f32[1,12]{1,0:T(1,128)} %weight_hbm.1, f32[1]{0:T(128)S(6)} %copy.15.dose_hbm, f32[64,8,128]{2,1,0:T(8,128)} %copy-done.2, bf16[512,256]{1,0:T(8,128)(2,1)} %constant.19.clone.both_hbm, bf16[128,512]{1,0:T(8,128)(2,1)} %get-tuple-element.9.y_rows_hbm, ...), custom_call_target="tpu_custom_call" | custom-call | tf_op jit(solution)/shard_map/image_rows/pallas_call | solution.py:577
  54.3 14.4 %all_to_all.21 = f32[64,8,128]{2,1,0:T(8,128)S(1)} all-to-all(f32[64,8,128]{2,1,0:T(8,128)} %image_rows.1), channel_id=1, replica_groups=mesh['cond'=4,'px'=64] {'px'}, dimensions={0} | all-to-all | bytes 524288 | tf_op jit(solution)/shard_map/all_to_all | solution.py:668
  68.6 0.1 reduce_sum.19
  68.7 5.2 %collective-permute-start.2 = (f32[8,128]{1,0:T(8,128)S(1)}, f32[8,128]{1,0:T(8,128)S(1)}, u32[]{:S(2)}, u32[]{:S(2)}) collective-permute-start(f32[8,128]{1,0:T(8,128)S(1)} %reduce_sum.19), channel_id=1, source_target_pairs={{0,192},{64,0},{128,64},{192,128},{1,193},{65,1},{129,65},{193,129... | collective-permute-start | bytes 12296 | tf_op jit(solution)/shard_map/ppermute | solution.py:659
  73.9 1.2 %collective-permute-start.1 = (f32[8,128]{1,0:T(8,128)S(1)}, f32[8,128]{1,0:T(8,128)S(1)}, u32[]{:S(2)}, u32[]{:S(2)}) collective-permute-start(f32[8,128]{1,0:T(8,128)S(1)} %reduce_sum.19), channel_id=1, source_target_pairs={{0,128},{64,192},{128,0},{192,64},{1,129},{65,193},{129,1},{193,65... | collective-permute-start | bytes 12296 | tf_op jit(solution)/shard_map/ppermute | solution.py:659
  75.0 2.1 %collective-permute-start = (f32[8,128]{1,0:T(8,128)S(1)}, f32[8,128]{1,0:T(8,128)S(1)}, u32[]{:S(2)}, u32[]{:S(2)}) collective-permute-start(f32[8,128]{1,0:T(8,128)S(1)} %reduce_sum.19), channel_id=1, source_target_pairs={{0,64},{64,128},{128,192},{192,0},{1,65},{65,129},{129,193},{193,1... | collective-permute-start | bytes 12296 | tf_op jit(solution)/shard_map/ppermute | solution.py:659
  77.1 0.0 collective-permute-done.2
  77.1 3.1 %collective-permute-done.1 = f32[8,128]{1,0:T(8,128)S(1)} collective-permute-done((f32[8,128]{1,0:T(8,128)S(1)}, f32[8,128]{1,0:T(8,128)S(1)}, u32[]{:S(2)}, u32[]{:S(2)}) %collective-permute-start.1) | collective-permute-done | bytes 4128 | tf_op jit(solution)/shard_map/ppermute | solution.py:659
  80.2 0.0 collective-permute-done
  80.3 15.2 %all_to_all.22.packed = f32[64,8,128]{2,1,0:T(8,128)S(1)} all-to-all(f32[64,8,128]{2,1,0:T(8,128)S(1)} %broadcast_in_dim.5), channel_id=1, replica_groups=mesh['cond'=4,'px'=64] {'px'}, dimensions={0} | all-to-all | bytes 524288 | tf_op jit(solution)/shard_map/all_to_all | solution.py:674
  95.5 0.0 copy-done
  95.5 0.0 copy-done.1
  95.5 2.0 %mask_gradient.1 = f32[128,2048]{1,0:T(8,128)} custom-call(f32[64,8,128]{2,1,0:T(8,128)S(1)} %all_to_all.22.packed, f32[392,256]{1,0:T(8,128)S(1)} %copy-done, f32[128,2048]{1,0:T(8,128)S(1)} %copy-done.1), custom_call_target="tpu_custom_call" | custom-call | tf_op jit(solution)/shard_map/mask_gradient/pallas_call | solution.py:628
  (2 shorter events, 0.0 us)
Async XLA Ops:
  24.8 5.8 %copy-start.3 = (f32[8,128]{1,0:T(8,128)}, f32[8,128]{1,0:T(8,128)S(1)}, u32[]{:S(2)}) copy-start(f32[8,128]{1,0:T(8,128)S(1)} %reduce_sum.18.after) | copy-start | bytes 12292
  25.5 14.3 %all-to-all-start.1 = ((f32[64,8,128]{2,1,0:T(8,128)}), f32[64,8,128]{2,1,0:T(8,128)S(1)}, u32[]{:S(2)}, u32[]{:S(2)}) async-start(f32[64,8,128]{2,1,0:T(8,128)} %broadcast_in_dim.4), calls=%async_computation.1 | async-start | bytes 524288 | tf_op jit(solution)/shard_map/all_to_all | solution.py:674
  39.8 0.7 copy-start.2
  40.5 55.0 %copy-start = (f32[392,256]{1,0:T(8,128)S(1)}, f32[392,256]{1,0:T(8,128)}, u32[]{:S(2)}) copy-start(f32[392,256]{1,0:T(8,128)} %constant.16.clone.table_hbm.table) | copy-start | bytes 1204228
  40.5 55.0 %copy-start.1 = (f32[128,2048]{1,0:T(8,128)S(1)}, f32[128,2048]{1,0:T(8,128)}, u32[]{:S(2)}) copy-start(f32[128,2048]{1,0:T(8,128)} %get-tuple-element.12.slope) | copy-start | bytes 3145732
  68.7 8.5 %collective-permute-start.2 = (f32[8,128]{1,0:T(8,128)S(1)}, f32[8,128]{1,0:T(8,128)S(1)}, u32[]{:S(2)}, u32[]{:S(2)}) collective-permute-start(f32[8,128]{1,0:T(8,128)S(1)} %reduce_sum.19), channel_id=1, source_target_pairs={{0,192},{64,0},{128,64},{192,128},{1,193},{65,1},{129,65},{193,129... | collective-permute-start | bytes 12296 | tf_op jit(solution)/shard_map/ppermute | solution.py:659
  73.9 6.4 %collective-permute-start.1 = (f32[8,128]{1,0:T(8,128)S(1)}, f32[8,128]{1,0:T(8,128)S(1)}, u32[]{:S(2)}, u32[]{:S(2)}) collective-permute-start(f32[8,128]{1,0:T(8,128)S(1)} %reduce_sum.19), channel_id=1, source_target_pairs={{0,128},{64,192},{128,0},{192,64},{1,129},{65,193},{129,1},{193,65... | collective-permute-start | bytes 12296 | tf_op jit(solution)/shard_map/ppermute | solution.py:659
  75.0 5.2 %collective-permute-start = (f32[8,128]{1,0:T(8,128)S(1)}, f32[8,128]{1,0:T(8,128)S(1)}, u32[]{:S(2)}, u32[]{:S(2)}) collective-permute-start(f32[8,128]{1,0:T(8,128)S(1)} %reduce_sum.19), channel_id=1, source_target_pairs={{0,64},{64,128},{128,192},{192,0},{1,65},{65,129},{129,193},{193,1... | collective-permute-start | bytes 12296 | tf_op jit(solution)/shard_map/ppermute | solution.py:659

commit v7 on v6

--- a/solution.py
+++ b/solution.py
@@ -11,7 +11,7 @@
 
 IMAGE = 2048
 LANES = 128
-SLOTS = 2
+SLOTS = 4
 ROOM = 60
 AHEAD = 4
 steepness = 6.0
@@ -521,7 +521,7 @@
 def call_mask(mask_level, table, pieces):
     rows_here, width = mask_level.shape
     band = table.shape[1]
-    chunk = min(512, width // 4)
+    chunk = min(1024, width // 4)
     steps = width // chunk
     return pl.pallas_call(
         mask_kernel,

time: 97.8 us -> 97.7 us (level)
  no operation moved by 1% of the time
where the time goes in v7:
time: 97.7 us; the launch traced here: 97.3 us
  blocking collectives  49.7 us (51%)
  Pallas kernels  23.6 us (24%)
  starting transfers between devices  12.9 us (13%)
  waiting for transfers between devices  8.91 us (9%)
  local copies, waits for them, and re-layouts  1.43 us (1%)
    all_to_all x2, blocking collectives, collect(): lax.all_to_all(packed, 'px', split_axis=0, concat_axis=0, tiled=True)  34.5 us
    all_to_all x1, blocking collectives, hand_out(): lax.all_to_all(outgoing, 'px', split_axis=0, concat_axis=0, tiled=True)  15.2 us
    pallas_call x1, Pallas kernels, call_field(): pl.pallas_call(functools.partial(field_kernel, width=width), out_shape=ja...  13.7 us
    ppermute x3, starting transfers between devices, local(): lax.ppermute(piece, 'cond', [(i, (i + d) % conds) for i in range(conds)])  8.45 us
    all_to_all x1, waiting for transfers between devices, hand_out(): lax.all_to_all(outgoing, 'px', split_axis=0, concat_axis=0, tiled=True)  5.8 us
    pallas_call x1, Pallas kernels, call_mask(): pl.pallas_call(mask_kernel, out_shape=jax.ShapeDtypeStruct(pieces, f32),...  4.47 us
    all_to_all x1, starting transfers between devices, hand_out(): lax.all_to_all(outgoing, 'px', split_axis=0, concat_axis=0, tiled=True)  4.46 us
    pallas_call x1, Pallas kernels, call_prepare(): pl.pallas_call(prepare_kernel, out_shape=[jax.ShapeDtypeStruct(*shape) fo...  3.37 us
  transfers between devices with their start and end apart: 4, of which 2 were waited for; matrix products, arithmetic and copies ran while one was open for 0% of the time, Pallas kernels for 3%

profile of v7, /device:TPU:1, one launch (start us, length us, event | category | flops | bytes accessed | tf_op | source)
XLA Modules:
  0.0 97.3 jit_solution(15183846403597264130)
XLA Ops:
  0.0 4.5 %mask_rows.1 = f32[64,8,128]{2,1,0:T(8,128)} custom-call(f32[128,8192]{1,0:T(8,128)} %mask_hbm.3, f32[392,256]{1,0:T(8,128)} %constant.16.clone.table_hbm.table), custom_call_target="tpu_custom_call" | custom-call | tf_op jit(solution)/shard_map/mask_rows/pallas_call | solution.py:526
  4.5 20.1 %all_to_all.20 = f32[64,8,128]{2,1,0:T(8,128)S(1)} all-to-all(f32[64,8,128]{2,1,0:T(8,128)} %mask_rows.1), channel_id=1, replica_groups=mesh['cond'=4,'px'=64] {'px'}, dimensions={0} | all-to-all | bytes 524288 | tf_op jit(solution)/shard_map/all_to_all | solution.py:668
  24.6 0.1 reduce_sum.18.after
  24.6 0.0 copy-start.3
  24.6 0.7 broadcast_in_dim.4
  25.3 4.5 %all-to-all-start.1 = ((f32[64,8,128]{2,1,0:T(8,128)}), f32[64,8,128]{2,1,0:T(8,128)S(1)}, u32[]{:S(2)}, u32[]{:S(2)}) async-start(f32[64,8,128]{2,1,0:T(8,128)} %broadcast_in_dim.4), calls=%async_computation.1 | async-start | bytes 524288 | tf_op jit(solution)/shard_map/all_to_all | solution.py:674
  30.5 0.0 copy-done.3
  30.5 3.4 %prepare.1 = (f32[32,2048]{1,0:T(8,128)}, bf16[128,512]{1,0:T(8,128)(2,1)}, bf16[512,192]{1,0:T(8,128)(2,1)}, f32[128,2048]{1,0:T(8,128)}) custom-call(s32[2,256]{1,0:T(2,128)} %bitcast.2, s32[2,256]{1,0:T(2,128)} %bitcast.3, f32[2,64,256]{2,1,0:T(8,128)} %constant.17.clone.y_big, f32[2,32,256]{2,1,0:T(8,128)} %constant.18.clone.y_fine, f32[8,128]{1,0:T(8,128)} %copy-done.3, ...), custom_call_target="tpu_custom_call" | custom-call | flops 1000000000 | bytes 20000000 | tf_op jit(solution)/shard_map/prepare/pallas_call | solution.py:555
  33.9 5.8 %all-to-all-done.1.packed_hbm = f32[64,8,128]{2,1,0:T(8,128)S(1)} async-done(((f32[64,8,128]{2,1,0:T(8,128)}), f32[64,8,128]{2,1,0:T(8,128)S(1)}, u32[]{:S(2)}, u32[]{:S(2)}) %all-to-all-start.1) | async-done | bytes 262176 | tf_op jit(solution)/shard_map/all_to_all | solution.py:674
  39.7 0.0 copy-start.2
  39.7 0.7 copy-done.2
  40.3 0.0 copy-start
  40.4 0.0 copy-start.1
  40.4 13.7 %image_rows.1 = f32[64,8,128]{2,1,0:T(8,128)} custom-call(s32[1,12]{1,0:T(1,128)} %cutoff_hbm.1, f32[1,12]{1,0:T(1,128)} %weight_hbm.1, f32[1]{0:T(128)S(6)} %copy.15.dose_hbm, f32[64,8,128]{2,1,0:T(8,128)} %copy-done.2, bf16[512,256]{1,0:T(8,128)(2,1)} %constant.19.clone.both_hbm, bf16[128,512]{1,0:T(8,128)(2,1)} %get-tuple-element.9.y_rows_hbm, ...), custom_call_target="tpu_custom_call" | custom-call | tf_op jit(solution)/shard_map/image_rows/pallas_call | solution.py:577
  54.1 14.4 %all_to_all.21 = f32[64,8,128]{2,1,0:T(8,128)S(1)} all-to-all(f32[64,8,128]{2,1,0:T(8,128)} %image_rows.1), channel_id=1, replica_groups=mesh['cond'=4,'px'=64] {'px'}, dimensions={0} | all-to-all | bytes 524288 | tf_op jit(solution)/shard_map/all_to_all | solution.py:668
  68.5 0.1 reduce_sum.19
  68.6 5.2 %collective-permute-start.2 = (f32[8,128]{1,0:T(8,128)S(1)}, f32[8,128]{1,0:T(8,128)S(1)}, u32[]{:S(2)}, u32[]{:S(2)}) collective-permute-start(f32[8,128]{1,0:T(8,128)S(1)} %reduce_sum.19), channel_id=1, source_target_pairs={{0,192},{64,0},{128,64},{192,128},{1,193},{65,1},{129,65},{193,129... | collective-permute-start | bytes 12296 | tf_op jit(solution)/shard_map/ppermute | solution.py:659
  73.8 1.2 %collective-permute-start.1 = (f32[8,128]{1,0:T(8,128)S(1)}, f32[8,128]{1,0:T(8,128)S(1)}, u32[]{:S(2)}, u32[]{:S(2)}) collective-permute-start(f32[8,128]{1,0:T(8,128)S(1)} %reduce_sum.19), channel_id=1, source_target_pairs={{0,128},{64,192},{128,0},{192,64},{1,129},{65,193},{129,1},{193,65... | collective-permute-start | bytes 12296 | tf_op jit(solution)/shard_map/ppermute | solution.py:659
  74.9 2.1 %collective-permute-start = (f32[8,128]{1,0:T(8,128)S(1)}, f32[8,128]{1,0:T(8,128)S(1)}, u32[]{:S(2)}, u32[]{:S(2)}) collective-permute-start(f32[8,128]{1,0:T(8,128)S(1)} %reduce_sum.19), channel_id=1, source_target_pairs={{0,64},{64,128},{128,192},{192,0},{1,65},{65,129},{129,193},{193,1... | collective-permute-start | bytes 12296 | tf_op jit(solution)/shard_map/ppermute | solution.py:659
  77.0 0.0 collective-permute-done.2
  77.0 3.1 %collective-permute-done.1 = f32[8,128]{1,0:T(8,128)S(1)} collective-permute-done((f32[8,128]{1,0:T(8,128)S(1)}, f32[8,128]{1,0:T(8,128)S(1)}, u32[]{:S(2)}, u32[]{:S(2)}) %collective-permute-start.1) | collective-permute-done | bytes 4128 | tf_op jit(solution)/shard_map/ppermute | solution.py:659
  80.1 0.0 collective-permute-done
  80.2 15.2 %all_to_all.22.packed = f32[64,8,128]{2,1,0:T(8,128)S(1)} all-to-all(f32[64,8,128]{2,1,0:T(8,128)S(1)} %broadcast_in_dim.5), channel_id=1, replica_groups=mesh['cond'=4,'px'=64] {'px'}, dimensions={0} | all-to-all | bytes 524288 | tf_op jit(solution)/shard_map/all_to_all | solution.py:674
  95.4 0.0 copy-done
  95.4 0.0 copy-done.1
  95.4 2.0 %mask_gradient.1 = f32[128,2048]{1,0:T(8,128)} custom-call(f32[64,8,128]{2,1,0:T(8,128)S(1)} %all_to_all.22.packed, f32[392,256]{1,0:T(8,128)S(1)} %copy-done, f32[128,2048]{1,0:T(8,128)S(1)} %copy-done.1), custom_call_target="tpu_custom_call" | custom-call | tf_op jit(solution)/shard_map/mask_gradient/pallas_call | solution.py:628
  (2 shorter events, 0.0 us)
Async XLA Ops:
  24.6 5.8 %copy-start.3 = (f32[8,128]{1,0:T(8,128)}, f32[8,128]{1,0:T(8,128)S(1)}, u32[]{:S(2)}) copy-start(f32[8,128]{1,0:T(8,128)S(1)} %reduce_sum.18.after) | copy-start | bytes 12292
  25.3 14.3 %all-to-all-start.1 = ((f32[64,8,128]{2,1,0:T(8,128)}), f32[64,8,128]{2,1,0:T(8,128)S(1)}, u32[]{:S(2)}, u32[]{:S(2)}) async-start(f32[64,8,128]{2,1,0:T(8,128)} %broadcast_in_dim.4), calls=%async_computation.1 | async-start | bytes 524288 | tf_op jit(solution)/shard_map/all_to_all | solution.py:674
  39.7 0.7 copy-start.2
  40.3 55.0 %copy-start = (f32[392,256]{1,0:T(8,128)S(1)}, f32[392,256]{1,0:T(8,128)}, u32[]{:S(2)}) copy-start(f32[392,256]{1,0:T(8,128)} %constant.16.clone.table_hbm.table) | copy-start | bytes 1204228
  40.4 55.0 %copy-start.1 = (f32[128,2048]{1,0:T(8,128)S(1)}, f32[128,2048]{1,0:T(8,128)}, u32[]{:S(2)}) copy-start(f32[128,2048]{1,0:T(8,128)} %get-tuple-element.12.slope) | copy-start | bytes 3145732
  68.6 8.5 %collective-permute-start.2 = (f32[8,128]{1,0:T(8,128)S(1)}, f32[8,128]{1,0:T(8,128)S(1)}, u32[]{:S(2)}, u32[]{:S(2)}) collective-permute-start(f32[8,128]{1,0:T(8,128)S(1)} %reduce_sum.19), channel_id=1, source_target_pairs={{0,192},{64,0},{128,64},{192,128},{1,193},{65,1},{129,65},{193,129... | collective-permute-start | bytes 12296 | tf_op jit(solution)/shard_map/ppermute | solution.py:659
  73.8 6.4 %collective-permute-start.1 = (f32[8,128]{1,0:T(8,128)S(1)}, f32[8,128]{1,0:T(8,128)S(1)}, u32[]{:S(2)}, u32[]{:S(2)}) collective-permute-start(f32[8,128]{1,0:T(8,128)S(1)} %reduce_sum.19), channel_id=1, source_target_pairs={{0,128},{64,192},{128,0},{192,64},{1,129},{65,193},{129,1},{193,65... | collective-permute-start | bytes 12296 | tf_op jit(solution)/shard_map/ppermute | solution.py:659
  74.9 5.2 %collective-permute-start = (f32[8,128]{1,0:T(8,128)S(1)}, f32[8,128]{1,0:T(8,128)S(1)}, u32[]{:S(2)}, u32[]{:S(2)}) collective-permute-start(f32[8,128]{1,0:T(8,128)S(1)} %reduce_sum.19), channel_id=1, source_target_pairs={{0,64},{64,128},{128,192},{192,0},{1,65},{65,129},{129,193},{193,1... | collective-permute-start | bytes 12296 | tf_op jit(solution)/shard_map/ppermute | solution.py:659
